TPU v7x, 32 devices: a whole 2x2x4 slice. The times are simulated.
32 devices in a mesh: clip: 16 (over z, y, core), head: 2 (over x).
Axes of the slice: x: 2, y: 2, z: 4, core: 2. Of those that a mesh axis runs over, the one named last changes fastest.
Arguments:
- frames: bfloat16 [32768, 1024], P(('clip', 'head')), may hold values from -6 to 6
- clip_lengths: int32 [64], P('clip'), may hold values from 1 to 1024, as said below
- timesteps: int32 [64], replicated, may hold values from 0 to 999
- w_qkv: float32 [3, 1024, 1024], P(None, 'clip', 'head'), may hold values from -0.25 to 0.25
- w_out: float32 [1024, 1024], P('head', 'clip'), may hold values from -0.75 to 0.75
- w_up: float32 [1024, 2048], P('clip', 'head'), may hold values from -0.1875 to 0.1875
- w_down: float32 [2048, 1024], P('head', 'clip'), may hold values from -0.125 to 0.125
- w_ada: float32 [1024, 6144], P(None, ('clip', 'head')), may hold values from -0.25 to 0.25
- b_ada: float32 [6144], P(('clip', 'head')), may hold values from -1.8 to 1.8
- grad_out: bfloat16 [32768, 1024], P(('clip', 'head')), may hold values from -6 to 6
Outputs:
- mixed: bfloat16 [32768, 1024], P(('clip', 'head'))
- grad_frames: float32 [32768, 1024], P(('clip', 'head'))
- grad_qkv: float32 [3, 1024, 1024], P(None, 'clip', 'head')
- grad_outw: float32 [1024, 1024], P('head', 'clip')
- grad_up: float32 [1024, 2048], P('clip', 'head')
- grad_down: float32 [2048, 1024], P('head', 'clip')
- grad_ada: float32 [1024, 6144], P(None, ('clip', 'head'))
- grad_bias: float32 [6144], P(('clip', 'head'))
Inputs may be any that keep to these rules, and one draw needn't show every extreme that they name: `clip_lengths`: in each group of 4 entries exactly one clip, at a place drawn from the seed, has 1024 frames and the others fewer; a group's lengths sum to less than 2048, and the slots after its last clip are padding.
All inputs are finite; a program needn't handle non-finite values.
Results may differ from a plain program's by a relative error of at most 0.02.
The roundings to bfloat16 on the way count: a program that leaves them out, or rounds other values in their place, can miss the bound.
Values may be sent and summed in bfloat16 or wider, within the bound.
No kernel may reach another device: no remote copies, remote signals or barrier semaphores. Data moves between devices by JAX's collectives and lax.ppermute only.
A program may use at most 320 MiB of HBM per device.

v0:
```python
import math

import jax
import jax.numpy as jnp
from jax import lax
from jax.sharding import PartitionSpec as P

HEAD_DIM = 64


HIGHEST = lax.Precision.HIGHEST
MASKED = -1e30
EPSILON = 1e-06


def clip_layout(lengths, frame_count):
    ends_at = jnp.cumsum(lengths, dtype=jnp.int32)
    starts_at = ends_at - lengths
    frame_index = jnp.arange(frame_count, dtype=jnp.int32)
    inside = (frame_index[:, None] >= starts_at[None, :]) & (
        frame_index[:, None] < ends_at[None, :]
    )
    member = inside.astype(jnp.float32)
    segment = jnp.sum(
        (frame_index[:, None] >= ends_at[None, :]).astype(jnp.int32), axis=1, dtype=jnp.int32
    )
    padding = segment == lengths.shape[0]
    begins = jnp.sum(jnp.where(inside, starts_at[None, :], 0), axis=1, dtype=jnp.int32) + jnp.where(
        padding, ends_at[-1], 0
    )
    return (member, segment, frame_index - begins)


def time_vector(steps, width):
    halfway = width // 2
    rates = jnp.exp(jnp.arange(halfway, dtype=jnp.float32) * (-math.log(10000.0) / (halfway - 1)))
    angles = steps.astype(jnp.float32)[:, None] * rates[None, :]
    return jnp.concatenate([jnp.sin(angles), jnp.cos(angles)], axis=1)


def rotary_tables(position, head_dim):
    halfway = head_dim // 2
    rates = jnp.exp(jnp.arange(halfway, dtype=jnp.float32) * (-2.0 * math.log(10000.0) / head_dim))
    angles = position.astype(jnp.float32)[:, None] * rates[None, :]
    return (jnp.cos(angles)[:, None, :], jnp.sin(angles)[:, None, :])


def rotate(vectors, cosine, sine):
    halfway = vectors.shape[-1] // 2
    first_half = vectors[..., :halfway]
    second_half = vectors[..., halfway:]
    return jnp.concatenate(
        [first_half * cosine - second_half * sine, second_half * cosine + first_half * sine],
        axis=-1,
    )


def rotate_back(gradient, cosine, sine):
    halfway = gradient.shape[-1] // 2
    first_half = gradient[..., :halfway]
    second_half = gradient[..., halfway:]
    return jnp.concatenate(
        [first_half * cosine + second_half * sine, second_half * cosine - first_half * sine],
        axis=-1,
    )


def layer_norm(values):
    centered = values - jnp.mean(values, axis=-1, keepdims=True)
    variance = jnp.mean(centered * centered, axis=-1, keepdims=True)
    return centered * lax.rsqrt(variance + EPSILON)


def modulate(values, scale, shift):
    return layer_norm(values) * (1.0 + scale) + shift


def gelu_tanh(values):
    return jax.nn.gelu(values, approximate=True)


def block_scores(query_block, segment_block, keys_all, segment):
    raw_scores = jnp.einsum(
        "qhd,khd->hqk", query_block, keys_all, preferred_element_type=jnp.float32
    )
    same_clip = segment_block[None, :, None] == segment[None, None, :]
    return jnp.where(same_clip, raw_scores * (1.0 / math.sqrt(query_block.shape[-1])), MASKED)


def body(frames, clip_lengths, timesteps, w_qkv, w_out, w_up, w_down, w_ada, b_ada, grad_out):
    frame_dev, width = frames.shape
    group_clips = clip_lengths.shape[0]
    group_rows = frame_dev * lax.axis_size("head")
    block_rows = min(512, group_rows)
    block_count = group_rows // block_rows
    scaling = 1.0 / math.sqrt(HEAD_DIM)
    member, segment, position = clip_layout(clip_lengths, group_rows)
    member_own = lax.dynamic_slice_in_dim(member, lax.axis_index("head") * frame_dev, frame_dev, 0)
    cosine, sine = rotary_tables(position, HEAD_DIM)
    qkv_part, out_part, up_part, down_part = (
        lax.all_gather(w_qkv.astype(jnp.bfloat16), "clip", axis=1, tiled=True),
        lax.all_gather(w_out.astype(jnp.bfloat16), "clip", axis=1, tiled=True),
        lax.all_gather(w_up.astype(jnp.bfloat16), "clip", axis=0, tiled=True),
        lax.all_gather(w_down.astype(jnp.bfloat16), "clip", axis=1, tiled=True),
    )
    condition_all = jax.nn.silu(time_vector(timesteps, width))
    condition = lax.dynamic_slice_in_dim(
        condition_all, lax.axis_index("clip") * group_clips, group_clips, 0
    )
    ada_whole, bias_whole = (
        lax.all_gather(w_ada.astype(jnp.bfloat16), ("clip", "head"), axis=1, tiled=True),
        lax.all_gather(b_ada.astype(jnp.bfloat16), ("clip", "head"), axis=0, tiled=True),
    )
    adaptive = jnp.dot(
        condition, ada_whole.astype(jnp.float32), precision=HIGHEST
    ) + bias_whole.astype(jnp.float32)
    modes = jnp.dot(member_own, adaptive, precision=HIGHEST)
    shift_one, scale_one, gate_one, shift_two, scale_two, gate_two = jnp.split(modes, 6, axis=1)
    inputs = frames.astype(jnp.float32)
    pre_one, norm_back_one = jax.vjp(modulate, inputs, scale_one, shift_one)
    normed_one = pre_one.astype(jnp.bfloat16)
    normed_full = lax.all_gather(normed_one, "head", axis=0, tiled=True)
    projected = jnp.einsum("fd,cde->cfe", normed_full, qkv_part, preferred_element_type=jnp.float32)
    local_heads = projected.shape[2] // HEAD_DIM
    head_shape = (group_rows, local_heads, HEAD_DIM)
    block_shape = (block_count, block_rows, local_heads, HEAD_DIM)
    query = rotate(projected[0].reshape(head_shape), cosine, sine).astype(jnp.bfloat16)
    keys_all = rotate(projected[1].reshape(head_shape), cosine, sine).astype(jnp.bfloat16)
    values_all = projected[2].reshape(head_shape).astype(jnp.bfloat16)
    query_blocks = query.reshape(block_shape)
    segment_blocks = segment.reshape(block_count, block_rows)

    def forward_block(item):
        query_block, segment_block = item
        scores = block_scores(query_block, segment_block, keys_all, segment)
        highest_score = jnp.max(scores, axis=-1, keepdims=True)
        unnormed = jnp.exp(scores - highest_score)
        row_total = jnp.sum(unnormed, axis=-1, keepdims=True)
        attention = (unnormed / row_total).astype(jnp.bfloat16)
        result = jnp.einsum(
            "hqk,khd->qhd", attention, values_all, preferred_element_type=jnp.float32
        )
        return (result.astype(jnp.bfloat16), highest_score, row_total)

    attended, highest_rows, total_rows = lax.map(forward_block, (query_blocks, segment_blocks))
    attended = attended.reshape(group_rows, local_heads * HEAD_DIM)
    branch_one = lax.psum_scatter(
        jnp.dot(attended, out_part, preferred_element_type=jnp.float32).astype(jnp.bfloat16),
        "head",
        scatter_dimension=0,
        tiled=True,
    ).astype(jnp.float32)
    middle = inputs + gate_one * branch_one
    pre_two, norm_back_two = jax.vjp(modulate, middle, scale_two, shift_two)
    normed_two = pre_two.astype(jnp.bfloat16)
    normed_two_full = lax.all_gather(normed_two, "head", axis=0, tiled=True)
    hidden = jnp.dot(normed_two_full, up_part, preferred_element_type=jnp.float32)
    active, gelu_back = jax.vjp(gelu_tanh, hidden)
    active_low = active.astype(jnp.bfloat16)
    branch_two = lax.psum_scatter(
        jnp.dot(active_low, down_part, preferred_element_type=jnp.float32).astype(jnp.bfloat16),
        "head",
        scatter_dimension=0,
        tiled=True,
    ).astype(jnp.float32)
    mixed = (middle + gate_two * branch_two).astype(jnp.bfloat16)
    upstream = grad_out.astype(jnp.float32)
    grad_branch_two = (upstream * gate_two).astype(jnp.bfloat16)
    grad_gate_two = upstream * branch_two
    grad_branch_full = lax.all_gather(grad_branch_two, "head", axis=0, tiled=True)
    grad_active = jnp.einsum(
        "fd,cd->fc", grad_branch_full, down_part, preferred_element_type=jnp.float32
    )
    grad_downw = jnp.einsum(
        "fc,fd->cd", active_low, grad_branch_full, preferred_element_type=jnp.float32
    )
    grad_hidden = gelu_back(grad_active)[0].astype(jnp.bfloat16)
    grad_upw = jnp.einsum(
        "fd,fc->dc", normed_two_full, grad_hidden, preferred_element_type=jnp.float32
    )
    part_rows = grad_hidden
    grad_pre_two = lax.psum_scatter(
        jnp.einsum("fc,dc->fd", part_rows, up_part, preferred_element_type=jnp.float32).astype(
            jnp.bfloat16
        ),
        "head",
        scatter_dimension=0,
        tiled=True,
    ).astype(jnp.float32)
    grad_middle_norm, grad_scale_two, grad_shift_two = norm_back_two(grad_pre_two)
    grad_middle = upstream + grad_middle_norm
    grad_branch_one = (grad_middle * gate_one).astype(jnp.bfloat16)
    grad_gate_one = grad_middle * branch_one
    grad_branch_one_full = lax.all_gather(grad_branch_one, "head", axis=0, tiled=True)
    grad_outw = jnp.einsum(
        "fe,fd->ed", attended, grad_branch_one_full, preferred_element_type=jnp.float32
    )
    grad_attended = jnp.einsum(
        "fd,ed->fe", grad_branch_one_full, out_part, preferred_element_type=jnp.float32
    ).astype(jnp.bfloat16)
    grad_blocks = grad_attended.reshape(block_shape)

    def backward_block(carry, item):
        key_grads, value_grads = carry
        query_block, segment_block, grad_block, highest_score, row_total = item
        scores = block_scores(query_block, segment_block, keys_all, segment)
        attention = jnp.exp(scores - highest_score) / row_total
        attention_low = attention.astype(jnp.bfloat16)
        grad_attention = jnp.einsum(
            "qhd,khd->hqk", grad_block, values_all, preferred_element_type=jnp.float32
        )
        centre = jnp.sum(attention * grad_attention, axis=-1, keepdims=True)
        grad_scores = (attention * (grad_attention - centre) * scaling).astype(jnp.bfloat16)
        query_grad = jnp.einsum(
            "hqk,khd->qhd", grad_scores, keys_all, preferred_element_type=jnp.float32
        )
        key_grads = key_grads + jnp.einsum(
            "hqk,qhd->khd", grad_scores, query_block, preferred_element_type=jnp.float32
        )
        value_grads = value_grads + jnp.einsum(
            "hqk,qhd->khd", attention_low, grad_block, preferred_element_type=jnp.float32
        )
        return ((key_grads, value_grads), query_grad)

    empty_grads = jnp.zeros(head_shape, jnp.float32)
    (key_grads, value_grads), query_grads = lax.scan(
        backward_block,
        (empty_grads, empty_grads),
        (query_blocks, segment_blocks, grad_blocks, highest_rows, total_rows),
    )
    query_grads = query_grads.reshape(head_shape)
    grad_projected = jnp.stack(
        [
            rotate_back(query_grads, cosine, sine).reshape(group_rows, -1),
            rotate_back(key_grads, cosine, sine).reshape(group_rows, -1),
            value_grads.reshape(group_rows, -1),
        ]
    ).astype(jnp.bfloat16)
    grad_qkvw = jnp.einsum(
        "fd,cfe->cde", normed_full, grad_projected, preferred_element_type=jnp.float32
    )
    part_rows = grad_projected
    grad_pre_one = lax.psum_scatter(
        jnp.einsum("cfe,cde->fd", part_rows, qkv_part, preferred_element_type=jnp.float32).astype(
            jnp.bfloat16
        ),
        "head",
        scatter_dimension=0,
        tiled=True,
    ).astype(jnp.float32)
    grad_input_norm, grad_scale_one, grad_shift_one = norm_back_one(grad_pre_one)
    grad_frames = grad_middle + grad_input_norm
    grad_modes = jnp.concatenate(
        [
            grad_shift_one,
            grad_scale_one,
            grad_gate_one,
            grad_shift_two,
            grad_scale_two,
            grad_gate_two,
        ],
        axis=1,
    )
    grad_adaptive = jnp.dot(member_own.T, grad_modes, precision=HIGHEST)
    ada_terms = jnp.dot(condition.T, grad_adaptive, precision=HIGHEST)
    bias_terms = jnp.sum(grad_adaptive, axis=0)
    grad_ada, grad_bias = (
        lax.psum_scatter(ada_terms, ("clip", "head"), scatter_dimension=1, tiled=True),
        lax.psum_scatter(bias_terms, ("clip", "head"), scatter_dimension=0, tiled=True),
    )
    grad_qkv, grad_outw, grad_up, grad_down = (
        lax.psum_scatter(
            grad_qkvw.astype(jnp.bfloat16), "clip", scatter_dimension=1, tiled=True
        ).astype(jnp.float32),
        lax.psum_scatter(
            grad_outw.astype(jnp.bfloat16), "clip", scatter_dimension=1, tiled=True
        ).astype(jnp.float32),
        lax.psum_scatter(
            grad_upw.astype(jnp.bfloat16), "clip", scatter_dimension=0, tiled=True
        ).astype(jnp.float32),
        lax.psum_scatter(
            grad_downw.astype(jnp.bfloat16), "clip", scatter_dimension=1, tiled=True
        ).astype(jnp.float32),
    )
    return (mixed, grad_frames, grad_qkv, grad_outw, grad_up, grad_down, grad_ada, grad_bias)


def solution(mesh):
    placed = (
        P(("clip", "head"), None),
        P("clip"),
        P(),
        P(None, "clip", "head"),
        P("head", "clip"),
        P("clip", "head"),
        P("head", "clip"),
        P(None, ("clip", "head")),
        P(("clip", "head")),
        P(("clip", "head"), None),
    )
    return jax.shard_map(
        body,
        mesh=mesh,
        in_specs=placed,
        out_specs=(
            P(("clip", "head"), None),
            P(("clip", "head"), None),
            P(None, "clip", "head"),
            P("head", "clip"),
            P("clip", "head"),
            P("head", "clip"),
            P(None, ("clip", "head")),
            P(("clip", "head")),
        ),
        check_vma=False,
    )
```

profile of v0, /device:TPU:1, one launch (start us, length us, event | category | flops | bytes accessed | tf_op | source)
XLA Modules:
  0.0 2212.3 jit_solution(4178744122092189417)
XLA Ops:
  13.5 42.4 %all-reduce = bf16[6144]{0:T(1024)(128)(2,1)S(1)} all-reduce(bf16[6144]{0:T(1024)(128)(2,1)S(1)} %dynamic-update-slice), channel_id=1, replica_groups=mesh['clip'=16,'head'=2] {'clip','head'}, use_global_device_ids=true, to_apply=%add | all-reduce | flops 6144 | bytes 24576
  60.0 51.0 %all-gather.10.cloned.1.call-done = bf16[1024,6144]{0,1:T(8,128)(2,1)} async-done(((bf16[1024,192]{0,1:T(8,128)(2,1)}), bf16[1024,6144]{0,1:T(8,128)(2,1)}) %all-gather.10.cloned.1.call-update) | async-done | bytes 12582928 | tf_op jit(solution)/shard_map/all_gather | solution.py:111
  157.2 57.3 %all-gather.12.cloned.1.call-done = bf16[2048,1024]{1,0:T(8,128)(2,1)} async-done(((bf16[1024,1024]{1,0:T(8,128)(2,1)}), bf16[2048,1024]{1,0:T(8,128)(2,1)}) %all-gather.12.cloned.1.call-update) | async-done | bytes 4194320 | tf_op jit(solution)/shard_map/all_gather | solution.py:122
  237.5 187.0 %while.29 = (s32[]{:T(128)}, bf16[4,512,8,64]{1,3,2,0:T(8,128)(2,1)}, f32[4,8,512,1]{2,1,3,0:T(8,128)S(1)}, f32[4,8,512,1]{2,1,3,0:T(8,128)S(1)}, s32[4,512]{1,0...) while((s32[]{:T(128)}, ...), condition=%wide.region_8.9_spmd, body=%wide.region_5.8_spmd.sunk | while | flops 2249449472 | bytes 110262392 | solution.py:145
  437.6 52.8 %reduce-scatter.9.cloned.1.call-done = bf16[1024,1024]{1,0:T(8,128)(2,1)} async-done(((bf16[2048,1024]{1,0:T(8,128)(2,1)}), bf16[1024,1024]{1,0:T(8,128)(2,1)}) %reduce-scatter.9.cloned.1.call-update) | async-done | bytes 2097168 | tf_op jit(solution)/shard_map/reduce_scatter | solution.py:147
  535.1 57.3 %all-gather.24.cloned.1.call-done = bf16[2048,1024]{1,0:T(8,128)(2,1)} async-done(((bf16[1024,1024]{1,0:T(8,128)(2,1)}), bf16[2048,1024]{1,0:T(8,128)(2,1)}) %all-gather.24.cloned.1.call-update) | async-done | bytes 4194320 | tf_op jit(solution)/shard_map/all_gather | solution.py:170
  637.2 57.3 %all-gather.18.cloned.1.call-done = bf16[2048,1024]{1,0:T(8,128)(2,1)} async-done(((bf16[1024,1024]{1,0:T(8,128)(2,1)}), bf16[2048,1024]{1,0:T(8,128)(2,1)}) %all-gather.18.cloned.1.call-update) | async-done | bytes 4194320 | tf_op jit(solution)/shard_map/all_gather | solution.py:156
  730.7 42.9 %reduce-scatter.13.cloned.1.call-done = bf16[1024,1024]{1,0:T(8,128)(2,1)} async-done(((bf16[2048,1024]{1,0:T(8,128)(2,1)}), bf16[1024,1024]{1,0:T(8,128)(2,1)}) %reduce-scatter.13.cloned.1.call-update) | async-done | bytes 2097168 | tf_op jit(solution)/shard_map/reduce_scatter | solution.py:182
  778.6 51.5 %reduce-scatter.11.cloned.1.call-done = bf16[1024,1024]{1,0:T(8,128)(2,1)} async-done(((bf16[2048,1024]{1,0:T(8,128)(2,1)}), bf16[1024,1024]{1,0:T(8,128)(2,1)}) %reduce-scatter.11.cloned.1.call-update) | async-done | bytes 2097168 | tf_op jit(solution)/shard_map/reduce_scatter | solution.py:160
  845.0 56.8 %all-gather.26.cloned.1.call-done = bf16[2048,1024]{1,0:T(8,128)(2,1)} async-done(((bf16[1024,1024]{1,0:T(8,128)(2,1)}), bf16[2048,1024]{1,0:T(8,128)(2,1)}) %all-gather.26.cloned.1.call-update) | async-done | bytes 4194320 | tf_op jit(solution)/shard_map/all_gather | solution.py:194
  919.4 640.0 %while.30 = (s32[]{:T(128)}, f32[2048,8,64]{0,2,1:T(8,128)}, f32[2048,8,64]{0,2,1:T(8,128)}, f32[4,512,8,64]{1,0,3,2:T(4,128)}, bf16[4,512,8,64]{1,3,2,0:T(8,128...) while((s32[]{:T(128)}, f32[2048,8,64]{0,2,1:T(8,128)}, ...), condition=%wide.region_18.19_spmd.clone, body=%wide.region_16.18_spmd.clone.sunk | while | flops 5499793408 | bytes 334608512 | solution.py:226
  967.7 43.2 %fusion.156 = f32[1,512,8,64]{1,3,2,0:T(8,128)} fusion(bf16[2048,8,64]{0,2,1:T(8,128)(2,1)} %get-tuple-element.538, f32[8,512,2048]{2,1,0:T(8,128)} %exponential_divide_fusion.2, f32[8,512,2048]{2,1,0:T(8,128)} %fusion.155), kind=kOutput, calls=%fused_computation.31.clone.1 | convolution fusion | flops 1115691008 | bytes 70254592 | tf_op jit(solution)/shard_map/while/body/eval_jaxpr/hqk,khd->qhd/dot_general | solution.py:214
  1010.9 43.4 %bitcast_add_fusion.4 = f32[2048,8,64]{0,2,1:T(8,128)} fusion(f32[2048,8,64]{0,2,1:T(8,128)} %get-tuple-element.518, f32[8,512,2048]{2,1,0:T(8,128)} %exponential_divide_fusion.2, f32[8,512,2048]{2,1,0:T(8,128)} %fusion.155, pred[]{:T(512)S(6)} %compare.3, bf16[4,512,8,64]{1,3,2,0:T(8,128)(2,1)} %get-tuple-element.535, s32[]{:T(128)S(6)} %copy.104), kind=kOutput, calls=%fused_computation.29.clone.1 | convolution fusion | flops 1117788160 | bytes 143130624 | tf_op jit(solution)/shard_map/while/body/eval_jaxpr/hqk,qhd->khd/dot_general | solution.py:217
  1127.1 43.2 %fusion.156 = f32[1,512,8,64]{1,3,2,0:T(8,128)} fusion(bf16[2048,8,64]{0,2,1:T(8,128)(2,1)} %get-tuple-element.538, f32[8,512,2048]{2,1,0:T(8,128)} %exponential_divide_fusion.2, f32[8,512,2048]{2,1,0:T(8,128)} %fusion.155), kind=kOutput, calls=%fused_computation.31.clone.1 | convolution fusion | flops 1115691008 | bytes 70254592 | tf_op jit(solution)/shard_map/while/body/eval_jaxpr/hqk,khd->qhd/dot_general | solution.py:214
  1170.2 44.6 %bitcast_add_fusion.4 = f32[2048,8,64]{0,2,1:T(8,128)} fusion(f32[2048,8,64]{0,2,1:T(8,128)} %get-tuple-element.518, f32[8,512,2048]{2,1,0:T(8,128)} %exponential_divide_fusion.2, f32[8,512,2048]{2,1,0:T(8,128)} %fusion.155, pred[]{:T(512)S(6)} %compare.3, bf16[4,512,8,64]{1,3,2,0:T(8,128)(2,1)} %get-tuple-element.535, s32[]{:T(128)S(6)} %copy.104), kind=kOutput, calls=%fused_computation.29.clone.1 | convolution fusion | flops 1117788160 | bytes 143130624 | tf_op jit(solution)/shard_map/while/body/eval_jaxpr/hqk,qhd->khd/dot_general | solution.py:217
  1287.5 43.2 %fusion.156 = f32[1,512,8,64]{1,3,2,0:T(8,128)} fusion(bf16[2048,8,64]{0,2,1:T(8,128)(2,1)} %get-tuple-element.538, f32[8,512,2048]{2,1,0:T(8,128)} %exponential_divide_fusion.2, f32[8,512,2048]{2,1,0:T(8,128)} %fusion.155), kind=kOutput, calls=%fused_computation.31.clone.1 | convolution fusion | flops 1115691008 | bytes 70254592 | tf_op jit(solution)/shard_map/while/body/eval_jaxpr/hqk,khd->qhd/dot_general | solution.py:214
  1330.7 44.6 %bitcast_add_fusion.4 = f32[2048,8,64]{0,2,1:T(8,128)} fusion(f32[2048,8,64]{0,2,1:T(8,128)} %get-tuple-element.518, f32[8,512,2048]{2,1,0:T(8,128)} %exponential_divide_fusion.2, f32[8,512,2048]{2,1,0:T(8,128)} %fusion.155, pred[]{:T(512)S(6)} %compare.3, bf16[4,512,8,64]{1,3,2,0:T(8,128)(2,1)} %get-tuple-element.535, s32[]{:T(128)S(6)} %copy.104), kind=kOutput, calls=%fused_computation.29.clone.1 | convolution fusion | flops 1117788160 | bytes 143130624 | tf_op jit(solution)/shard_map/while/body/eval_jaxpr/hqk,qhd->khd/dot_general | solution.py:217
  1447.9 43.2 %fusion.156 = f32[1,512,8,64]{1,3,2,0:T(8,128)} fusion(bf16[2048,8,64]{0,2,1:T(8,128)(2,1)} %get-tuple-element.538, f32[8,512,2048]{2,1,0:T(8,128)} %exponential_divide_fusion.2, f32[8,512,2048]{2,1,0:T(8,128)} %fusion.155), kind=kOutput, calls=%fused_computation.31.clone.1 | convolution fusion | flops 1115691008 | bytes 70254592 | tf_op jit(solution)/shard_map/while/body/eval_jaxpr/hqk,khd->qhd/dot_general | solution.py:214
  1491.1 44.6 %bitcast_add_fusion.4 = f32[2048,8,64]{0,2,1:T(8,128)} fusion(f32[2048,8,64]{0,2,1:T(8,128)} %get-tuple-element.518, f32[8,512,2048]{2,1,0:T(8,128)} %exponential_divide_fusion.2, f32[8,512,2048]{2,1,0:T(8,128)} %fusion.155, pred[]{:T(512)S(6)} %compare.3, bf16[4,512,8,64]{1,3,2,0:T(8,128)(2,1)} %get-tuple-element.535, s32[]{:T(128)S(6)} %copy.104), kind=kOutput, calls=%fused_computation.29.clone.1 | convolution fusion | flops 1117788160 | bytes 143130624 | tf_op jit(solution)/shard_map/while/body/eval_jaxpr/hqk,qhd->khd/dot_general | solution.py:217
  1716.8 61.3 %reduce-scatter.19.cloned.1.call-done = bf16[64,1024]{1,0:T(8,128)(2,1)} async-done(((bf16[1024,1024]{1,0:T(8,128)(2,1)}), bf16[64,1024]{1,0:T(8,128)(2,1)}) %reduce-scatter.19.cloned.1.call-update) | async-done | bytes 131088 | tf_op jit(solution)/shard_map/reduce_scatter | solution.py:278
  1779.7 113.0 %all-reduce.5.cloned.1.call-done = bf16[3,1024,512]{2,0,1:T(4,128)(2,1)} async-done(((bf16[3,1024,512]{2,0,1:T(4,128)(2,1)}), bf16[3,1024,512]{2,0,1:T(4,128)(2,1)}) %all-reduce.5.cloned.1.call-update) | async-done | bytes 3145744
  1894.5 57.6 %reduce-scatter.17.cloned.1.call-done = bf16[512,64]{0,1:T(8,128)(2,1)} async-done(((bf16[512,1024]{0,1:T(8,128)(2,1)}), bf16[512,64]{0,1:T(8,128)(2,1)}) %reduce-scatter.17.cloned.1.call-update) | async-done | bytes 65552 | tf_op jit(solution)/shard_map/reduce_scatter | solution.py:275
  1953.7 41.3 %all-reduce.2 = f32[6144]{0:T(1024)S(1)} all-reduce(f32[6144]{0:T(1024)S(1)} %get-tuple-element.329), channel_id=11, replica_groups=mesh['clip'=16,'head'=2] {'clip','head'}, use_global_device_ids=true, to_apply=%region_28.29.clone | all-reduce | flops 6144 | bytes 49152
  1995.6 209.6 %reduce-scatter.23.cloned.1.call-done = f32[1024,192]{0,1:T(8,128)} async-done(((f32[1024,6144]{0,1:T(8,128)}), f32[1024,192]{0,1:T(8,128)}) %reduce-scatter.23.cloned.1.call-update) | async-done | bytes 786448 | tf_op jit(solution)/shard_map/reduce_scatter | solution.py:268
  (284 shorter events, 893.0 us)
Async XLA Ops:
  7.2 103.8 %all-gather.10.cloned.1.call-start = ((), (), s32[]{:S(2)}) async-start(), calls=%async_computation.8 | async-start | bytes 12976128 | tf_op jit(solution)/shard_map/all_gather | solution.py:111
  9.3 147.9 %all-gather.14.cloned.1.call-start = ((), (), s32[]{:S(2)}) async-start(), calls=%async_computation.10 | async-start | bytes 3342336 | tf_op jit(solution)/shard_map/all_gather | solution.py:101
  11.1 203.4 %all-gather.12.cloned.1.call-start = ((), (), s32[]{:S(2)}) async-start(), calls=%async_computation.9 | async-start | bytes 6291456 | tf_op jit(solution)/shard_map/all_gather | solution.py:122
  58.0 75.9 %copy-start.30 = (f32[1024]{0:T(1024)}, f32[1024]{0:T(1024)S(1)}, u32[]{:S(2)}) copy-start(f32[1024]{0:T(1024)S(1)} %broadcast_multiply_fusion.1) | copy-start | bytes 12292
  59.3 74.6 %copy-start.32 = (f32[1024]{0:T(1024)}, f32[1024]{0:T(1024)S(1)}, u32[]{:S(2)}) copy-start(f32[1024]{0:T(1024)S(1)} %fusion.83) | copy-start | bytes 12292
  145.0 284.7 %all-gather.16.cloned.1.call-start = ((), (), s32[]{:S(2)}) async-start(), calls=%async_computation.11 | async-start | bytes 1114112 | tf_op jit(solution)/shard_map/all_gather | solution.py:102
  145.7 344.7 %reduce-scatter.9.cloned.1.call-start = ((), (), s32[]{:S(2)}) async-start(), calls=%async_computation.12 | async-start | bytes 6291456 | tf_op jit(solution)/shard_map/reduce_scatter | solution.py:147
  148.3 84.6 %copy-start.16 = (f32[2048,32]{0,1:T(8,128)}, f32[2048,32]{0,1:T(8,128)S(1)}, u32[]{:S(2)}) copy-start(f32[2048,32]{0,1:T(8,128)S(1)} %get-tuple-element.323) | copy-start | bytes 786436
  148.4 84.6 %copy-start.18 = (f32[2048,32]{0,1:T(8,128)}, f32[2048,32]{0,1:T(8,128)S(1)}, u32[]{:S(2)}) copy-start(f32[2048,32]{0,1:T(8,128)S(1)} %get-tuple-element.324) | copy-start | bytes 786436
  436.0 99.1 %all-gather.22.cloned.1.call-start = ((), (), s32[]{:S(2)}) async-start(), calls=%async_computation.15 | async-start | bytes 2228224 | tf_op jit(solution)/shard_map/all_gather | solution.py:104
  437.6 154.8 %all-gather.24.cloned.1.call-start = ((), (), s32[]{:S(2)}) async-start(), calls=%async_computation.17 | async-start | bytes 6291456 | tf_op jit(solution)/shard_map/all_gather | solution.py:170
  494.7 335.5 %copy-start.27 = (f32[1024]{0:T(1024)}, f32[1024]{0:T(1024)S(1)}, u32[]{:S(2)}) copy-start(f32[1024]{0:T(1024)S(1)} %broadcast_multiply_fusion) | copy-start | bytes 12292
  497.8 332.4 %copy-start.34 = (f32[1024]{0:T(1024)}, f32[1024]{0:T(1024)S(1)}, u32[]{:S(2)}) copy-start(f32[1024]{0:T(1024)S(1)} %fusion.84) | copy-start | bytes 12292
  505.3 131.9 %all-gather.20.cloned.1.call-start = ((), (), s32[]{:S(2)}) async-start(), calls=%async_computation.14 | async-start | bytes 2228224 | tf_op jit(solution)/shard_map/all_gather | solution.py:103
  506.1 188.5 %all-gather.18.cloned.1.call-start = ((), (), s32[]{:S(2)}) async-start(), calls=%async_computation.13 | async-start | bytes 6291456 | tf_op jit(solution)/shard_map/all_gather | solution.py:156
  506.8 266.8 %reduce-scatter.13.cloned.1.call-start = ((), (), s32[]{:S(2)}) async-start(), calls=%async_computation.18 | async-start | bytes 6291456 | tf_op jit(solution)/shard_map/reduce_scatter | solution.py:182
  719.1 111.1 %reduce-scatter.11.cloned.1.call-start = ((), (), s32[]{:S(2)}) async-start(), calls=%async_computation.16 | async-start | bytes 6291456 | tf_op jit(solution)/shard_map/reduce_scatter | solution.py:160
  730.6 171.2 %all-gather.26.cloned.1.call-start = ((), (), s32[]{:S(2)}) async-start(), calls=%async_computation.19 | async-start | bytes 6291456 | tf_op jit(solution)/shard_map/all_gather | solution.py:194
  844.9 804.9 %reduce-scatter.15.cloned.1.call-start = ((), (), s32[]{:S(2)}) async-start(), calls=%async_computation.20 | async-start | bytes 6291456 | tf_op jit(solution)/shard_map/reduce_scatter | solution.py:243
  1595.4 119.7 %reduce-scatter.21.cloned.1.call-start = ((), (), s32[]{:S(2)}) async-start(), calls=%async_computation.23 | async-start | bytes 2228224 | tf_op jit(solution)/shard_map/reduce_scatter | solution.py:281
  1606.3 171.7 %reduce-scatter.19.cloned.1.call-start = ((), (), s32[]{:S(2)}) async-start(), calls=%async_computation.22 | async-start | bytes 2228224 | tf_op jit(solution)/shard_map/reduce_scatter | solution.py:278
  1616.0 276.7 %all-reduce.5.cloned.1.call-start = ((), (), s32[]{:S(2)}) async-start(), calls=%async_computation.25 | async-start | bytes 8388608
  1632.4 319.7 %reduce-scatter.17.cloned.1.call-start = ((), (), s32[]{:S(2)}) async-start(), calls=%async_computation.21 | async-start | bytes 1114112 | tf_op jit(solution)/shard_map/reduce_scatter | solution.py:275
  1639.6 565.7 %reduce-scatter.23.cloned.1.call-start = ((), (), s32[]{:S(2)}) async-start(), calls=%async_computation.24 | async-start | bytes 25952256 | tf_op jit(solution)/shard_map/reduce_scatter | solution.py:268
  (41 other events, 565.6 us)
Sparse Core Ops, SparseCore 0:
  11.5 99.4 all-gather.9
  113.7 43.4 all-gather.13
  159.3 55.1 all-gather.11
  217.1 38.3 all-gather.15
  436.1 54.2 reduce-scatter.8
  493.2 41.7 all-gather.21
  537.3 55.0 all-gather.23
  595.4 41.8 all-gather.19
  639.4 55.0 all-gather.17
  719.2 54.3 reduce-scatter.12
  775.9 54.2 reduce-scatter.10
  845.0 56.7 all-gather.25
  1595.5 54.3 reduce-scatter.14
  1653.4 59.9 reduce-scatter.20
  1717.5 60.5 reduce-scatter.18
  1781.6 111.0 all-reduce.4
  1896.6 55.5 reduce-scatter.16
  1959.0 246.1 reduce-scatter.22
where the time goes:
time: 2220 us; the launch traced here: 2210 us
  waiting for transfers between devices  951 us (43%)
  matrix products  840 us (38%)
  local copies, waits for them, and re-layouts  166 us (7%)
  other arithmetic  154 us (7%)
  blocking collectives  83.8 us (4%)
    reduce_scatter x1, waiting for transfers between devices, body(): lax.psum_scatter(ada_terms, ('clip', 'head'), scatter_dimension=1, tiled=...  210 us
    dot_general x4, matrix products, backward_block(): jnp.einsum('hqk,qhd->khd', grad_scores, query_block, preferred_element_ty...  177 us
    dot_general x4, matrix products, backward_block(): jnp.einsum('hqk,khd->qhd', grad_scores, keys_all, preferred_element_type=...  173 us
    dot_general x8, matrix products, block_scores(): jnp.einsum('qhd,khd->hqk', query_block, keys_all, preferred_element_type=...  131 us
    unnamed x19, waiting for transfers between devices  114 us
    dynamic_update_slice x8, local copies, waits for them, and re-layouts, body(): lax.scan(backward_block, (empty_grads, empty_grads), (query_blocks, segme...  93.2 us
    unnamed x2, blocking collectives  83.8 us
    dot_general x4, matrix products, backward_block(): jnp.einsum('hqk,qhd->khd', attention_low, grad_block, preferred_element_t...  66.6 us
  transfers between devices with their start and end apart: 18, of which 16 were waited for; matrix products, arithmetic and copies ran while one was open for 18% of the time, Pallas kernels for 0%

commit v1 on v0

v1 whole, which is shorter than its diff:
```python
import functools
import math

import jax
import jax.numpy as jnp
from jax import lax
from jax.experimental import pallas as pl
from jax.experimental.pallas import tpu as pltpu
from jax.sharding import Mesh
from jax.sharding import PartitionSpec as P

HEAD_DIM = 64
HEADS = 16
HIGHEST = lax.Precision.HIGHEST
MASKED = -1e30
EPSILON = 1e-06
VMEM_LIMIT = 60 * 1024 * 1024
F32 = jnp.float32
BF16 = jnp.bfloat16

ALL = ("za", "zb", "core", "hh", "hl")
MOVE = ("core", "hh", "hl")
SUB = ("core", "hl")

NT = (((1,), (1,)), ((), ()))
NN = (((1,), (0,)), ((), ()))
TN = (((0,), (0,)), ((), ()))


def dot(a, b, dims=NN, precision=None):
    return lax.dot_general(a, b, dims, precision=precision, preferred_element_type=F32)


def params(**more):
    return pltpu.CompilerParams(vmem_limit_bytes=VMEM_LIMIT, **more)


def cost(flops, bytes_accessed, transcendentals=0):
    return pl.CostEstimate(
        flops=int(flops), bytes_accessed=int(bytes_accessed), transcendentals=int(transcendentals)
    )


def whole(shape, buffers=None):
    zeros = (0,) * len(shape)
    if buffers is None:
        return pl.BlockSpec(shape, lambda *_: zeros)
    return pl.BlockSpec(shape, lambda *_: zeros, pipeline_mode=pl.Buffered(buffers))


def move_pairs(hl):
    pairs = []
    for core in range(2):
        for place in range(2 * hl):
            source = core * 2 * hl + place
            target = ((place // hl) * 2 + core) * hl + place % hl
            pairs.append((source, target))
    return pairs


def moved(value):
    return lax.ppermute(value, MOVE, move_pairs(lax.axis_size("hl")))


def moved_back(value):
    pairs = [(b, a) for a, b in move_pairs(lax.axis_size("hl"))]
    return lax.ppermute(value, MOVE, pairs)


def from_sub(value, step):
    size = lax.axis_size("hl") * 2
    return lax.ppermute(value, SUB, [((d + step) % size, d) for d in range(size)])


def to_sub(value, step):
    size = lax.axis_size("hl") * 2
    return lax.ppermute(value, SUB, [(d, (d + step) % size) for d in range(size)])


SWAP = [(0, 1), (1, 0)]


def across(value, bit):
    size = lax.axis_size("za")
    return lax.ppermute(value, "za", [(i, i ^ bit) for i in range(size)])


def place_kernel(half, where, own, by_zb, by_hh, both_low, both_high, out):
    zb = where[0]
    hh = where[1]
    out[0, zb, hh] = own[0]
    out[0, 1 - zb, hh] = by_zb[0]
    out[0, zb, 1 - hh] = by_hh[0]

    @pl.when(pl.program_id(0) < half)
    def _():
        out[0, 1 - zb, 1 - hh] = both_low[0]

    @pl.when(pl.program_id(0) >= half)
    def _():
        out[0, 1 - zb, 1 - hh] = both_high[0]


def gather_plane(shard):
    rows, columns = shard.shape
    size = lax.axis_size("za")
    half = size // 2
    held, order, bit = shard[None], [0], half
    while bit:
        held = jnp.concatenate([held, across(held, bit)], axis=0)
        order = order + [at ^ bit for at in order]
        bit //= 2
    by_zb = lax.ppermute(held, "zb", SWAP)
    by_hh = lax.ppermute(held, "hh", SWAP)
    both_low = lax.ppermute(by_zb[:half], "hh", SWAP)
    both_high = lax.ppermute(by_hh[half:], "zb", SWAP)
    where = [lax.axis_index("zb"), lax.axis_index("hh")]
    where += [lax.axis_index("za") ^ at for at in order]
    where = jnp.stack(where).astype(jnp.int32)
    block = (1, rows, columns)
    full = pl.pallas_call(
        functools.partial(place_kernel, half),
        grid_spec=pltpu.PrefetchScalarGridSpec(
            num_scalar_prefetch=1,
            grid=(size,),
            in_specs=[pl.BlockSpec(block, lambda i, w: (i, 0, 0))] * 3
            + [
                pl.BlockSpec(block, lambda i, w: (jnp.minimum(i, half - 1), 0, 0)),
                pl.BlockSpec(block, lambda i, w: (jnp.maximum(i - half, 0), 0, 0)),
            ],
            out_specs=pl.BlockSpec((1, 2, 2, rows, columns), lambda i, w: (w[2 + i], 0, 0, 0, 0)),
        ),
        out_shape=jax.ShapeDtypeStruct((size, 2, 2, rows, columns), shard.dtype),
        compiler_params=params(),
        cost_estimate=cost(0, size * 4 * rows * columns * 4),
        name="place",
    )(where, held, by_zb, by_hh, both_low, both_high)
    return full.reshape(size * 4 * rows, columns)


def reduce_plane(weights):
    size = lax.axis_size("za")
    half = size // 2
    zb, hh = lax.axis_index("zb"), lax.axis_index("hh")

    def piece(dz, dh):
        parts = []
        for terms in weights:
            part = 0.0
            for term in terms:
                rows = term.shape[0] // (size * 4)
                view = term.reshape(size, 2, 2, rows, term.shape[1])
                at = (0, zb ^ dz, hh ^ dh, 0, 0)
                cut = lax.dynamic_slice(view, at, (size, 1, 1, rows, term.shape[1]))
                part = part + cut.reshape(size, rows, -1).astype(F32)
            parts.append(part)
        return parts[0] if len(parts) == 1 else jnp.concatenate(parts, axis=2)

    far = piece(1, 1).astype(BF16)
    low = lax.ppermute(far[:half], "hh", SWAP)
    high = lax.ppermute(far[half:], "zb", SWAP)
    none = jnp.zeros_like(low)
    to_zb = (piece(1, 0) + jnp.concatenate([low, none]).astype(F32)).astype(BF16)
    to_hh = (piece(0, 1) + jnp.concatenate([none, high]).astype(F32)).astype(BF16)
    from_zb = lax.ppermute(to_zb, "zb", SWAP)
    from_hh = lax.ppermute(to_hh, "hh", SWAP)
    total = piece(0, 0) + from_zb.astype(F32) + from_hh.astype(F32)
    mine, bit = lax.axis_index("za"), 1
    while bit < size:
        total = total.astype(BF16)
        pairs = total.reshape(total.shape[0] // 2, 2, *total.shape[1:])
        place = (mine // bit) % 2
        keep = lax.dynamic_index_in_dim(pairs, place, 1, keepdims=False)
        send = lax.dynamic_index_in_dim(pairs, 1 - place, 1, keepdims=False)
        total = keep.astype(F32) + across(send, bit).astype(F32)
        bit *= 2
    return total[0].astype(BF16)


def norm(values):
    centred = values - jnp.mean(values, axis=-1, keepdims=True)
    variance = jnp.mean(centred * centred, axis=-1, keepdims=True)
    inverse = lax.rsqrt(variance + EPSILON)
    return centred * inverse, inverse


def pick(member, table):
    return dot(member, table, precision=HIGHEST)


def first_norm_kernel(x, member, adaptive, out):
    width = x.shape[1]
    normed, _ = norm(x[...].astype(F32))
    shift = pick(member[...], adaptive[:, :width])
    scale = pick(member[...], adaptive[:, width : 2 * width])
    out[...] = (normed * (1.0 + scale) + shift).astype(BF16)


def first_norm(x, member, adaptive):
    rows, width = x.shape
    tile = min(256, rows)
    return pl.pallas_call(
        first_norm_kernel,
        grid=(rows // tile,),
        out_shape=jax.ShapeDtypeStruct((rows, width), BF16),
        in_specs=[
            pl.BlockSpec((tile, width), lambda i: (i, 0)),
            pl.BlockSpec((tile, 8), lambda i: (i, 0)),
            whole(adaptive.shape),
        ],
        out_specs=pl.BlockSpec((tile, width), lambda i: (i, 0)),
        compiler_params=params(),
        cost_estimate=cost(rows * width * 40, rows * width * 4),
        name="first_norm",
    )(x, member, adaptive)


def turn(values, cosine, sine):
    lanes = values.shape[1]
    place = lax.broadcasted_iota(jnp.int32, (1, 128), 1) % HEAD_DIM
    first = place < HEAD_DIM // 2
    parts = []
    for at in range(0, lanes, 128):
        part = values[:, at : at + 128]
        ahead = pltpu.roll(part, 128 - HEAD_DIM // 2, 1)
        behind = pltpu.roll(part, HEAD_DIM // 2, 1)
        swapped = jnp.where(first, ahead, behind)
        parts.append(part * cosine + swapped * sine)
    return parts[0] if len(parts) == 1 else jnp.concatenate(parts, axis=1)


def project_kernel(place, a, w, cosine, sine, out):
    kind = lax.rem(pl.program_id(0), 3)
    product = dot(a[...], w[...])

    @pl.when(kind == 2)
    def _():
        out[...] = product.astype(BF16)

    @pl.when(kind != 2)
    def _():
        scale = jnp.where(kind == 0, HEAD_DIM**-0.5, 1.0)
        out[...] = (turn(product, cosine[...], sine[...]) * scale).astype(BF16)


def project(place, a, w, cosine, sine, lanes):
    rows, width = a.shape
    columns = w.shape[1]
    return pl.pallas_call(
        project_kernel,
        grid_spec=pltpu.PrefetchScalarGridSpec(
            num_scalar_prefetch=1,
            grid=(columns // lanes,),
            in_specs=[
                pl.BlockSpec((rows, width), lambda i, s: (0, 0)),
                pl.BlockSpec((width, lanes), lambda i, s: (0, i)),
                pl.BlockSpec((rows, 128), lambda i, s: (s[0], 0)),
                pl.BlockSpec((rows, 128), lambda i, s: (s[0], 0)),
            ],
            out_specs=pl.BlockSpec((rows, lanes), lambda i, s: (0, i)),
        ),
        out_shape=jax.ShapeDtypeStruct((rows, columns), BF16),
        compiler_params=params(),
        cost_estimate=cost(2 * rows * width * columns, rows * (width + columns) * 2),
        name="project",
    )(place, a, w, cosine, sine)


def lane_mask(lanes, head):
    return lax.broadcasted_iota(jnp.int32, (1, lanes), 1) // HEAD_DIM == head


def piece_start(place, piece, pieces, rows):
    return pl.multiple_of(lax.rem(place[0] + piece, pieces) * rows, rows)


def flip(values):
    return jnp.transpose(values.astype(F32))


def attend_kernel(pieces, heads, step_q, step_k, place, bounds, seg_col, seg_row, *refs):
    inputs = refs[: 3 * pieces]
    outs = refs[3 * pieces : 4 * pieces]
    lse, q_all, k_all, v_flip, o_all, total = refs[4 * pieces :]
    rows, lanes = inputs[0].shape
    for piece in range(pieces):
        start = piece_start(place, piece, pieces, rows)
        q_all[pl.ds(start, rows), :] = inputs[3 * piece][...]
        k_all[pl.ds(start, rows), :] = inputs[3 * piece + 1][...]
        v_flip[:, pl.ds(start, rows)] = flip(inputs[3 * piece + 2][...]).astype(BF16)

    def one_block(i, _):
        at = pl.multiple_of(i * step_q, step_q)
        query = q_all[pl.ds(at, step_q), :]
        masked = [
            jnp.where(lane_mask(lanes, head), query, jnp.zeros_like(query)) for head in range(heads)
        ]
        seg_q = seg_row[0:1, pl.ds(at, step_q)]
        total[...] = jnp.zeros_like(total)

        def one_key(j, carry):
            highest, sums = carry
            key_at = pl.multiple_of(j * step_k, step_k)
            key = k_all[pl.ds(key_at, step_k), :]
            same = seg_col[pl.ds(key_at, step_k), :] == seg_q
            new_highest, new_sums = [], []
            for head in range(heads):
                scores = jnp.where(same, dot(key, masked[head], NT), MASKED)
                top = jnp.maximum(highest[head], jnp.max(scores, axis=0, keepdims=True))
                weight = jnp.exp(scores - top)
                fade = jnp.exp(highest[head] - top)
                new_highest.append(top)
                new_sums.append(sums[head] * fade + jnp.sum(weight, axis=0, keepdims=True))
                span = pl.ds(head * HEAD_DIM, HEAD_DIM)
                value = v_flip[span, pl.ds(key_at, step_k)]
                total[span, :] = total[span, :] * fade + dot(value, weight.astype(BF16))
            return tuple(new_highest), tuple(new_sums)

        empty = tuple(jnp.full((1, step_q), MASKED, F32) for _ in range(heads))
        zero = tuple(jnp.zeros((1, step_q), F32) for _ in range(heads))
        highest, sums = lax.fori_loop(bounds[0, i], bounds[1, i], one_key, (empty, zero))
        for head in range(heads):
            span = pl.ds(head * HEAD_DIM, HEAD_DIM)
            total[span, :] = total[span, :] / sums[head]
            lse[0, head : head + 1, pl.ds(at, step_q)] = highest[head] + jnp.log(sums[head])
        o_all[pl.ds(at, step_q), :] = flip(total[...]).astype(BF16)
        return 0

    lax.fori_loop(0, q_all.shape[0] // step_q, one_block, 0)
    for piece in range(pieces):
        start = piece_start(place, piece, pieces, rows)
        outs[piece][...] = o_all[pl.ds(start, rows), :]


def attend(place, bounds, seg_col, seg_row, qkv, lanes, step_q, step_k):
    pieces = len(qkv)
    rows, columns = qkv[0].shape
    groups = columns // (3 * lanes)
    heads = lanes // HEAD_DIM
    frames = rows * pieces
    specs = []
    for _ in range(pieces):
        for kind in range(3):
            specs.append(pl.BlockSpec((rows, lanes), lambda g, kind=kind: (0, 3 * g + kind)))
    smem = pl.BlockSpec(memory_space=pltpu.SMEM)
    area = frames * frames // 2 * heads * groups
    results = pl.pallas_call(
        functools.partial(attend_kernel, pieces, heads, step_q, step_k),
        grid=(groups,),
        out_shape=[jax.ShapeDtypeStruct((rows, groups * lanes), BF16)] * pieces
        + [jax.ShapeDtypeStruct((groups, heads, frames), F32)],
        in_specs=[smem, smem, whole(seg_col.shape), whole(seg_row.shape)] + specs,
        out_specs=[pl.BlockSpec((rows, lanes), lambda g: (0, g))] * pieces
        + [pl.BlockSpec((1, heads, frames), lambda g: (g, 0, 0))],
        scratch_shapes=[
            pltpu.VMEM((frames, lanes), BF16),
            pltpu.VMEM((frames, lanes), BF16),
            pltpu.VMEM((lanes, frames), BF16),
            pltpu.VMEM((frames, lanes), BF16),
            pltpu.VMEM((lanes, step_q), F32),
        ],
        compiler_params=params(),
        cost_estimate=cost(area * 4 * 256, frames * columns * 4, area),
        name="attend",
    )(place, bounds, seg_col, seg_row, *[array for array in qkv for _ in range(3)])
    return results[:pieces], results[pieces]


def attend_back_kernel(pieces, heads, step_q, step_k, place, bounds, seg_col, seg_row, *refs):
    inputs = refs[: 5 * pieces]
    lse, cosine, sine = refs[5 * pieces : 5 * pieces + 3]
    outs = refs[5 * pieces + 3 : 6 * pieces + 3]
    q_all, k_all, v_all, o_all, do_all, k_flip, dq_all, dk_all, dv_all, total = refs[6 * pieces + 3 :]
    rows, lanes = inputs[0].shape
    for piece in range(pieces):
        start = piece_start(place, piece, pieces, rows)
        span = pl.ds(start, rows)
        for array, ref in zip((q_all, k_all, v_all, o_all, do_all), inputs[5 * piece : 5 * piece + 5]):
            array[span, :] = ref[...]
        k_flip[:, span] = flip(inputs[5 * piece + 1][...]).astype(BF16)
    dk_all[...] = jnp.zeros_like(dk_all)
    dv_all[...] = jnp.zeros_like(dv_all)
    head_rows = lax.broadcasted_iota(jnp.int32, (8, lanes), 0)
    head_lanes = lax.broadcasted_iota(jnp.int32, (8, lanes), 1) // HEAD_DIM
    head_sum = (head_rows == head_lanes).astype(BF16)

    def one_block(i, _):
        at = pl.multiple_of(i * step_q, step_q)
        block = pl.ds(at, step_q)
        query = q_all[block, :]
        grad = do_all[block, :]
        queries, grads = [], []
        for head in range(heads):
            keep = lane_mask(lanes, head)
            queries.append(jnp.where(keep, query, jnp.zeros_like(query)))
            grads.append(jnp.where(keep, grad, jnp.zeros_like(grad)))
        stacked_queries = jnp.concatenate(queries, axis=0)
        stacked_grads = jnp.concatenate(grads, axis=0)
        product = grad.astype(F32) * o_all[block, :].astype(F32)
        coarse = product.astype(BF16)
        fine = (product - coarse.astype(F32)).astype(BF16)
        centre = dot(head_sum, coarse, NT) + dot(head_sum, fine, NT)
        seg_q = seg_row[0:1, block]
        total[...] = jnp.zeros_like(total)

        def one_key(j, _):
            key_at = pl.multiple_of(j * step_k, step_k)
            span = pl.ds(key_at, step_k)
            key = k_all[span, :]
            value = v_all[span, :]
            same = seg_col[span, :] == seg_q
            weights, slopes = [], []
            for head in range(heads):
                scores = dot(key, queries[head], NT) - lse[0, head : head + 1, block]
                weight = jnp.exp(jnp.where(same, scores, MASKED))
                slope = dot(value, grads[head], NT) - centre[head : head + 1, :]
                slope = (weight * slope).astype(BF16)
                weights.append(weight.astype(BF16))
                slopes.append(slope)
                lines = pl.ds(head * HEAD_DIM, HEAD_DIM)
                total[lines, :] += dot(k_flip[lines, span], slope)
            dv_all[span, :] += dot(jnp.concatenate(weights, axis=1), stacked_grads)
            dk_all[span, :] += dot(jnp.concatenate(slopes, axis=1), stacked_queries)
            return 0

        lax.fori_loop(bounds[0, i], bounds[1, i], one_key, 0)
        dq_all[block, :] = flip(total[...]) * HEAD_DIM**-0.5
        return 0

    lax.fori_loop(0, q_all.shape[0] // step_q, one_block, 0)
    for piece in range(pieces):
        start = piece_start(place, piece, pieces, rows)
        span = pl.ds(start, rows)
        cos = cosine[span, :]
        sin = -sine[span, :]
        outs[piece][:, 0:lanes] = turn(dq_all[span, :], cos, sin).astype(BF16)
        outs[piece][:, lanes : 2 * lanes] = turn(dk_all[span, :], cos, sin).astype(BF16)
        outs[piece][:, 2 * lanes : 3 * lanes] = dv_all[span, :].astype(BF16)


def attend_back(
    place, bounds, seg_col, seg_row, qkv, attended, grads, lse, cosine, sine, lanes, group, step_q, step_k
):
    pieces = len(qkv)
    rows = qkv[0].shape[0]
    heads = lanes // HEAD_DIM
    frames = rows * pieces
    specs, arrays = [], []
    for piece in range(pieces):
        for kind in range(3):
            specs.append(pl.BlockSpec((rows, lanes), lambda i, kind=kind: (0, 3 * group + kind)))
            arrays.append(qkv[piece])
        for array in (attended[piece], grads[piece]):
            specs.append(pl.BlockSpec((rows, lanes), lambda i: (0, group)))
            arrays.append(array)
    smem = pl.BlockSpec(memory_space=pltpu.SMEM)
    area = frames * frames // 2 * heads
    return pl.pallas_call(
        functools.partial(attend_back_kernel, pieces, heads, step_q, step_k),
        grid=(1,),
        out_shape=[jax.ShapeDtypeStruct((rows, 3 * lanes), BF16)] * pieces,
        in_specs=[smem, smem, whole(seg_col.shape, 1), whole(seg_row.shape, 1)]
        + specs
        + [
            pl.BlockSpec((1, heads, frames), lambda i: (group, 0, 0)),
            whole(cosine.shape, 1),
            whole(sine.shape, 1),
        ],
        out_specs=[whole((rows, 3 * lanes), 1)] * pieces,
        scratch_shapes=[pltpu.VMEM((frames, lanes), BF16)] * 5
        + [pltpu.VMEM((lanes, frames), BF16)]
        + [pltpu.VMEM((frames, lanes), F32)] * 3
        + [pltpu.VMEM((lanes, step_q), F32)],
        compiler_params=params(),
        cost_estimate=cost(area * 10 * 256, frames * lanes * 16, area),
        name="attend_back",
    )(place, bounds, seg_col, seg_row, *arrays, lse, cosine, sine)


def gelu_pair(h):
    root = math.sqrt(2.0 / math.pi)
    square = h * h
    bend = jnp.tanh(root * h * (1.0 + 0.044715 * square))
    half = 0.5 * (1.0 + bend)
    slope = half + 0.5 * h * (1.0 - bend * bend) * (root * (1.0 + 0.134145 * square))
    return h * half, slope


def middle_kernel(pieces, *refs):
    x, member, member_flip, adaptive, dy = refs[:5]
    refs = refs[5:]
    attended, refs = refs[:pieces], refs[pieces:]
    w_out, refs = refs[:pieces], refs[pieces:]
    w_up, refs = refs[:pieces], refs[pieces:]
    w_down, refs = refs[:pieces], refs[pieces:]
    mixed, dx2, a2_out, d2_out, d1_out, dadaptive = refs[:6]
    refs = refs[6:]
    active, refs = refs[:pieces], refs[pieces:]
    dhidden, refs = refs[:pieces], refs[pieces:]
    dattended = refs[:pieces]
    width = x.shape[1]
    here = member[...]
    gate1, shift2, scale2, gate2 = (
        pick(here, adaptive[:, n * width : (n + 1) * width]) for n in (2, 3, 4, 5)
    )
    branch1 = sum(dot(attended[p][...], w_out[p][...], NT) for p in range(pieces))
    x2 = x[...].astype(F32) + gate1 * branch1
    n2, r2 = norm(x2)
    a2 = (n2 * (1.0 + scale2) + shift2).astype(BF16)
    a2_out[...] = a2
    branch2 = jnp.zeros_like(x2)
    slopes = []
    for p in range(pieces):
        value, slope = gelu_pair(dot(a2, w_up[p][...]))
        value = value.astype(BF16)
        active[p][...] = value
        slopes.append(slope)
        branch2 = branch2 + dot(value, w_down[p][...], NT)
    mixed[...] = (x2 + gate2 * branch2).astype(BF16)
    upstream = dy[...].astype(F32)
    d2 = (upstream * gate2).astype(BF16)
    d2_out[...] = d2
    da2 = jnp.zeros_like(x2)
    for p in range(pieces):
        dh = (dot(d2, w_down[p][...]) * slopes[p]).astype(BF16)
        dhidden[p][...] = dh
        da2 = da2 + dot(dh, w_up[p][...], NT)
    u2 = da2 * (1.0 + scale2)
    back = upstream + r2 * (
        u2 - jnp.mean(u2, axis=-1, keepdims=True) - n2 * jnp.mean(u2 * n2, axis=-1, keepdims=True)
    )
    dx2[...] = back
    d1 = (back * gate1).astype(BF16)
    d1_out[...] = d1
    for p in range(pieces):
        dattended[p][...] = dot(d1, w_out[p][...]).astype(BF16)

    @pl.when(pl.program_id(0) == 0)
    def _():
        dadaptive[...] = jnp.zeros_like(dadaptive)

    for n, term in enumerate((back * branch1, da2, da2 * n2, upstream * branch2)):
        dadaptive[:, n * width : (n + 1) * width] += pick(member_flip[...], term)


def middle(x, member, member_flip, adaptive, dy, attended, weights):
    pieces = len(attended)
    rows, width = x.shape
    head_columns = attended[0].shape[1]
    hidden = 2 * head_columns
    tile = min(256, rows)

    def tiled(columns):
        return pl.BlockSpec((tile, columns), lambda i: (i, 0))

    def shaped(columns, kind):
        return jax.ShapeDtypeStruct((rows, columns), kind)

    def resident(columns, at):
        return pl.BlockSpec((width, columns), lambda i: (0, at), pipeline_mode=pl.Buffered(1))

    cuts = [resident(head_columns, 4), resident(hidden, 0), resident(hidden, 1)]
    work = 2 * rows * width * pieces * (3 * hidden * 2 + head_columns * 2)
    results = pl.pallas_call(
        functools.partial(middle_kernel, pieces),
        grid=(rows // tile,),
        in_specs=[
            tiled(width),
            tiled(8),
            pl.BlockSpec((8, tile), lambda i: (0, i)),
            whole(adaptive.shape, 1),
            tiled(width),
        ]
        + [tiled(head_columns)] * pieces
        + [cut for cut in cuts for _ in range(pieces)],
        out_shape=[
            shaped(width, BF16),
            shaped(width, F32),
            shaped(width, BF16),
            shaped(width, BF16),
            shaped(width, BF16),
            jax.ShapeDtypeStruct((8, 4 * width), F32),
        ]
        + [shaped(hidden, BF16)] * (2 * pieces)
        + [shaped(head_columns, BF16)] * pieces,
        out_specs=[tiled(width)] * 5
        + [whole((8, 4 * width))]
        + [tiled(hidden)] * (2 * pieces)
        + [tiled(head_columns)] * pieces,
        compiler_params=params(),
        cost_estimate=cost(work, rows * width * 30, rows * hidden * pieces),
        name="middle",
    )(x, member, member_flip, adaptive, dy, *attended, *weights, *weights, *weights)
    head, rest = results[:6], results[6:]
    return head, rest[:pieces], rest[pieces : 2 * pieces], rest[2 * pieces :]


def last_kernel(groups, arrivals, *refs):
    x, member, member_flip, adaptive, dx2 = refs[:5]
    refs = refs[5:]
    arrived, refs = refs[:arrivals], refs[arrivals:]
    slopes, refs = refs[:groups], refs[groups:]
    weights, refs = refs[:groups], refs[groups:]
    grad, dadaptive = refs
    width = x.shape[1]
    normed, inverse = norm(x[...].astype(F32))
    scale = pick(member[...], adaptive[:, width : 2 * width])
    da1 = sum(dot(slopes[g][...], weights[g][...], NT) for g in range(groups))
    for piece in arrived:
        da1 = da1 + piece[...].astype(F32)
    u1 = da1 * (1.0 + scale)
    back = inverse * (
        u1
        - jnp.mean(u1, axis=-1, keepdims=True)
        - normed * jnp.mean(u1 * normed, axis=-1, keepdims=True)
    )
    grad[...] = (dx2[...] + back).astype(BF16)

    @pl.when(pl.program_id(0) == 0)
    def _():
        dadaptive[...] = jnp.zeros_like(dadaptive)

    dadaptive[:, :width] += pick(member_flip[...], da1)
    dadaptive[:, width:] += pick(member_flip[...], da1 * normed)


def last(x, member, member_flip, adaptive, dx2, arrived, slopes, weights):
    rows, width = x.shape
    tile = min(256, rows)

    def tiled(columns):
        return pl.BlockSpec((tile, columns), lambda i: (i, 0))

    return pl.pallas_call(
        functools.partial(last_kernel, len(slopes), len(arrived)),
        grid=(rows // tile,),
        in_specs=[
            tiled(width),
            tiled(8),
            pl.BlockSpec((8, tile), lambda i: (0, i)),
            whole(adaptive.shape, 1),
            tiled(width),
        ]
        + [tiled(width)] * len(arrived)
        + [tiled(s.shape[1]) for s in slopes]
        + [
            pl.BlockSpec(
                (width, s.shape[1]), lambda i, g=g: (0, g), pipeline_mode=pl.Buffered(1)
            )
            for g, s in enumerate(slopes)
        ],
        out_shape=[
            jax.ShapeDtypeStruct((rows, width), BF16),
            jax.ShapeDtypeStruct((8, 2 * width), F32),
        ],
        out_specs=[tiled(width), whole((8, 2 * width))],
        compiler_params=params(),
        cost_estimate=cost(2 * rows * width * sum(s.shape[1] for s in slopes), rows * width * 12),
        name="last",
    )(x, member, member_flip, adaptive, dx2, *arrived, *slopes, *[weights] * len(slopes))


def time_vector(steps, width):
    halfway = width // 2
    rates = jnp.exp(jnp.arange(halfway, dtype=F32) * (-math.log(10000.0) / (halfway - 1)))
    angles = steps.astype(F32)[:, None] * rates[None, :]
    return jnp.concatenate([jnp.sin(angles), jnp.cos(angles)], axis=1)


def body(frames, clip_lengths, timesteps, w_qkv, w_out, w_up, w_down, w_ada, b_ada, grad_out):
    rows, width = frames.shape
    clips = clip_lengths.shape[0]
    pieces = lax.axis_size("hl") * 2
    group_rows = rows * pieces
    own_rows = w_qkv.shape[1]
    head_columns = width // pieces
    lanes = min(256, head_columns)
    groups = head_columns // lanes
    step = min(256, group_rows)
    place = lax.axis_index(SUB).astype(jnp.int32)

    qkv_shard = w_qkv.astype(BF16).reshape(3, own_rows, groups, lanes)
    qkv_shard = jnp.transpose(qkv_shard, (1, 2, 0, 3)).reshape(own_rows, groups * 3 * lanes)
    mlp_shard = jnp.concatenate(
        [w_up.astype(BF16), w_down.astype(BF16).T, w_out.astype(BF16).T], axis=1
    )
    lengths = moved(clip_lengths)
    shards = moved(jnp.concatenate([qkv_shard, mlp_shard], axis=1))
    x = moved(frames)
    qkv_full = gather_plane(shards[:, : 3 * head_columns])
    mlp_own = gather_plane(shards[:, 3 * head_columns :])

    def around(value):
        return [value] + [from_sub(value, step) for step in range(1, pieces)]

    mlp_full = around(mlp_own)

    condition = jax.nn.silu(time_vector(timesteps, width))
    columns = w_ada.shape[1]
    devices = [lax.axis_size(axis) for axis in ALL]
    za, zb, cores, hh, hl = devices
    table = (
        jnp.dot(condition, lax.reduce_precision(w_ada, 8, 7), precision=HIGHEST)
        + lax.reduce_precision(b_ada, 8, 7)[None, :]
    )
    table = table.reshape(za, zb, 1, hh, 1, clips, columns)
    table = jnp.broadcast_to(table, (za, zb, cores, hh, hl, clips, columns))
    table = lax.all_to_all(table.reshape(-1, clips, columns), ALL, 0, 0, tiled=True)
    adaptive = jnp.transpose(table, (1, 0, 2)).reshape(clips, -1)
    adaptive = jnp.pad(adaptive, ((0, 8 - clips), (0, 0)))

    ends = jnp.cumsum(lengths, dtype=jnp.int32)
    starts = ends - lengths
    index = jnp.arange(group_rows, dtype=jnp.int32)
    segment = jnp.sum((index[:, None] >= ends[None, :]).astype(jnp.int32), axis=1, dtype=jnp.int32)
    edges = jnp.concatenate([jnp.zeros((1,), jnp.int32), ends])
    begins = jnp.max(jnp.where(index[:, None] >= edges[None, :], edges[None, :], 0), axis=1)
    position = (index - begins).astype(F32)
    lane = jnp.arange(128, dtype=jnp.int32) % HEAD_DIM
    rates = jnp.exp((lane % (HEAD_DIM // 2)).astype(F32) * (-2.0 * math.log(10000.0) / HEAD_DIM))
    angles = position[:, None] * rates[None, :]
    cosine = jnp.cos(angles)
    sine = jnp.sin(angles) * jnp.where(lane < HEAD_DIM // 2, -1.0, 1.0)[None, :]
    seg_col = segment[:, None]
    seg_row = segment[None, :]
    block_first = jnp.arange(0, group_rows, step, dtype=jnp.int32)
    first_seg = jnp.sum((block_first[:, None] >= ends[None, :]).astype(jnp.int32), axis=1)
    last_seg = jnp.sum((block_first[:, None] + (step - 1) >= ends[None, :]).astype(jnp.int32), axis=1)
    closing = jnp.concatenate([ends, jnp.full((1,), group_rows, jnp.int32)])
    low_at = jnp.sum(jnp.where(first_seg[:, None] == jnp.arange(clips + 1)[None, :], edges[None, :], 0), axis=1)
    high_at = jnp.sum(jnp.where(last_seg[:, None] == jnp.arange(clips + 1)[None, :], closing[None, :], 0), axis=1)
    bounds = jnp.stack([low_at // step, (high_at + step - 1) // step]).astype(jnp.int32)
    own_index = place * rows + jnp.arange(rows, dtype=jnp.int32)
    member = ((own_index[:, None] >= starts[None, :]) & (own_index[:, None] < ends[None, :])).astype(F32)
    member = jnp.pad(member, ((0, 0), (0, 8 - clips)))
    member_flip = member.T

    a1 = first_norm(x, member, adaptive)
    dy = moved(lax.optimization_barrier((grad_out, a1))[0])
    a1_all = around(a1)
    places = [((place + piece) % pieces).reshape(1) for piece in range(pieces)]
    qkv = [
        project(places[piece], a1_all[piece], qkv_full, cosine, sine, lanes)
        for piece in range(pieces)
    ]
    at_place = place.reshape(1)
    attended, lse = attend(at_place, bounds, seg_col, seg_row, qkv, lanes, step, step)
    attended_own = [attended[0]] + [
        from_sub_piece(attended, step_) for step_ in range(1, pieces)
    ]

    head, active, dhidden, dattended = middle(
        x, member, member_flip, adaptive, dy, attended_own, mlp_full
    )
    mixed, dx2, a2, d2, d1, dada_late = head
    grads_attended = [dattended[0]] + [
        from_sub_piece(dattended, step_) for step_ in range(1, pieces)
    ]
    mixed_back = moved_back(mixed)

    def summed(left, right):
        parts = [dot(left, part, TN).astype(BF16) for part in right]
        return [parts[0]] + [to_sub(parts[step], step) for step in range(1, pieces)]

    late = reduce_plane([summed(a2, dhidden), summed(d2, active), summed(d1, attended_own)])
    late = moved_back(late)
    hidden_columns = w_up.shape[1]
    grad_up = late[:, :hidden_columns]
    grad_down = late[:, hidden_columns : 2 * hidden_columns]
    grad_outw = late[:, 2 * hidden_columns :]

    slopes, grad_groups = [], []
    for group in range(groups):
        dqkv = attend_back(
            at_place, bounds, seg_col, seg_row, qkv, attended, grads_attended, lse, cosine, sine,
            lanes, group, step, step,
        )
        slopes.append(dqkv)
        total = sum(dot(a1_all[piece], dqkv[piece], TN) for piece in range(pieces)).astype(BF16)
        grad_groups.append(moved_back(reduce_plane([[total]])))
    arrived = []
    for piece in range(1, pieces):
        part = sum(
            dot(slopes[g][piece], qkv_full[:, 3 * lanes * g : 3 * lanes * (g + 1)], NT)
            for g in range(groups)
        ).astype(BF16)
        arrived.append(to_sub(part, piece))
    grad_frames, dada_early = last(
        x, member, member_flip, adaptive, dx2, arrived, [s[0] for s in slopes], qkv_full
    )
    grad_frames = moved_back(grad_frames).astype(F32)

    dadaptive = jnp.concatenate([dada_early, dada_late], axis=1)[:clips]
    dadaptive = jnp.transpose(dadaptive.reshape(clips, -1, columns), (1, 0, 2))
    dadaptive = lax.all_to_all(dadaptive, ALL, 0, 0, tiled=True)
    dadaptive = dadaptive.reshape(za, zb, cores, hh, hl, clips, columns)
    dadaptive = jnp.sum(dadaptive, axis=(2, 4)).reshape(-1, columns)
    grad_ada = dot(condition, dadaptive, TN, HIGHEST)
    grad_bias = jnp.sum(dadaptive, axis=0)

    grad_qkv = jnp.stack(grad_groups, axis=1).reshape(own_rows, groups, 3, lanes)
    grad_qkv = jnp.transpose(grad_qkv, (2, 0, 1, 3)).reshape(w_qkv.shape).astype(F32)
    return (
        mixed_back,
        grad_frames,
        grad_qkv,
        grad_outw.astype(F32).T,
        grad_up.astype(F32),
        grad_down.astype(F32).T,
        grad_ada,
        grad_bias,
    )


def from_sub_piece(parts, step):
    pieces = len(parts)
    return from_sub(parts[pieces - step], step)


def solution(mesh):
    clip, head = mesh.shape["clip"], mesh.shape["head"]
    fine = Mesh(mesh.devices.reshape(clip // 4, 2, 2, 2, head // 2), ALL)
    by_clip = ("za", "zb", "core")
    by_head = ("hh", "hl")
    everywhere = by_clip + by_head
    placed = (
        P(everywhere, None),
        P(by_clip),
        P(),
        P(None, by_clip, by_head),
        P(by_head, by_clip),
        P(by_clip, by_head),
        P(by_head, by_clip),
        P(None, everywhere),
        P(everywhere),
        P(everywhere, None),
    )
    return jax.shard_map(
        body,
        mesh=fine,
        in_specs=placed,
        out_specs=(
            P(everywhere, None),
            P(everywhere, None),
            P(None, by_clip, by_head),
            P(by_head, by_clip),
            P(by_clip, by_head),
            P(by_head, by_clip),
            P(None, everywhere),
            P(everywhere),
        ),
        check_vma=False,
    )
```

time: 2220 us -> 713 us (0.32)
  the two profiles are of different devices: /device:TPU:1 before, /device:TPU:0 now
where the time goes in v1:
time: 713 us; the launch traced here: 701 us
  Pallas kernels  332 us (47%)
  starting transfers between devices  136 us (19%)
  waiting for transfers between devices  133 us (19%)
  matrix products  41.5 us (6%)
  other arithmetic  28.9 us (4%)
  local copies, waits for them, and re-layouts  26.9 us (4%)
    pallas_call x2, Pallas kernels, attend_back(): pl.pallas_call(functools.partial(attend_back_kernel, pieces, heads, step_...  133 us
    pallas_call x1, Pallas kernels, attend(): pl.pallas_call(functools.partial(attend_kernel, pieces, heads, step_q, st...  88 us
    pallas_call x1, Pallas kernels, middle(): pl.pallas_call(functools.partial(middle_kernel, pieces), grid=(rows // ti...  53.6 us
    dot_general x13, matrix products, dot(): lax.dot_general(a, b, dims, precision=precision, preferred_element_type=F32)  40 us
    ppermute x5, starting transfers between devices, moved_back(): return lax.ppermute(value, MOVE, pairs)  38.4 us
    ppermute x10, waiting for transfers between devices, across(): return lax.ppermute(value, 'za', [(i, i ^ bit) for i in range(size)])  37.3 us
    ppermute x2, waiting for transfers between devices, gather_plane(): by_hh = lax.ppermute(held, 'hh', SWAP)  32.5 us
    ppermute x3, waiting for transfers between devices, reduce_plane(): from_zb = lax.ppermute(to_zb, 'zb', SWAP)  27.6 us
  transfers between devices with their start and end apart: 49, of which 15 were waited for; matrix products, arithmetic and copies ran while one was open for 12% of the time, Pallas kernels for 40%

profile of v1, /device:TPU:0, one launch (start us, length us, event | category | flops | bytes accessed | tf_op | source)
XLA Modules:
  0.0 700.9 jit_solution(15846707802357954820)
XLA Ops:
  8.2 8.6 %collective-permute-done.12 = bf16[1,64,2560]{2,1,0:T(8,128)(2,1)S(1)} collective-permute-done((bf16[1,64,2560]{2,1,0:T(8,128)(2,1)S(1)}, bf16[1,64,2560]{2,1,0:T(8,128)(2,1)S(1)}, u32[]{:S(2)}, u32[]{:S(2)}) %collective-permute-start.12) | collective-permute-done | bytes 327712 | tf_op jit(solution)/shard_map/ppermute | solution.py:85
  21.4 9.7 %collective-permute-done.13 = bf16[2,64,2560]{2,1,0:T(8,128)(2,1)S(1)} collective-permute-done((bf16[2,64,2560]{2,1,0:T(8,128)(2,1)S(1)}, bf16[2,64,2560]{2,1,0:T(8,128)(2,1)S(1)}, u32[]{:S(2)}, u32[]{:S(2)}) %collective-permute-start.13) | collective-permute-done | bytes 655392 | tf_op jit(solution)/shard_map/ppermute | solution.py:85
  33.4 6.8 collective-permute-start.15
  52.0 7.1 %collective-permute-done.14.by_zb = bf16[4,64,2560]{2,1,0:T(8,128)(2,1)} collective-permute-done((bf16[4,64,2560]{2,1,0:T(8,128)(2,1)S(1)}, bf16[4,64,2560]{2,1,0:T(8,128)(2,1)}, u32[]{:S(2)}, u32[]{:S(2)}) %collective-permute-start.14) | collective-permute-done | bytes 1310752 | tf_op jit(solution)/shard_map/ppermute | solution.py:113
  63.7 32.5 %collective-permute-done.15.by_hh = bf16[4,64,2560]{2,1,0:T(8,128)(2,1)} collective-permute-done((bf16[4,64,2560]{2,1,0:T(8,128)(2,1)S(1)}, bf16[4,64,2560]{2,1,0:T(8,128)(2,1)}, u32[]{:S(2)}, u32[]{:S(2)}) %collective-permute-start.15) | collective-permute-done | bytes 1310752 | tf_op jit(solution)/shard_map/ppermute | solution.py:114
  120.6 9.3 %first_norm.1.a = bf16[1024,1024]{1,0:T(8,128)(2,1)} custom-call(bf16[1024,1024]{1,0:T(8,128)(2,1)} %copy-done.1, f32[1024,8]{1,0:T(8,128)} %copy.221.member.refs_1_, f32[8,6144]{1,0:T(8,128)} %pad.18.adaptive.refs_3_), custom_call_target="tpu_custom_call" | custom-call | flops 41943040 | bytes 4194304 | tf_op jit(solution)/shard_map/first_norm/pallas_call | solution.py:202
  137.9 13.3 %collective-permute-done.6.by_zb = bf16[4,64,1536]{2,1,0:T(8,128)(2,1)S(1)} collective-permute-done((bf16[4,64,1536]{2,1,0:T(8,128)(2,1)S(1)}, bf16[4,64,1536]{2,1,0:T(8,128)(2,1)S(1)}, u32[]{:S(2)}, u32[]{:S(2)}) %collective-permute-start.6) | collective-permute-done | bytes 786464 | tf_op jit(solution)/shard_map/ppermute | solution.py:113
  161.0 17.1 %collective-permute-start.2 = (bf16[1024,1024]{1,0:T(8,128)(2,1)}, bf16[1024,1024]{1,0:T(8,128)(2,1)}, u32[]{:S(2)}, u32[]{:S(2)}) collective-permute-start(bf16[1024,1024]{1,0:T(8,128)(2,1)} %param.19), channel_id=1, source_target_pairs={{0,0},{1,2},{2,1},{3,3},{4,4},{5,6},{6,5},{7,7},{8,8},{9,10},{10,9... | collective-permute-start | bytes 6291464 | tf_op jit(solution)/shard_map/ppermute | solution.py:62
  184.6 10.4 %project.2.refs_0_.refs_1_.refs_2_ = bf16[1024,1536]{1,0:T(8,128)(2,1)} custom-call(s32[1]{0:T(128)} %bitcast.10.place, bf16[1024,1024]{1,0:T(8,128)(2,1)} %first_norm.1.a, bf16[1024,1536]{1,0:T(8,128)(2,1)} %bitcast.232, f32[2048,128]{1,0:T(8,128)} %get-tuple-element.79.cosine.refs_11_, f32[2048,128]{1,0:T(8,128)} %get-tuple-element.78.sine.refs_12_), custom_call_target="tpu_custom_call" | custom-call | flops 3221225472 | bytes 5242880 | tf_op jit(solution)/shard_map/project/pallas_call | solution.py:249
  195.1 10.4 %project.3.refs_3_.refs_4_.refs_5_.refs_6_.refs_7_ = bf16[1024,1536]{1,0:T(8,128)(2,1)} custom-call(s32[1]{0:T(128)} %bitcast.22.place, bf16[1024,1024]{1,0:T(8,128)(2,1)} %collective-permute-done.10.a, bf16[1024,1536]{1,0:T(8,128)(2,1)} %bitcast.233, f32[2048,128]{1,0:T(8,128)} %get-tuple-element.79.cosine.refs_11_, f32[2048,128]{1,0:T(8,128)} %get-tuple-element.78.sine.refs_12_), custom_call_target="tpu_custom_call" | custom-call | flops 3221225472 | bytes 5242880 | tf_op jit(solution)/shard_map/project/pallas_call | solution.py:249
  205.5 88.0 %attend.1 = (bf16[1024,512]{1,0:T(8,128)(2,1)}, bf16[1024,512]{1,0:T(8,128)(2,1)}, f32[2,4,2048]{2,1,0:T(4,128)}) custom-call(s32[1]{0:T(128)} %bitcast.5.place, s32[2,8]{1,0:T(2,128)} %pad_add_fusion.bounds, s32[2048,1]{1,0:T(8,128)} %copy.220.seg_col, s32[1,2048]{1,0:T(1,128)} %bitcast.263, bf16[1024,1536]{1,0:T(8,128)(2,1)} %project.2.refs_0_.refs_1_.refs_2_, ...), custom_call_target="tpu_custom_call" | custom-call | flops 17179869184 | bytes 12582912 | tf_op jit(solution)/shard_map/attend/pallas_call | solution.py:347
  297.4 53.6 %middle.1 = (bf16[1024,1024]{1,0:T(8,128)(2,1)}, f32[1024,1024]{1,0:T(8,128)}, bf16[1024,1024]{1,0:T(8,128)(2,1)}, bf16[1024,1024]{1,0:T(8,128)(2,1)}, bf16[1024...) custom-call(bf16[1024,1024]{1,0:T(8,128)(2,1)} %copy-done.1, ...), custom_call_target="tpu_custom_call" | custom-call | flops 30064771072 | bytes 31457280 | tf_op jit(solution)/shard_map/middle/pallas_call | solution.py:564
  351.2 6.1 convolution_convert_fusion.2
  373.1 66.4 %attend_back.2 = (bf16[1024,768]{1,0:T(8,128)(2,1)}, bf16[1024,768]{1,0:T(8,128)(2,1)}) custom-call(s32[1]{0:T(128)} %bitcast.5.place, s32[2,8]{1,0:T(2,128)} %pad_add_fusion.bounds, s32[2048,1]{1,0:T(8,128)} %copy.220.seg_col, s32[1,2048]{1,0:T(1,128)} %bitcast.264, bf16[1024,1536]{1,0:T(8,128)(2,1)} %project.2.refs_0_.refs_1_.refs_2_, ...), custom_call_target="tpu_custom_call" | custom-call | flops 21474836480 | bytes 8388608 | tf_op jit(solution)/shard_map/attend_back/pallas_call | solution.py:458
  447.0 14.8 %collective-permute-start.25 = (bf16[2,64,768]{2,1,0:T(8,128)(2,1)S(1)}, bf16[2,64,768]{2,1,0:T(8,128)(2,1)S(1)}, u32[]{:S(2)}, u32[]{:S(2)}) collective-permute-start(bf16[2,64,768]{2,1,0:T(8,128)(2,1)S(1)} %get-tuple-element.69), channel_id=1, source_target_pairs={{0,4},{4,0},{1,5},{5,1},{2,6},{6,2},{3,7},{7,3},{8,12},{12,8},{9,1... | collective-permute-start | bytes 589832 | tf_op jit(solution)/shard_map/ppermute | solution.py:161
  461.8 66.5 %attend_back.3 = (bf16[1024,768]{1,0:T(8,128)(2,1)}, bf16[1024,768]{1,0:T(8,128)(2,1)}) custom-call(s32[1]{0:T(128)} %bitcast.5.place, s32[2,8]{1,0:T(2,128)} %pad_add_fusion.bounds, s32[2048,1]{1,0:T(8,128)} %copy.220.seg_col, s32[1,2048]{1,0:T(1,128)} %bitcast.265, bf16[1024,1536]{1,0:T(8,128)(2,1)} %project.2.refs_0_.refs_1_.refs_2_, ...), custom_call_target="tpu_custom_call" | custom-call | flops 21474836480 | bytes 8388608 | tf_op jit(solution)/shard_map/attend_back/pallas_call | solution.py:458
  555.5 10.0 %collective-permute-done.40 = bf16[2,64,2560]{2,1,0:T(8,128)(2,1)S(1)} collective-permute-done((bf16[2,64,2560]{2,1,0:T(8,128)(2,1)S(1)}, bf16[2,64,2560]{2,1,0:T(8,128)(2,1)S(1)}, u32[]{:S(2)}, u32[]{:S(2)}) %collective-permute-start.40) | collective-permute-done | bytes 655392 | tf_op jit(solution)/shard_map/ppermute | solution.py:160
  567.8 7.2 %collective-permute-done.24 = bf16[4,64,768]{2,1,0:T(8,128)(2,1)S(1)} collective-permute-done((bf16[4,64,768]{2,1,0:T(8,128)(2,1)S(1)}, bf16[4,64,768]{2,1,0:T(8,128)(2,1)S(1)}, u32[]{:S(2)}, u32[]{:S(2)}) %collective-permute-start.24) | collective-permute-done | bytes 393248 | tf_op jit(solution)/shard_map/ppermute | solution.py:165
  576.3 7.2 %collective-permute-done.31 = bf16[4,64,768]{2,1,0:T(8,128)(2,1)S(1)} collective-permute-done((bf16[4,64,768]{2,1,0:T(8,128)(2,1)S(1)}, bf16[4,64,768]{2,1,0:T(8,128)(2,1)S(1)}, u32[]{:S(2)}, u32[]{:S(2)}) %collective-permute-start.31) | collective-permute-done | bytes 393248 | tf_op jit(solution)/shard_map/ppermute | solution.py:165
  597.2 13.1 %collective-permute-done.41 = bf16[4,64,2560]{2,1,0:T(8,128)(2,1)S(1)} collective-permute-done((bf16[4,64,2560]{2,1,0:T(8,128)(2,1)S(1)}, bf16[4,64,2560]{2,1,0:T(8,128)(2,1)S(1)}, u32[]{:S(2)}, u32[]{:S(2)}) %collective-permute-start.41) | collective-permute-done | bytes 1310752 | tf_op jit(solution)/shard_map/ppermute | solution.py:165
  616.9 17.1 %collective-permute-start.19 = (bf16[1024,1024]{1,0:T(8,128)(2,1)}, bf16[1024,1024]{1,0:T(8,128)(2,1)}, u32[]{:S(2)}, u32[]{:S(2)}) collective-permute-start(bf16[1024,1024]{1,0:T(8,128)(2,1)} %get-tuple-element.33), channel_id=1, source_target_pairs={{0,0},{2,1},{1,2},{3,3},{4,4},{6,5},{5,6},{7,7},{8,8},{10,9},{9,10... | collective-permute-start | bytes 6291464 | tf_op jit(solution)/shard_map/ppermute | solution.py:67
  637.9 17.0 %last.1 = (bf16[1024,1024]{1,0:T(8,128)(2,1)}, f32[8,2048]{1,0:T(8,128)}) custom-call(bf16[1024,1024]{1,0:T(8,128)(2,1)} %copy-done.1, f32[1024,8]{1,0:T(8,128)} %copy.221.member.refs_1_, f32[8,1024]{1,0:T(8,128)} %get-tuple-element.80.refs_2_, f32[8,6144]{1,0:T(8,128)} %pad.18.adaptive.refs_3_, f32[1024,1024]{1,0:T(8,128)} %get-tuple-element.34.refs_4_, ...), custom_call_target="tpu_custom_call" | custom-call | flops 3221225472 | bytes 12582912 | tf_op jit(solution)/shard_map/last/pallas_call | solution.py:634
  654.9 17.2 %collective-permute-start.22 = (bf16[1024,1024]{1,0:T(8,128)(2,1)}, bf16[1024,1024]{1,0:T(8,128)(2,1)}, u32[]{:S(2)}, u32[]{:S(2)}) collective-permute-start(bf16[1024,1024]{1,0:T(8,128)(2,1)} %get-tuple-element.42), channel_id=1, source_target_pairs={{0,0},{2,1},{1,2},{3,3},{4,4},{6,5},{5,6},{7,7},{8,8},{10,9},{9,10... | collective-permute-start | bytes 6291464 | tf_op jit(solution)/shard_map/ppermute | solution.py:67
  678.9 8.2 %collective-permute-done.45 = bf16[1,64,2560]{2,1,0:T(8,128)(2,1)S(1)} collective-permute-done((bf16[1,64,2560]{2,1,0:T(8,128)(2,1)S(1)}, bf16[1,64,2560]{2,1,0:T(8,128)(2,1)S(1)}, u32[]{:S(2)}, u32[]{:S(2)}) %collective-permute-start.45) | collective-permute-done | bytes 327712 | tf_op jit(solution)/shard_map/ppermute | solution.py:85
  (279 shorter events, 181.1 us)
Async XLA Ops:
  17.9 32.5 %collective-permute-start.1 = (s32[4]{0:T(128)S(1)}, s32[4]{0:T(128)}, u32[]{:S(2)}, u32[]{:S(2)}) collective-permute-start(s32[4]{0:T(128)S(1)} %copy-done.36), channel_id=1, source_target_pairs={{0,0},{1,2},{2,1},{3,3},{4,4},{5,6},{6,5},{7,7},{8,8},{9,10},{10,9... | collective-permute-start | bytes 56 | tf_op jit(solution)/shard_map/ppermute | solution.py:62
  19.1 100.2 %collective-permute-start = (bf16[1024,1024]{1,0:T(8,128)(2,1)}, bf16[1024,1024]{1,0:T(8,128)(2,1)S(1)}, u32[]{:S(2)}, u32[]{:S(2)}) collective-permute-start(bf16[1024,1024]{1,0:T(8,128)(2,1)} %param.10), channel_id=1, source_target_pairs={{0,0},{1,2},{2,1},{3,3},{4,4},{5,6},{6,5},{7,7},{8,8},{9,10},{10,9... | collective-permute-start | bytes 6291464 | tf_op jit(solution)/shard_map/ppermute | solution.py:62
  31.2 27.9 %collective-permute-start.14 = (bf16[4,64,2560]{2,1,0:T(8,128)(2,1)S(1)}, bf16[4,64,2560]{2,1,0:T(8,128)(2,1)}, u32[]{:S(2)}, u32[]{:S(2)}) collective-permute-start(bf16[4,64,2560]{2,1,0:T(8,128)(2,1)S(1)} %pad_maximum_fusion.own), channel_id=1, source_target_pairs={{0,4},{4,0},{1,5},{5,1},{2,6},{6,2},{3,7},{7,3},{8,12},{12,8},{9,1... | collective-permute-start | bytes 3932168 | tf_op jit(solution)/shard_map/ppermute | solution.py:113
  33.4 62.8 %collective-permute-start.15 = (bf16[4,64,2560]{2,1,0:T(8,128)(2,1)S(1)}, bf16[4,64,2560]{2,1,0:T(8,128)(2,1)}, u32[]{:S(2)}, u32[]{:S(2)}) collective-permute-start(bf16[4,64,2560]{2,1,0:T(8,128)(2,1)S(1)} %pad_maximum_fusion.own), channel_id=1, source_target_pairs={{0,1},{1,0},{2,3},{3,2},{4,5},{5,4},{6,7},{7,6},{8,9},{9,8},{10,11... | collective-permute-start | bytes 3932168 | tf_op jit(solution)/shard_map/ppermute | solution.py:114
  44.6 73.9 %all-to-all-start = ((f32[32,4,192]{2,1,0:T(4,128)}), f32[32,4,192]{2,1,0:T(4,128)S(1)}, u32[]{:S(2)}, u32[]{:S(2)}) async-start(f32[32,4,192]{2,1,0:T(4,128)} %bitcast.261), calls=%async_computation | async-start | bytes 262144 | tf_op jit(solution)/shard_map/all_to_all | solution.py:708
  60.2 48.7 %collective-permute-start.16 = (bf16[2,64,2560]{2,1,0:T(8,128)(2,1)S(1)}, bf16[2,64,2560]{2,1,0:T(8,128)(2,1)S(1)}, u32[]{:S(2)}, u32[]{:S(2)}) collective-permute-start(bf16[2,64,2560]{2,1,0:T(8,128)(2,1)S(1)} %slice.92), channel_id=1, source_target_pairs={{0,1},{1,0},{2,3},{3,2},{4,5},{5,4},{6,7},{7,6},{8,9},{9,8},{10,11... | collective-permute-start | bytes 1966088 | tf_op jit(solution)/shard_map/ppermute | solution.py:115
  117.3 179.1 %collective-permute-start.18 = (bf16[1024,2560]{1,0:T(8,128)(2,1)}, bf16[1024,2560]{1,0:T(8,128)(2,1)}, u32[]{:S(2)}, u32[]{:S(2)}) collective-permute-start(bf16[1024,2560]{1,0:T(8,128)(2,1)} %bitcast.238), channel_id=1, source_target_pairs={{2,0},{0,2},{3,1},{1,3},{6,4},{4,6},{7,5},{5,7},{10,8},{8,10},{11,... | collective-permute-start | bytes 15728648 | tf_op jit(solution)/shard_map/ppermute | solution.py:72
  129.9 65.2 %collective-permute-start.10 = (bf16[1024,1024]{1,0:T(8,128)(2,1)}, bf16[1024,1024]{1,0:T(8,128)(2,1)}, u32[]{:S(2)}, u32[]{:S(2)}) collective-permute-start(bf16[1024,1024]{1,0:T(8,128)(2,1)} %first_norm.1.a), channel_id=1, source_target_pairs={{2,0},{0,2},{3,1},{1,3},{6,4},{4,6},{7,5},{5,7},{10,8},{8,10},{11,... | collective-permute-start | bytes 6291464 | tf_op jit(solution)/shard_map/ppermute | solution.py:72
  151.3 26.9 %collective-permute-start.8 = (bf16[2,64,1536]{2,1,0:T(8,128)(2,1)S(1)}, bf16[2,64,1536]{2,1,0:T(8,128)(2,1)S(1)}, u32[]{:S(2)}, u32[]{:S(2)}) collective-permute-start(bf16[2,64,1536]{2,1,0:T(8,128)(2,1)S(1)} %slice.89), channel_id=1, source_target_pairs={{0,1},{1,0},{2,3},{3,2},{4,5},{5,4},{6,7},{7,6},{8,9},{9,8},{10,11... | collective-permute-start | bytes 1179656 | tf_op jit(solution)/shard_map/ppermute | solution.py:115
  153.7 24.5 %collective-permute-start.9 = (bf16[2,64,1536]{2,1,0:T(8,128)(2,1)S(1)}, bf16[2,64,1536]{2,1,0:T(8,128)(2,1)S(1)}, u32[]{:S(2)}, u32[]{:S(2)}) collective-permute-start(bf16[2,64,1536]{2,1,0:T(8,128)(2,1)S(1)} %slice.90), channel_id=1, source_target_pairs={{0,4},{4,0},{1,5},{5,1},{2,6},{6,2},{3,7},{7,3},{8,12},{12,8},{9,1... | collective-permute-start | bytes 1179656 | tf_op jit(solution)/shard_map/ppermute | solution.py:116
  161.0 132.6 %collective-permute-start.2 = (bf16[1024,1024]{1,0:T(8,128)(2,1)}, bf16[1024,1024]{1,0:T(8,128)(2,1)}, u32[]{:S(2)}, u32[]{:S(2)}) collective-permute-start(bf16[1024,1024]{1,0:T(8,128)(2,1)} %param.19), channel_id=1, source_target_pairs={{0,0},{1,2},{2,1},{3,3},{4,4},{5,6},{6,5},{7,7},{8,8},{9,10},{10,9... | collective-permute-start | bytes 6291464 | tf_op jit(solution)/shard_map/ppermute | solution.py:62
  351.0 22.2 %collective-permute-start.20 = (bf16[1024,512]{1,0:T(8,128)(2,1)}, bf16[1024,512]{1,0:T(8,128)(2,1)}, u32[]{:S(2)}, u32[]{:S(2)}) collective-permute-start(bf16[1024,512]{1,0:T(8,128)(2,1)} %get-tuple-element.36), channel_id=1, source_target_pairs={{2,0},{0,2},{3,1},{1,3},{6,4},{4,6},{7,5},{5,7},{10,8},{8,10},{11,... | collective-permute-start | bytes 3145736 | tf_op jit(solution)/shard_map/ppermute | solution.py:72
  357.3 181.7 %collective-permute-start.37 = (bf16[1024,1024]{1,0:T(8,128)(2,1)}, bf16[1024,1024]{1,0:T(8,128)(2,1)}, u32[]{:S(2)}, u32[]{:S(2)}) collective-permute-start(bf16[1024,1024]{1,0:T(8,128)(2,1)} %convolution_convert_fusion.2), channel_id=1, source_target_pairs={{0,2},{2,0},{1,3},{3,1},{4,6},{6,4},{5,7},{7,5},{8,10},{10,8},{9,1... | collective-permute-start | bytes 6291464 | tf_op jit(solution)/shard_map/ppermute | solution.py:77
  361.4 185.3 %collective-permute-start.38 = (bf16[1024,1024]{1,0:T(8,128)(2,1)}, bf16[1024,1024]{1,0:T(8,128)(2,1)S(1)}, u32[]{:S(2)}, u32[]{:S(2)}) collective-permute-start(bf16[1024,1024]{1,0:T(8,128)(2,1)} %convolution_convert_fusion), channel_id=1, source_target_pairs={{0,2},{2,0},{1,3},{3,1},{4,6},{6,4},{5,7},{7,5},{8,10},{10,8},{9,1... | collective-permute-start | bytes 6291464 | tf_op jit(solution)/shard_map/ppermute | solution.py:77
  365.2 169.4 %collective-permute-start.39 = (bf16[1024,512]{1,0:T(8,128)(2,1)}, bf16[1024,512]{1,0:T(8,128)(2,1)}, u32[]{:S(2)}, u32[]{:S(2)}) collective-permute-start(bf16[1024,512]{1,0:T(8,128)(2,1)} %convolution_convert_fusion.4), channel_id=1, source_target_pairs={{0,2},{2,0},{1,3},{3,1},{4,6},{6,4},{5,7},{7,5},{8,10},{10,8},{9,1... | collective-permute-start | bytes 3145736 | tf_op jit(solution)/shard_map/ppermute | solution.py:77
  446.9 102.1 %collective-permute-start.23 = (bf16[2,64,768]{2,1,0:T(8,128)(2,1)S(1)}, bf16[2,64,768]{2,1,0:T(8,128)(2,1)S(1)}, u32[]{:S(2)}, u32[]{:S(2)}) collective-permute-start(bf16[2,64,768]{2,1,0:T(8,128)(2,1)S(1)} %get-tuple-element.68), channel_id=1, source_target_pairs={{0,1},{1,0},{2,3},{3,2},{4,5},{5,4},{6,7},{7,6},{8,9},{9,8},{10,11... | collective-permute-start | bytes 589832 | tf_op jit(solution)/shard_map/ppermute | solution.py:160
  447.0 105.3 %collective-permute-start.25 = (bf16[2,64,768]{2,1,0:T(8,128)(2,1)S(1)}, bf16[2,64,768]{2,1,0:T(8,128)(2,1)S(1)}, u32[]{:S(2)}, u32[]{:S(2)}) collective-permute-start(bf16[2,64,768]{2,1,0:T(8,128)(2,1)S(1)} %get-tuple-element.69), channel_id=1, source_target_pairs={{0,4},{4,0},{1,5},{5,1},{2,6},{6,2},{3,7},{7,3},{8,12},{12,8},{9,1... | collective-permute-start | bytes 589832 | tf_op jit(solution)/shard_map/ppermute | solution.py:161
  552.3 84.3 %collective-permute-start.21 = (bf16[1024,1024]{1,0:T(8,128)(2,1)}, bf16[1024,1024]{1,0:T(8,128)(2,1)S(1)}, u32[]{:S(2)}, u32[]{:S(2)}) collective-permute-start(bf16[1024,1024]{1,0:T(8,128)(2,1)} %add_convert_fusion), channel_id=1, source_target_pairs={{0,2},{2,0},{1,3},{3,1},{4,6},{6,4},{5,7},{7,5},{8,10},{10,8},{9,1... | collective-permute-start | bytes 6291464 | tf_op jit(solution)/shard_map/ppermute | solution.py:77
  552.4 22.6 %collective-permute-start.24 = (bf16[4,64,768]{2,1,0:T(8,128)(2,1)S(1)}, bf16[4,64,768]{2,1,0:T(8,128)(2,1)S(1)}, u32[]{:S(2)}, u32[]{:S(2)}) collective-permute-start(bf16[4,64,768]{2,1,0:T(8,128)(2,1)S(1)} %get-tuple-element.66), channel_id=1, source_target_pairs={{0,4},{4,0},{1,5},{5,1},{2,6},{6,2},{3,7},{7,3},{8,12},{12,8},{9,1... | collective-permute-start | bytes 1179656 | tf_op jit(solution)/shard_map/ppermute | solution.py:165
  575.1 35.3 %collective-permute-start.41 = (bf16[4,64,2560]{2,1,0:T(8,128)(2,1)S(1)}, bf16[4,64,2560]{2,1,0:T(8,128)(2,1)S(1)}, u32[]{:S(2)}, u32[]{:S(2)}) collective-permute-start(bf16[4,64,2560]{2,1,0:T(8,128)(2,1)S(1)} %fusion.2), channel_id=1, source_target_pairs={{0,4},{4,0},{1,5},{5,1},{2,6},{6,2},{3,7},{7,3},{8,12},{12,8},{9,1... | collective-permute-start | bytes 3932168 | tf_op jit(solution)/shard_map/ppermute | solution.py:165
  575.1 35.3 %collective-permute-start.43 = (bf16[4,64,2560]{2,1,0:T(8,128)(2,1)S(1)}, bf16[4,64,2560]{2,1,0:T(8,128)(2,1)S(1)}, u32[]{:S(2)}, u32[]{:S(2)}) collective-permute-start(bf16[4,64,2560]{2,1,0:T(8,128)(2,1)S(1)} %fusion.3), channel_id=1, source_target_pairs={{0,1},{1,0},{2,3},{3,2},{4,5},{5,4},{6,7},{7,6},{8,9},{9,8},{10,11... | collective-permute-start | bytes 3932168 | tf_op jit(solution)/shard_map/ppermute | solution.py:166
  611.8 60.3 %collective-permute-start.44 = (bf16[2,64,2560]{2,1,0:T(8,128)(2,1)}, bf16[2,64,2560]{2,1,0:T(8,128)(2,1)}, u32[]{:S(2)}, u32[]{:S(2)}) collective-permute-start(bf16[2,64,2560]{2,1,0:T(8,128)(2,1)} %dynamic-slice_bitcast_fusion), channel_id=1, source_target_pairs={{0,8},{8,0},{16,24},{24,16},{1,9},{9,1},{17,25},{25,17},{2,10},{10... | collective-permute-start | bytes 1966088 | tf_op jit(solution)/shard_map/ppermute | solution.py:85
  616.9 72.5 %collective-permute-start.19 = (bf16[1024,1024]{1,0:T(8,128)(2,1)}, bf16[1024,1024]{1,0:T(8,128)(2,1)}, u32[]{:S(2)}, u32[]{:S(2)}) collective-permute-start(bf16[1024,1024]{1,0:T(8,128)(2,1)} %get-tuple-element.33), channel_id=1, source_target_pairs={{0,0},{2,1},{1,2},{3,3},{4,4},{6,5},{5,6},{7,7},{8,8},{10,9},{9,10... | collective-permute-start | bytes 6291464 | tf_op jit(solution)/shard_map/ppermute | solution.py:67
  654.9 36.9 %collective-permute-start.22 = (bf16[1024,1024]{1,0:T(8,128)(2,1)}, bf16[1024,1024]{1,0:T(8,128)(2,1)}, u32[]{:S(2)}, u32[]{:S(2)}) collective-permute-start(bf16[1024,1024]{1,0:T(8,128)(2,1)} %get-tuple-element.42), channel_id=1, source_target_pairs={{0,0},{2,1},{1,2},{3,3},{4,4},{6,5},{5,6},{7,7},{8,8},{10,9},{9,10... | collective-permute-start | bytes 6291464 | tf_op jit(solution)/shard_map/ppermute | solution.py:67
  (71 other events, 874.7 us)

commit v2 on v1

v2 whole, which is shorter than its diff:
```python
import functools
import math

import jax
import jax.numpy as jnp
from jax import lax
from jax.experimental import pallas as pl
from jax.experimental.pallas import tpu as pltpu
from jax.sharding import Mesh
from jax.sharding import PartitionSpec as P

HEAD_DIM = 64
HEADS = 16
HIGHEST = lax.Precision.HIGHEST
MASKED = -1e30
EPSILON = 1e-06
VMEM_LIMIT = 60 * 1024 * 1024
F32 = jnp.float32
BF16 = jnp.bfloat16

ALL = ("za", "zb", "core", "hh", "hl")
MOVE = ("core", "hh", "hl")
SUB = ("core", "hl")

NT = (((1,), (1,)), ((), ()))
NN = (((1,), (0,)), ((), ()))
TN = (((0,), (0,)), ((), ()))


def dot(a, b, dims=NN, precision=None):
    return lax.dot_general(a, b, dims, precision=precision, preferred_element_type=F32)


def params(**more):
    return pltpu.CompilerParams(vmem_limit_bytes=VMEM_LIMIT, **more)


def cost(flops, bytes_accessed, transcendentals=0):
    return pl.CostEstimate(
        flops=int(flops), bytes_accessed=int(bytes_accessed), transcendentals=int(transcendentals)
    )


def whole(shape, buffers=None):
    zeros = (0,) * len(shape)
    if buffers is None:
        return pl.BlockSpec(shape, lambda *_: zeros)
    return pl.BlockSpec(shape, lambda *_: zeros, pipeline_mode=pl.Buffered(buffers))


def moved(value):
    stays = lax.axis_index("core") == lax.axis_index("hh")
    return jnp.where(stays, value, lax.ppermute(value, ("core", "hh"), [(1, 2), (2, 1)]))


def from_sub(value, step):
    size = lax.axis_size("hl") * 2
    return lax.ppermute(value, SUB, [((d + step) % size, d) for d in range(size)])


def to_sub(value, step):
    size = lax.axis_size("hl") * 2
    return lax.ppermute(value, SUB, [(d, (d + step) % size) for d in range(size)])


SWAP = [(0, 1), (1, 0)]


def across(value, bit):
    size = lax.axis_size("za")
    return lax.ppermute(value, "za", [(i, i ^ bit) for i in range(size)])


def place_kernel(half, where, own, by_zb, by_hh, both_low, both_high, out):
    zb = where[0]
    hh = where[1]
    out[0, zb, hh] = own[0]
    out[0, 1 - zb, hh] = by_zb[0]
    out[0, zb, 1 - hh] = by_hh[0]

    @pl.when(pl.program_id(0) < half)
    def _():
        out[0, 1 - zb, 1 - hh] = both_low[0]

    @pl.when(pl.program_id(0) >= half)
    def _():
        out[0, 1 - zb, 1 - hh] = both_high[0]


def gather_line(shard):
    return jnp.stack([shard] + [across(shard, bits) for bits in range(1, lax.axis_size("za"))])


def gather_near(held):
    return held, lax.ppermute(held, "zb", SWAP), lax.ppermute(held, "hh", SWAP)


def gather_far(held, by_zb, by_hh):
    half = held.shape[0] // 2
    both_low = lax.ppermute(by_zb[:half], "hh", SWAP)
    both_high = lax.ppermute(by_hh[half:], "zb", SWAP)
    return held, by_zb, by_hh, both_low, both_high


def gathered(held, by_zb, by_hh, both_low, both_high):
    size, rows, columns = held.shape
    half = size // 2
    where = [lax.axis_index("zb"), lax.axis_index("hh")]
    where += [lax.axis_index("za") ^ bits for bits in range(size)]
    where = jnp.stack(where).astype(jnp.int32)
    block = (1, rows, columns)
    full = pl.pallas_call(
        functools.partial(place_kernel, half),
        grid_spec=pltpu.PrefetchScalarGridSpec(
            num_scalar_prefetch=1,
            grid=(size,),
            in_specs=[pl.BlockSpec(block, lambda i, w: (i, 0, 0))] * 3
            + [
                pl.BlockSpec(block, lambda i, w: (jnp.minimum(i, half - 1), 0, 0)),
                pl.BlockSpec(block, lambda i, w: (jnp.maximum(i - half, 0), 0, 0)),
            ],
            out_specs=pl.BlockSpec((1, 2, 2, rows, columns), lambda i, w: (w[2 + i], 0, 0, 0, 0)),
        ),
        out_shape=jax.ShapeDtypeStruct((size, 2, 2, rows, columns), held.dtype),
        compiler_params=params(),
        cost_estimate=cost(0, size * 4 * rows * columns * 4),
        name="place",
    )(where, held, by_zb, by_hh, both_low, both_high)
    return full.reshape(size * 4 * rows, columns)


FOUR = ((0, 0), (1, 0), (0, 1), (1, 1))


def cut_kernel(counts, where, *refs):
    outs = refs[-4:]
    zb, hh = where[0], where[1]
    first = start = 0
    for count in counts:
        terms = refs[first : first + count]
        columns = terms[0].shape[-1]
        for out, (dz, dh) in zip(outs, FOUR):
            z, h = lax.rem(zb + dz, 2), lax.rem(hh + dh, 2)
            part = terms[0][0, z, h]
            if count > 1:
                part = sum(term[0, z, h].astype(F32) for term in terms).astype(BF16)
            out[0, :, start : start + columns] = part
        first += count
        start += columns


def cut_plane(weights):
    size = lax.axis_size("za")
    where = jnp.stack([lax.axis_index("zb"), lax.axis_index("hh")]).astype(jnp.int32)
    terms = [term for group in weights for term in group]
    rows = terms[0].shape[0] // (size * 4)
    total = sum(group[0].shape[1] for group in weights)
    return pl.pallas_call(
        functools.partial(cut_kernel, [len(group) for group in weights]),
        grid_spec=pltpu.PrefetchScalarGridSpec(
            num_scalar_prefetch=1,
            grid=(size,),
            in_specs=[
                pl.BlockSpec((1, 2, 2, rows, term.shape[1]), lambda i, w: (i, 0, 0, 0, 0))
                for term in terms
            ],
            out_specs=[pl.BlockSpec((1, rows, total), lambda i, w: (i, 0, 0))] * 4,
        ),
        out_shape=[jax.ShapeDtypeStruct((size, rows, total), BF16)] * 4,
        compiler_params=params(),
        cost_estimate=cost(0, sum(2 * term.size for term in terms) + size * 8 * rows * total),
        name="cut",
    )(where, *[term.reshape(size, 2, 2, rows, -1) for term in terms])


def swap_plane(pieces):
    own, to_zb, to_hh, to_both = pieces
    from_both = lax.ppermute(to_both, ("zb", "hh"), [(0, 3), (1, 2), (2, 1), (3, 0)])
    from_hh = lax.ppermute(to_hh, "hh", SWAP)
    from_zb = lax.ppermute(to_zb, "zb", SWAP)
    return own, from_zb, from_hh, from_both


def cut_line(pieces):
    total = sum(piece.astype(F32) for piece in pieces).astype(BF16)
    mine = lax.axis_index("za")
    return [
        lax.dynamic_index_in_dim(total, mine ^ bits, 0, keepdims=False)
        for bits in range(total.shape[0])
    ]


def swap_line(cuts):
    return [cuts[0]] + [across(cut, bits) for bits, cut in enumerate(cuts) if bits]


def total_of(cuts):
    return sum(cut.astype(F32) for cut in cuts).astype(BF16)


def together(*values):
    return lax.optimization_barrier(values)


def norm(values):
    centred = values - jnp.mean(values, axis=-1, keepdims=True)
    variance = jnp.mean(centred * centred, axis=-1, keepdims=True)
    inverse = lax.rsqrt(variance + EPSILON)
    return centred * inverse, inverse


def pick(member, table):
    high = table.astype(BF16)
    rest = table - high.astype(F32)
    middle = rest.astype(BF16)
    low = (rest - middle.astype(F32)).astype(BF16)
    return dot(member, jnp.concatenate([high, middle, low, jnp.zeros_like(low)], axis=0))


def gather(member_flip, term):
    high = term.astype(BF16)
    low = (term - high.astype(F32)).astype(BF16)
    return (dot(member_flip, high) + dot(member_flip, low))[0:8]


def first_norm_kernel(x, member, adaptive, out):
    width = x.shape[1]
    normed, _ = norm(x[...].astype(F32))
    shift = pick(member[...], adaptive[:, :width])
    scale = pick(member[...], adaptive[:, width : 2 * width])
    out[...] = (normed * (1.0 + scale) + shift).astype(BF16)


def first_norm(x, member, adaptive):
    rows, width = x.shape
    tile = min(256, rows)
    return pl.pallas_call(
        first_norm_kernel,
        grid=(rows // tile,),
        out_shape=jax.ShapeDtypeStruct((rows, width), BF16),
        in_specs=[
            pl.BlockSpec((tile, width), lambda i: (i, 0)),
            pl.BlockSpec((tile, 32), lambda i: (i, 0)),
            whole(adaptive.shape),
        ],
        out_specs=pl.BlockSpec((tile, width), lambda i: (i, 0)),
        compiler_params=params(),
        cost_estimate=cost(rows * width * 40, rows * width * 4),
        name="first_norm",
    )(x, member, adaptive)


def turn(values, cosine, sine):
    lanes = values.shape[1]
    place = lax.broadcasted_iota(jnp.int32, (1, 128), 1) % HEAD_DIM
    first = place < HEAD_DIM // 2
    parts = []
    for at in range(0, lanes, 128):
        part = values[:, at : at + 128]
        ahead = pltpu.roll(part, 128 - HEAD_DIM // 2, 1)
        behind = pltpu.roll(part, HEAD_DIM // 2, 1)
        swapped = jnp.where(first, ahead, behind)
        parts.append(part * cosine + swapped * sine)
    return parts[0] if len(parts) == 1 else jnp.concatenate(parts, axis=1)


def project_kernel(lanes, place, a, w, cosine, sine, out):
    for start in range(0, w.shape[1], 3 * lanes):
        products = dot(a[...], w[:, start : start + 3 * lanes])
        for at in range(0, 3 * lanes, 128):
            product = products[:, at : at + 128]
            kind = at // 128 % 3
            if kind < 2:
                product = turn(product, cosine[...], sine[...])
            if kind == 0:
                product = product * HEAD_DIM**-0.5
            out[:, start + at : start + at + 128] = product.astype(BF16)


def project(place, a, w, cosine, sine, lanes):
    rows, width = a.shape
    columns = w.shape[1]
    tile = min(256, rows)
    tiles = rows // tile
    return pl.pallas_call(
        functools.partial(project_kernel, lanes),
        grid_spec=pltpu.PrefetchScalarGridSpec(
            num_scalar_prefetch=1,
            grid=(tiles,),
            in_specs=[
                pl.BlockSpec((tile, width), lambda i, s: (i, 0)),
                whole(w.shape, 1),
                pl.BlockSpec((tile, 128), lambda i, s: (s[0] * tiles + i, 0)),
                pl.BlockSpec((tile, 128), lambda i, s: (s[0] * tiles + i, 0)),
            ],
            out_specs=pl.BlockSpec((tile, columns), lambda i, s: (i, 0)),
        ),
        out_shape=jax.ShapeDtypeStruct((rows, columns), BF16),
        compiler_params=params(),
        cost_estimate=cost(2 * rows * width * columns, rows * (width + columns) * 2),
        name="project",
    )(place, a, w, cosine, sine)


def lane_mask(lanes, head):
    return lax.broadcasted_iota(jnp.int32, (1, lanes), 1) // HEAD_DIM == head


def piece_start(place, piece, pieces, rows):
    return pl.multiple_of(lax.rem(place[0] + piece, pieces) * rows, rows)


def flip(values):
    return jnp.transpose(values.astype(F32))


def spread(ref, span, arrays):
    for at in range(0, ref.shape[1], 128):
        start = at // 384 * 128
        arrays[at // 128 % 3][span, start : start + 128] = ref[:, at : at + 128]


def each_width(count, limit, run):
    for width in range(1, limit + 1):

        @pl.when(count == width)
        def _(width=width):
            run(width)


def attend_kernel(pieces, heads, step, place, bounds, seg_col, seg_row, *refs):
    inputs = refs[:pieces]
    outs = refs[pieces : 2 * pieces]
    lse, q_all, k_all, v_all, o_all, bias = refs[2 * pieces :]
    rows = inputs[0].shape[0]
    for piece in range(pieces):
        span = pl.ds(piece_start(place, piece, pieces, rows), rows)
        spread(inputs[piece], span, (q_all, k_all, v_all))
    frames, lanes = q_all.shape
    lane = lax.broadcasted_iota(jnp.int32, (1, 128), 1)

    def one_block(i, _):
        block = pl.ds(pl.multiple_of(i * step, step), step)
        low = pl.multiple_of(bounds[0, i], 128)

        def run(width):
            width = width * step
            span = pl.ds(low, width)
            same = seg_col[block, :] == seg_row[0:1, span]
            bias[:, 0:width] = jnp.where(same, 0.0, MASKED)
            query, key, value = q_all[block, :], k_all[span, :], v_all[span, :]
            result = jnp.zeros((step, lanes), F32)
            stats = jnp.zeros((step, 128), F32)
            for head in range(heads):
                keep = lane_mask(lanes, head)
                masked = jnp.where(keep, query, jnp.zeros_like(query))
                scores = dot(masked, key, NT) + bias[:, 0:width]
                highest = jnp.max(scores, axis=1, keepdims=True)
                weight = jnp.exp(scores - highest)
                total = jnp.sum(weight, axis=1, keepdims=True)
                part = dot(weight.astype(BF16), value)
                result = jnp.where(keep, part / total, result)
                stats = jnp.where(lane == head, highest + jnp.log(total), stats)
            o_all[block, :] = result.astype(BF16)
            lse[0, block, :] = stats

        each_width(bounds[1, i], frames // step, run)
        return 0

    lax.fori_loop(0, frames // step, one_block, 0)
    for piece in range(pieces):
        outs[piece][...] = o_all[pl.ds(piece_start(place, piece, pieces, rows), rows), :]


def attend(place, bounds, seg_col, seg_row, qkv, lanes, step):
    pieces = len(qkv)
    rows, columns = qkv[0].shape
    groups = columns // (3 * lanes)
    heads = lanes // HEAD_DIM
    frames = rows * pieces
    specs = [pl.BlockSpec((rows, 3 * lanes), lambda g: (0, g))] * pieces
    smem = pl.BlockSpec(memory_space=pltpu.SMEM)
    area = frames * frames // 2 * heads * groups
    results = pl.pallas_call(
        functools.partial(attend_kernel, pieces, heads, step),
        grid=(groups,),
        out_shape=[jax.ShapeDtypeStruct((rows, groups * lanes), BF16)] * pieces
        + [jax.ShapeDtypeStruct((groups, frames, 128), F32)],
        in_specs=[smem, smem, whole(seg_col.shape), whole(seg_row.shape)] + specs,
        out_specs=[pl.BlockSpec((rows, lanes), lambda g: (0, g))] * pieces
        + [pl.BlockSpec((1, frames, 128), lambda g: (g, 0, 0))],
        scratch_shapes=[pltpu.VMEM((frames, lanes), BF16)] * 4 + [pltpu.VMEM((step, frames), F32)],
        compiler_params=params(),
        cost_estimate=cost(area * 4 * 256, frames * columns * 4, area),
        name="attend",
    )(place, bounds, seg_col, seg_row, *qkv)
    return results[:pieces], results[pieces]


def attend_back_kernel(pieces, first, heads, step, place, bounds, seg_col, seg_row, *refs):
    inputs = refs[: 3 * pieces]
    lse, cosine, sine = refs[3 * pieces : 3 * pieces + 3]
    normed = refs[3 * pieces + 3 : 4 * pieces + 3]
    out, grad_w = refs[4 * pieces + 3 : 4 * pieces + 5]
    q_all, k_all, v_all, o_all, do_all, dq_all, dk_all, dv_all, bias, weights, slopes = refs[
        4 * pieces + 5 :
    ]
    rows = inputs[0].shape[0]
    for piece in range(pieces):
        span = pl.ds(piece_start(place, piece, pieces, rows), rows)
        spread(inputs[3 * piece], span, (q_all, k_all, v_all))
        o_all[span, :] = inputs[3 * piece + 1][...]
        do_all[span, :] = inputs[3 * piece + 2][...]
    frames, lanes = q_all.shape
    dk_all[...] = jnp.zeros_like(dk_all)
    dv_all[...] = jnp.zeros_like(dv_all)

    def one_block(i, _):
        block = pl.ds(pl.multiple_of(i * step, step), step)
        low = pl.multiple_of(bounds[0, i], 128)

        def run(width):
            width = width * step
            span = pl.ds(low, width)
            same = seg_col[block, :] == seg_row[0:1, span]
            bias[:, 0:width] = jnp.where(same, 0.0, MASKED)
            query, key, value = q_all[block, :], k_all[span, :], v_all[span, :]
            grad = do_all[block, :]
            product = grad.astype(F32) * o_all[block, :].astype(F32)
            result = jnp.zeros((step, lanes), F32)
            queries, grads = [], []
            for head in range(heads):
                keep = lane_mask(lanes, head)
                queries.append(jnp.where(keep, query, jnp.zeros_like(query)))
                grads.append(jnp.where(keep, grad, jnp.zeros_like(grad)))
                centre = jnp.sum(jnp.where(keep, product, 0.0), axis=1, keepdims=True)
                scores = dot(queries[head], key, NT) + bias[:, 0:width]
                weight = jnp.exp(scores - lse[0, block, first + head : first + head + 1])
                slope = dot(grads[head], value, NT) - centre
                slope = (weight * slope).astype(BF16)
                at = pl.ds(head * step, step)
                weights[at, 0:width] = weight.astype(BF16)
                slopes[at, 0:width] = slope
                result = jnp.where(keep, dot(slope, key), result)
            dq_all[block, :] = result * HEAD_DIM**-0.5
            dv_all[span, :] += dot(weights[:, 0:width], jnp.concatenate(grads, axis=0), TN)
            dk_all[span, :] += dot(slopes[:, 0:width], jnp.concatenate(queries, axis=0), TN)

        each_width(bounds[1, i], frames // step, run)
        return 0

    lax.fori_loop(0, frames // step, one_block, 0)
    for piece in range(pieces):
        span = pl.ds(piece_start(place, piece, pieces, rows), rows)
        cos = cosine[span, :]
        sin = -sine[span, :]
        out[piece, :, 0:lanes] = turn(dq_all[span, :], cos, sin).astype(BF16)
        out[piece, :, lanes : 2 * lanes] = turn(dk_all[span, :], cos, sin).astype(BF16)
        out[piece, :, 2 * lanes : 3 * lanes] = dv_all[span, :].astype(BF16)
    grad_w[...] = sum(dot(normed[p][...], out[p], TN) for p in range(pieces)).astype(BF16)


def attend_back(
    place, bounds, seg_col, seg_row, qkv, attended, grads, lse, cosine, sine, normed, pair, step
):
    pieces = len(qkv)
    rows = qkv[0].shape[0]
    lanes, heads = 128, 128 // HEAD_DIM
    width = normed[0].shape[1]
    per_group = attended[0].shape[1] // lanes // lse.shape[0]
    frames = rows * pieces
    specs, arrays = [], []
    for piece in range(pieces):
        specs.append(pl.BlockSpec((rows, 3 * lanes), lambda i: (0, pair)))
        specs += [pl.BlockSpec((rows, lanes), lambda i: (0, pair))] * 2
        arrays += [qkv[piece], attended[piece], grads[piece]]
    smem = pl.BlockSpec(memory_space=pltpu.SMEM)
    area = frames * frames // 2 * heads
    return pl.pallas_call(
        functools.partial(attend_back_kernel, pieces, pair % per_group * heads, heads, step),
        grid=(1,),
        out_shape=[
            jax.ShapeDtypeStruct((pieces, rows, 3 * lanes), BF16),
            jax.ShapeDtypeStruct((width, 3 * lanes), BF16),
        ],
        in_specs=[smem, smem, whole(seg_col.shape, 1), whole(seg_row.shape, 1)]
        + specs
        + [
            pl.BlockSpec(
                (1, frames, 128), lambda i: (pair // per_group, 0, 0), pipeline_mode=pl.Buffered(1)
            ),
            whole(cosine.shape, 1),
            whole(sine.shape, 1),
        ]
        + [whole(normed[0].shape, 1)] * pieces,
        out_specs=[whole((pieces, rows, 3 * lanes), 1), whole((width, 3 * lanes), 1)],
        scratch_shapes=[pltpu.VMEM((frames, lanes), BF16)] * 5
        + [pltpu.VMEM((frames, lanes), F32)] * 3
        + [pltpu.VMEM((step, frames), F32)]
        + [pltpu.VMEM((heads * step, frames), BF16)] * 2,
        compiler_params=params(),
        cost_estimate=cost(area * 10 * 256, frames * lanes * 16, area),
        name="attend_back",
    )(place, bounds, seg_col, seg_row, *arrays, lse, cosine, sine, *normed)


def gelu_pair(h):
    root = math.sqrt(2.0 / math.pi)
    square = h * h
    bend = jnp.tanh(root * h * (1.0 + 0.044715 * square))
    half = 0.5 * (1.0 + bend)
    slope = half + 0.5 * h * (1.0 - bend * bend) * (root * (1.0 + 0.134145 * square))
    return h * half, slope


def flat(ref, span=slice(None)):
    value = ref[:, 0, :, span]
    return value.reshape(value.shape[0] * value.shape[1], value.shape[2])


def middle_kernel(pieces, place, *refs):
    x, member, member_flip, adaptive, dy = refs[:5]
    refs = refs[5:]
    attended, refs = refs[:pieces], refs[pieces:]
    w_out, refs = refs[:pieces], refs[pieces:]
    w_up, refs = refs[:pieces], refs[pieces:]
    w_down, refs = refs[:pieces], refs[pieces:]
    mixed, dx2, a2_out, d2_out, d1_out, dadaptive = refs[:6]
    refs = refs[6:]
    active, refs = refs[:pieces], refs[pieces:]
    dhidden, refs = refs[:pieces], refs[pieces:]
    dattended = refs[:pieces]
    width = x.shape[1]
    here = member[...]
    gate1, shift2, scale2, gate2 = (
        pick(here, adaptive[:, n * width : (n + 1) * width]) for n in (2, 3, 4, 5)
    )
    branch1 = sum(dot(attended[p][...], flat(w_out[p]), NT) for p in range(pieces))
    x2 = x[...].astype(F32) + gate1 * branch1
    n2, r2 = norm(x2)
    a2 = (n2 * (1.0 + scale2) + shift2).astype(BF16)
    a2_out[...] = a2
    branch2 = jnp.zeros_like(x2)
    slopes = []
    for p in range(pieces):
        value, slope = gelu_pair(dot(a2, flat(w_up[p])))
        value = value.astype(BF16)
        active[p][...] = value
        slopes.append(slope)
        branch2 = branch2 + dot(value, flat(w_down[p]), NT)
    mixed[...] = (x2 + gate2 * branch2).astype(BF16)
    upstream = dy[...].astype(F32)
    d2 = (upstream * gate2).astype(BF16)
    d2_out[...] = d2
    da2 = jnp.zeros_like(x2)
    for p in range(pieces):
        dh = (dot(d2, flat(w_down[p])) * slopes[p]).astype(BF16)
        dhidden[p][...] = dh
        da2 = da2 + dot(dh, flat(w_up[p]), NT)
    u2 = da2 * (1.0 + scale2)
    back = upstream + r2 * (
        u2 - jnp.mean(u2, axis=-1, keepdims=True) - n2 * jnp.mean(u2 * n2, axis=-1, keepdims=True)
    )
    dx2[...] = back
    d1 = (back * gate1).astype(BF16)
    d1_out[...] = d1
    for p in range(pieces):
        dattended[p][...] = dot(d1, flat(w_out[p])).astype(BF16)

    @pl.when(pl.program_id(0) == 0)
    def _():
        dadaptive[...] = jnp.zeros_like(dadaptive)

    for n, term in enumerate((back * branch1, da2, da2 * n2, upstream * branch2)):
        dadaptive[:, n * width : (n + 1) * width] += gather(member_flip[...], term)


def middle(place, x, member, member_flip, adaptive, dy, attended, weights):
    pieces = len(attended)
    rows, width = x.shape
    head_columns = attended[0].shape[1]
    hidden = 2 * head_columns
    tile = min(256, rows)

    def tiled(columns):
        return pl.BlockSpec((tile, columns), lambda i, s: (i, 0))

    def shaped(columns, kind):
        return jax.ShapeDtypeStruct((rows, columns), kind)

    shards, slices, own_rows, _ = weights.shape

    def resident(columns, at):
        return [
            pl.BlockSpec(
                (shards, 1, own_rows, columns),
                lambda i, s, piece=piece: (0, lax.rem(s[0] + piece, slices), 0, at),
                pipeline_mode=pl.Buffered(1),
            )
            for piece in range(pieces)
        ]

    cuts = resident(head_columns, 4) + resident(hidden, 0) + resident(hidden, 1)
    work = 2 * rows * width * pieces * (3 * hidden * 2 + head_columns * 2)
    results = pl.pallas_call(
        functools.partial(middle_kernel, pieces),
        grid_spec=pltpu.PrefetchScalarGridSpec(
        num_scalar_prefetch=1,
        grid=(rows // tile,),
        in_specs=[
            tiled(width),
            tiled(32),
            pl.BlockSpec((16, tile), lambda i, s: (0, i)),
            whole(adaptive.shape, 1),
            tiled(width),
        ]
        + [tiled(head_columns)] * pieces
        + cuts,
        out_specs=[tiled(width)] * 5
        + [whole((8, 4 * width))]
        + [tiled(hidden)] * (2 * pieces)
        + [tiled(head_columns)] * pieces,
        ),
        out_shape=[
            shaped(width, BF16),
            shaped(width, F32),
            shaped(width, BF16),
            shaped(width, BF16),
            shaped(width, BF16),
            jax.ShapeDtypeStruct((8, 4 * width), F32),
        ]
        + [shaped(hidden, BF16)] * (2 * pieces)
        + [shaped(head_columns, BF16)] * pieces,
        compiler_params=params(),
        cost_estimate=cost(work, rows * width * 30, rows * hidden * pieces),
        name="middle",
    )(place, x, member, member_flip, adaptive, dy, *attended, *[weights] * (3 * pieces))
    head, rest = results[:6], results[6:]
    return head, rest[:pieces], rest[pieces : 2 * pieces], rest[2 * pieces :]


def part_kernel(groups, *refs):
    slopes, weights, out = refs[:groups], refs[groups], refs[-1]
    slope = jnp.concatenate([slope[...] for slope in slopes], axis=1)
    out[...] = dot(slope, weights[...], NT).astype(BF16)


def input_part(slopes, weights, piece):
    rows, columns = slopes[0].shape[1:]
    width = weights.shape[0]
    tile = min(256, rows)
    groups = len(slopes)
    return pl.pallas_call(
        functools.partial(part_kernel, groups),
        grid=(rows // tile,),
        in_specs=[pl.BlockSpec((None, tile, columns), lambda i: (piece, i, 0))] * groups
        + [whole(weights.shape, 1)],
        out_shape=jax.ShapeDtypeStruct((rows, width), BF16),
        out_specs=pl.BlockSpec((tile, width), lambda i: (i, 0)),
        compiler_params=params(),
        cost_estimate=cost(2 * rows * width * columns * groups, rows * width * 8),
        name="input_part",
    )(*slopes, weights)


def last_kernel(groups, arrivals, *refs):
    x, member, member_flip, adaptive, dx2 = refs[:5]
    refs = refs[5:]
    arrived, refs = refs[:arrivals], refs[arrivals:]
    slopes, refs = refs[:groups], refs[groups:]
    weights, grad, dadaptive = refs
    width = x.shape[1]
    normed, inverse = norm(x[...].astype(F32))
    scale = pick(member[...], adaptive[:, width : 2 * width])
    slope = jnp.concatenate([slope[...] for slope in slopes], axis=1)
    da1 = dot(slope, weights[...], NT)
    for piece in arrived:
        da1 = da1 + piece[...].astype(F32)
    u1 = da1 * (1.0 + scale)
    back = inverse * (
        u1
        - jnp.mean(u1, axis=-1, keepdims=True)
        - normed * jnp.mean(u1 * normed, axis=-1, keepdims=True)
    )
    grad[...] = (dx2[...] + back).astype(BF16)

    @pl.when(pl.program_id(0) == 0)
    def _():
        dadaptive[...] = jnp.zeros_like(dadaptive)

    dadaptive[:, :width] += gather(member_flip[...], da1)
    dadaptive[:, width:] += gather(member_flip[...], da1 * normed)


def last(x, member, member_flip, adaptive, dx2, arrived, slopes, weights):
    rows, width = x.shape
    tile = min(256, rows)

    def tiled(columns):
        return pl.BlockSpec((tile, columns), lambda i: (i, 0))

    return pl.pallas_call(
        functools.partial(last_kernel, len(slopes), len(arrived)),
        grid=(rows // tile,),
        in_specs=[
            tiled(width),
            tiled(32),
            pl.BlockSpec((16, tile), lambda i: (0, i)),
            whole(adaptive.shape, 1),
            tiled(width),
        ]
        + [tiled(width)] * len(arrived)
        + [pl.BlockSpec((None, tile, s.shape[2]), lambda i: (0, i, 0)) for s in slopes]
        + [whole(weights.shape, 1)],
        out_shape=[
            jax.ShapeDtypeStruct((rows, width), BF16),
            jax.ShapeDtypeStruct((8, 2 * width), F32),
        ],
        out_specs=[tiled(width), whole((8, 2 * width))],
        compiler_params=params(),
        cost_estimate=cost(2 * rows * width * sum(s.shape[2] for s in slopes), rows * width * 12),
        name="last",
    )(x, member, member_flip, adaptive, dx2, *arrived, *slopes, weights)


def time_vector(steps, width):
    halfway = width // 2
    rates = jnp.exp(jnp.arange(halfway, dtype=F32) * (-math.log(10000.0) / (halfway - 1)))
    angles = steps.astype(F32)[:, None] * rates[None, :]
    return jnp.concatenate([jnp.sin(angles), jnp.cos(angles)], axis=1)


def body(frames, clip_lengths, timesteps, w_qkv, w_out, w_up, w_down, w_ada, b_ada, grad_out):
    rows, width = frames.shape
    clips = clip_lengths.shape[0]
    pieces = lax.axis_size("hl") * 2
    group_rows = rows * pieces
    own_rows = w_qkv.shape[1]
    head_columns = width // pieces
    lanes = min(256, head_columns)
    pairs = head_columns // 128
    step = min(256, group_rows)
    place = lax.axis_index(SUB).astype(jnp.int32)

    qkv_shard = w_qkv.astype(BF16).reshape(3, own_rows, pairs, 128)
    qkv_shard = jnp.transpose(qkv_shard, (1, 2, 0, 3)).reshape(own_rows, 3 * head_columns)
    mlp_shard = jnp.concatenate(
        [w_up.astype(BF16), w_down.astype(BF16).T, w_out.astype(BF16).T], axis=1
    )
    qkv_shard = moved(qkv_shard)
    lengths = moved(clip_lengths)

    def around(value):
        return [value] + [from_sub(value, step) for step in range(1, pieces)]

    condition = jax.nn.silu(time_vector(timesteps, width))
    columns = w_ada.shape[1]
    devices = [lax.axis_size(axis) for axis in ALL]
    za, zb, cores, hh, hl = devices
    table = (
        jnp.dot(condition, lax.reduce_precision(w_ada, 8, 7), precision=HIGHEST)
        + lax.reduce_precision(b_ada, 8, 7)[None, :]
    )
    table, qkv_shard, lengths = together(table, qkv_shard, lengths)
    table = table.reshape(za, zb, 1, hh, 1, clips, columns)
    table = jnp.broadcast_to(table, (za, zb, cores, hh, hl, clips, columns))
    table = lax.all_to_all(table.reshape(-1, clips, columns), ALL, 0, 0, tiled=True)
    adaptive = jnp.transpose(table, (1, 0, 2)).reshape(clips, -1)
    adaptive = jnp.pad(adaptive, ((0, 8 - clips), (0, 0)))

    ends = jnp.cumsum(lengths, dtype=jnp.int32)
    starts = ends - lengths
    index = jnp.arange(group_rows, dtype=jnp.int32)
    segment = jnp.sum((index[:, None] >= ends[None, :]).astype(jnp.int32), axis=1, dtype=jnp.int32)
    edges = jnp.concatenate([jnp.zeros((1,), jnp.int32), ends])
    begins = jnp.max(jnp.where(index[:, None] >= edges[None, :], edges[None, :], 0), axis=1)
    position = (index - begins).astype(F32)
    lane = jnp.arange(128, dtype=jnp.int32) % HEAD_DIM
    rates = jnp.exp((lane % (HEAD_DIM // 2)).astype(F32) * (-2.0 * math.log(10000.0) / HEAD_DIM))
    angles = position[:, None] * rates[None, :]
    cosine = jnp.cos(angles)
    sine = jnp.sin(angles) * jnp.where(lane < HEAD_DIM // 2, -1.0, 1.0)[None, :]
    seg_col = segment[:, None]
    seg_row = segment[None, :]
    block_first = jnp.arange(0, group_rows, step, dtype=jnp.int32)
    first_seg = jnp.sum((block_first[:, None] >= ends[None, :]).astype(jnp.int32), axis=1)
    last_seg = jnp.sum((block_first[:, None] + (step - 1) >= ends[None, :]).astype(jnp.int32), axis=1)
    closing = jnp.concatenate([ends, jnp.full((1,), group_rows, jnp.int32)])
    low_at = jnp.sum(jnp.where(first_seg[:, None] == jnp.arange(clips + 1)[None, :], edges[None, :], 0), axis=1)
    high_at = jnp.sum(jnp.where(last_seg[:, None] == jnp.arange(clips + 1)[None, :], closing[None, :], 0), axis=1)
    low_at = low_at // 128 * 128
    widths = (high_at - low_at + step - 1) // step
    low_at = jnp.minimum(low_at, group_rows - widths * step)
    bounds = jnp.stack([low_at, widths]).astype(jnp.int32)
    own_index = place * rows + jnp.arange(rows, dtype=jnp.int32)
    member = ((own_index[:, None] >= starts[None, :]) & (own_index[:, None] < ends[None, :])).astype(F32)
    member = jnp.pad(member, ((0, 0), (0, 8 - clips))).astype(BF16)
    member_flip = jnp.pad(member.T, ((0, 8), (0, 0)))
    member = jnp.concatenate([member, member, member, jnp.zeros_like(member)], axis=1)

    x = moved(frames)
    held = gather_line(qkv_shard)
    held, adaptive, x, cosine, sine, member = together(held, adaptive, x, cosine, sine, member)
    near = gather_near(held)
    a1_all = around(first_norm(x, member, adaptive))
    near, a1_all, mlp_shard, grad_out = together(near, a1_all, mlp_shard, grad_out)
    mlp_full = lax.all_gather(mlp_shard, ALL, axis=0, tiled=True)
    mlp_full = mlp_full.reshape(-1, pieces, own_rows, mlp_shard.shape[1])
    qkv_full = gathered(*gather_far(*near))
    places = [((place + piece) % pieces).reshape(1) for piece in range(pieces)]
    qkv = [
        project(places[piece], a1_all[piece], qkv_full, cosine, sine, lanes)
        for piece in range(pieces)
    ]
    at_place = place.reshape(1)
    qkv, grad_out = together(qkv, grad_out)
    dy = moved(grad_out)
    attended, lse = attend(at_place, bounds, seg_col, seg_row, qkv, lanes, step)
    attended, lse, dy = together(attended, lse, dy)
    attended_own = [attended[0]] + [
        from_sub_piece(attended, step_) for step_ in range(1, pieces)
    ]

    head, active, dhidden, dattended = middle(
        at_place, x, member, member_flip, adaptive, dy, attended_own, mlp_full
    )
    mixed, dx2, a2, d2, d1, dada_late = head
    grads_attended = [dattended[0]] + [
        from_sub_piece(dattended, step_) for step_ in range(1, pieces)
    ]
    mixed_back = moved(mixed)

    def summed(left, right):
        parts = [dot(left, part, TN).astype(BF16) for part in right]
        return [parts[0]] + [to_sub(parts[step], step) for step in range(1, pieces)]

    late = [summed(a2, dhidden), summed(d2, active), summed(d1, attended_own)]

    def back(pair, qkv):
        return attend_back(
            at_place, bounds, seg_col, seg_row, qkv, attended, grads_attended, lse, cosine, sine,
            a1_all, pair, step,
        )

    slopes, grads_qkv = [], []
    early = final = None

    def next_pair():
        slope, grad = back(len(slopes), qkv)
        slopes.append(slope)
        grads_qkv.append(grad)

    next_pair()
    late, slopes, grads_qkv, mixed_back = together(late, slopes, grads_qkv, mixed_back)
    late, qkv = together(cut_plane(late), qkv)
    late = swap_plane(late)
    while len(slopes) < pairs - 1:
        next_pair()
    if pairs > 1:
        early = cut_plane([[grad] for grad in grads_qkv])
    late, early, slopes, grads_qkv = together(late, early, slopes, grads_qkv)
    late, qkv = together(cut_line(late), qkv)
    late = swap_line(late)
    if pairs > 1:
        early = swap_plane(early)
        next_pair()
    late, early, slopes, grads_qkv = together(late, early, slopes, grads_qkv)
    final = cut_plane([grads_qkv[-1:]])
    if pairs > 1:
        early = cut_line(early)
    final, early, slopes = together(final, early, slopes)
    final = swap_plane(final)
    if pairs > 1:
        early = swap_line(early)
    arrived = [to_sub(input_part(slopes, qkv_full, piece), piece) for piece in range(1, pieces)]
    final, early, arrived = together(final, early, arrived)
    final, dx2 = together(cut_line(final), dx2)
    final = swap_line(final)
    grad_frames, dada_early = last(
        x, member, member_flip, adaptive, dx2, arrived, slopes, qkv_full
    )
    late, early, final, grad_frames, dada_early = together(
        late, early, final, grad_frames, dada_early
    )
    grad_frames = moved(grad_frames).astype(F32)
    sums = [total_of(cuts) for cuts in (late, early, final) if cuts]
    sums = moved(jnp.concatenate(sums, axis=1))
    late, rest = sums[:, : mlp_shard.shape[1]], sums[:, mlp_shard.shape[1] :]
    hidden_columns = w_up.shape[1]
    grad_up = late[:, :hidden_columns]
    grad_down = late[:, hidden_columns : 2 * hidden_columns]
    grad_outw = late[:, 2 * hidden_columns :]
    dadaptive = jnp.concatenate([dada_early, dada_late], axis=1)[:clips]
    dadaptive = jnp.transpose(dadaptive.reshape(clips, -1, columns), (1, 0, 2))
    dadaptive = lax.all_to_all(dadaptive, ALL, 0, 0, tiled=True)
    dadaptive = dadaptive.reshape(za, zb, cores, hh, hl, clips, columns)
    dadaptive = jnp.sum(dadaptive, axis=(2, 4)).reshape(-1, columns)
    grad_ada = dot(condition, dadaptive, TN, HIGHEST)
    grad_bias = jnp.sum(dadaptive, axis=0)

    grad_qkv = rest.reshape(own_rows, pairs, 3, 128)
    grad_qkv = jnp.transpose(grad_qkv, (2, 0, 1, 3)).reshape(w_qkv.shape).astype(F32)
    return (
        mixed_back,
        grad_frames,
        grad_qkv,
        grad_outw.astype(F32).T,
        grad_up.astype(F32),
        grad_down.astype(F32).T,
        grad_ada,
        grad_bias,
    )


def from_sub_piece(parts, step):
    pieces = len(parts)
    return from_sub(parts[pieces - step], step)


def solution(mesh):
    clip, head = mesh.shape["clip"], mesh.shape["head"]
    fine = Mesh(mesh.devices.reshape(clip // 4, 2, 2, 2, head // 2), ALL)
    by_clip = ("za", "zb", "core")
    by_head = ("hh", "hl")
    everywhere = by_clip + by_head
    placed = (
        P(everywhere, None),
        P(by_clip),
        P(),
        P(None, by_clip, by_head),
        P(by_head, by_clip),
        P(by_clip, by_head),
        P(by_head, by_clip),
        P(None, everywhere),
        P(everywhere),
        P(everywhere, None),
    )
    return jax.shard_map(
        body,
        mesh=fine,
        in_specs=placed,
        out_specs=(
            P(everywhere, None),
            P(everywhere, None),
            P(None, by_clip, by_head),
            P(by_head, by_clip),
            P(by_clip, by_head),
            P(by_head, by_clip),
            P(None, everywhere),
            P(everywhere),
        ),
        check_vma=False,
    )
```

time: 713 us -> 486 us (0.68)
  the two profiles are of different devices: /device:TPU:0 before, /device:TPU:1 now
where the time goes in v2:
time: 486 us; the launch traced here: 478 us
  Pallas kernels  231 us (48%)
  starting transfers between devices  82.1 us (17%)
  waiting for transfers between devices  74.1 us (15%)
  other arithmetic  37.2 us (8%)
  matrix products  24.6 us (5%)
  between operations  15.1 us (3%)
  local copies, waits for them, and re-layouts  14.4 us (3%)
    pallas_call x4, Pallas kernels, attend_back(): pl.pallas_call(functools.partial(attend_back_kernel, pieces, pair % per_g...  94.2 us
    pallas_call x1, Pallas kernels, middle(): pl.pallas_call(functools.partial(middle_kernel, pieces), grid_spec=pltpu....  38.9 us
    pallas_call x1, Pallas kernels, attend(): pl.pallas_call(functools.partial(attend_kernel, pieces, heads, step), gri...  35.9 us
    ppermute x7, starting transfers between devices, moved(): lax.ppermute(value, ('core', 'hh'), [(1, 2), (2, 1)])  25.6 us
    ppermute x12, starting transfers between devices, across(): return lax.ppermute(value, 'za', [(i, i ^ bit) for i in range(size)])  24.1 us
    dot_general x7, matrix products, dot(): lax.dot_general(a, b, dims, precision=precision, preferred_element_type=F32)  23.7 us
    ppermute x1, waiting for transfers between devices, gather_near(): lax.ppermute(held, 'hh', SWAP)  16.6 us
    pallas_call x3, Pallas kernels, cut_plane(): pl.pallas_call(functools.partial(cut_kernel, [len(group) for group in wei...  16.1 us
  transfers between devices with their start and end apart: 42, of which 12 were waited for; matrix products, arithmetic and copies ran while one was open for 10% of the time, Pallas kernels for 35%

profile of v2, /device:TPU:1, one launch (start us, length us, event | category | flops | bytes accessed | tf_op | source)
XLA Modules:
  0.0 478.2 jit_solution(8666333089422065086)
XLA Ops:
  26.3 5.2 %all-to-all-start = ((f32[32,4,192]{2,1,0:T(4,128)}), f32[32,4,192]{2,1,0:T(4,128)S(1)}, u32[]{:S(2)}, u32[]{:S(2)}) async-start(f32[32,4,192]{2,1,0:T(4,128)} %bitcast.6), calls=%async_computation | async-start | bytes 262144 | tf_op jit(solution)/shard_map/all_to_all | solution.py:767
  32.6 5.6 %fusion = (f32[2048,128]{1,0:T(8,128)}, f32[2048,128]{1,0:T(8,128)}) fusion(f32[128]{0:T(128)S(1)} %get-tuple-element.326, f32[128]{0:T(128)S(1)} %get-tuple-element.327, f32[2048]{0:T(1024)S(1)} %subtract_convert_fusion), kind=kLoop, calls=%fused_computation.15 | loop fusion | flops 524288 | bytes 2106368 | tf_op jit(solution)/shard_map/mul | solution.py:782
  38.3 6.7 %all-to-all-done = f32[32,4,192]{2,1,0:T(4,128)S(1)} async-done(((f32[32,4,192]{2,1,0:T(4,128)}), f32[32,4,192]{2,1,0:T(4,128)S(1)}, u32[]{:S(2)}, u32[]{:S(2)}) %all-to-all-start) | async-done | bytes 98336 | tf_op jit(solution)/shard_map/all_to_all | solution.py:767
  51.2 4.9 %first_norm.1.a.refs_9_ = bf16[1024,1024]{1,0:T(8,128)(2,1)} custom-call(bf16[1024,1024]{1,0:T(8,128)(2,1)} %broadcast_select_fusion.2.x.refs_0_, bf16[1024,32]{1,0:T(8,128)(2,1)} %copy.76.member.refs_1_, f32[8,6144]{1,0:T(8,128)} %pad.15.adaptive.refs_3_), custom_call_target="tpu_custom_call" | custom-call | flops 41943040 | bytes 4194304 | tf_op jit(solution)/shard_map/first_norm/pallas_call | solution.py:237
  59.3 16.6 %collective-permute-done.7.by_hh = bf16[4,64,1536]{2,1,0:T(8,128)(2,1)S(1)} collective-permute-done((bf16[4,64,1536]{2,1,0:T(8,128)(2,1)S(1)}, bf16[4,64,1536]{2,1,0:T(8,128)(2,1)S(1)}, u32[]{:S(2)}, u32[]{:S(2)}) %collective-permute-start.7) | collective-permute-done | bytes 786464 | tf_op jit(solution)/shard_map/ppermute | solution.py:95
  78.6 8.1 %collective-permute-done.10.both_high = bf16[2,64,1536]{2,1,0:T(8,128)(2,1)S(1)} collective-permute-done((bf16[2,64,1536]{2,1,0:T(8,128)(2,1)S(1)}, bf16[2,64,1536]{2,1,0:T(8,128)(2,1)S(1)}, u32[]{:S(2)}, u32[]{:S(2)}) %collective-permute-start.10) | collective-permute-done | bytes 393248 | tf_op jit(solution)/shard_map/ppermute | solution.py:101
  88.2 5.0 %place.1 = bf16[4,2,2,64,1536]{4,3,2,1,0:T(8,128)(2,1)} custom-call(s32[6]{0:T(128)} %stack.64.where, bf16[4,64,1536]{2,1,0:T(8,128)(2,1)} %copy-done, bf16[4,64,1536]{2,1,0:T(8,128)(2,1)} %copy-done.7, bf16[4,64,1536]{2,1,0:T(8,128)(2,1)} %copy-done.6, bf16[2,64,1536]{2,1,0:T(8,128)(2,1)} %copy-done.12, bf16[2,64,1536]{2,1,0:T(8,128)(2,1)} %copy-done.11), custom_call_target="tpu_custom_call" | custom-call | bytes 6291456 | tf_op jit(solution)/shard_map/place/pallas_call | solution.py:112
  93.2 8.0 %project.3.refs_1_.refs_3_ = bf16[1024,1536]{1,0:T(8,128)(2,1)} custom-call(s32[1]{0:T(128)} %bitcast.25.place, bf16[1024,1024]{1,0:T(8,128)(2,1)} %collective-permute-done.8.a.refs_10_, bf16[1024,1536]{1,0:T(8,128)(2,1)} %bitcast.111, f32[2048,128]{1,0:T(8,128)} %get-tuple-element.164.cosine.refs_7_, f32[2048,128]{1,0:T(8,128)} %get-tuple-element.165.sine.refs_8_), custom_call_target="tpu_custom_call" | custom-call | flops 3221225472 | bytes 5242880 | tf_op jit(solution)/shard_map/project/pallas_call | solution.py:285
  101.2 8.1 %project.2.refs_0_ = bf16[1024,1536]{1,0:T(8,128)(2,1)} custom-call(s32[1]{0:T(128)} %bitcast.15.place, bf16[1024,1024]{1,0:T(8,128)(2,1)} %first_norm.1.a.refs_9_, bf16[1024,1536]{1,0:T(8,128)(2,1)} %bitcast.112, f32[2048,128]{1,0:T(8,128)} %get-tuple-element.164.cosine.refs_7_, f32[2048,128]{1,0:T(8,128)} %get-tuple-element.165.sine.refs_8_), custom_call_target="tpu_custom_call" | custom-call | flops 3221225472 | bytes 5242880 | tf_op jit(solution)/shard_map/project/pallas_call | solution.py:285
  115.9 35.9 %attend.1 = (bf16[1024,512]{1,0:T(8,128)(2,1)}, bf16[1024,512]{1,0:T(8,128)(2,1)}, f32[2,2048,128]{2,1,0:T(8,128)}) custom-call(s32[1]{0:T(128)} %bitcast.place, s32[2,8]{1,0:T(2,128)} %pad_add_fusion.bounds, s32[2048,1]{1,0:T(8,128)} %copy.75.seg_col, s32[1,2048]{1,0:T(1,128)} %bitcast.131, bf16[1024,1536]{1,0:T(8,128)(2,1)} %project.2.refs_0_, ...), custom_call_target="tpu_custom_call" | custom-call | flops 17179869184 | bytes 12582912 | tf_op jit(solution)/shard_map/attend/pallas_call | solution.py:384
  159.2 13.4 %all-gather.2.cloned.1.call-done = bf16[2048,2560]{1,0:T(8,128)(2,1)} async-done(((bf16[64,2560]{1,0:T(8,128)(2,1)}), bf16[2048,2560]{1,0:T(8,128)(2,1)}) %all-gather.2.cloned.1.call-update) | async-done | bytes 10485776 | tf_op jit(solution)/shard_map/all_gather | solution.py:807
  172.6 38.9 %middle.1 = (bf16[1024,1024]{1,0:T(8,128)(2,1)}, f32[1024,1024]{1,0:T(8,128)}, bf16[1024,1024]{1,0:T(8,128)(2,1)}, bf16[1024,1024]{1,0:T(8,128)(2,1)}, bf16[1024...) custom-call(s32[1]{0:T(128)} %bitcast.place, ...), custom_call_target="tpu_custom_call" | custom-call | flops 30064771072 | bytes 31457280 | tf_op jit(solution)/shard_map/middle/pallas_call | solution.py:605
  211.6 6.1 %convolution_convert_fusion.3 = bf16[1024,1024]{1,0:T(8,128)(2,1)} fusion(bf16[1024,1024]{1,0:T(8,128)(2,1)} %get-tuple-element.178, bf16[1024,1024]{1,0:T(8,128)(2,1)} %get-tuple-element.179), kind=kOutput, calls=%fused_computation.8 | convolution fusion | flops 2148532224 | bytes 6291456 | tf_op jit(solution)/shard_map/dot_general | solution.py:31
  236.9 23.0 %attend_back.4 = (bf16[2,1024,384]{2,1,0:T(8,128)(2,1)}, bf16[1024,384]{1,0:T(8,128)(2,1)}) custom-call(s32[1]{0:T(128)} %bitcast.place, s32[2,8]{1,0:T(2,128)} %pad_add_fusion.bounds, s32[2048,1]{1,0:T(8,128)} %copy.75.seg_col, s32[1,2048]{1,0:T(1,128)} %bitcast.132, bf16[1024,1536]{1,0:T(8,128)(2,1)} %project.2.refs_0_, ...), custom_call_target="tpu_custom_call" | custom-call | flops 10737418240 | bytes 4194304 | tf_op jit(solution)/shard_map/attend_back/pallas_call | solution.py:479
  264.0 7.4 %cut.3 = (bf16[4,64,2560]{2,1,0:T(8,128)(2,1)}, bf16[4,64,2560]{2,1,0:T(8,128)(2,1)}, bf16[4,64,2560]{2,1,0:T(8,128)(2,1)}, bf16[4,64,2560]{2,1,0:T(8,128)(2,1)}) custom-call(s32[2]{0:T(128)} %pad_add_fusion.3.where, bf16[4,2,2,64,1024]{4,3,2,1,0:T(8,128)(2,1)} %bitcast.116, bf16[4,2,2,64,1024]{4,3,2,1,0:T(8,128)(2,1)} %bitcast.28.refs_1_, ...), custom_call_target="tpu_custom_call" | custom-call | bytes 15728640 | tf_op jit(solution)/shard_map/cut/pallas_call | solution.py:158
  276.2 22.9 %attend_back.6 = (bf16[2,1024,384]{2,1,0:T(8,128)(2,1)}, bf16[1024,384]{1,0:T(8,128)(2,1)}) custom-call(s32[1]{0:T(128)} %bitcast.place, s32[2,8]{1,0:T(2,128)} %pad_add_fusion.bounds, s32[2048,1]{1,0:T(8,128)} %copy.75.seg_col, s32[1,2048]{1,0:T(1,128)} %bitcast.133, bf16[1024,1536]{1,0:T(8,128)(2,1)} %project.2.refs_0_, ...), custom_call_target="tpu_custom_call" | custom-call | flops 10737418240 | bytes 4194304 | tf_op jit(solution)/shard_map/attend_back/pallas_call | solution.py:479
  299.0 25.5 %attend_back.5 = (bf16[2,1024,384]{2,1,0:T(8,128)(2,1)}, bf16[1024,384]{1,0:T(8,128)(2,1)}) custom-call(s32[1]{0:T(128)} %bitcast.place, s32[2,8]{1,0:T(2,128)} %pad_add_fusion.bounds, s32[2048,1]{1,0:T(8,128)} %copy.75.seg_col, s32[1,2048]{1,0:T(1,128)} %bitcast.134, bf16[1024,1536]{1,0:T(8,128)(2,1)} %project.2.refs_0_, ...), custom_call_target="tpu_custom_call" | custom-call | flops 10737418240 | bytes 4194304 | tf_op jit(solution)/shard_map/attend_back/pallas_call | solution.py:479
  337.9 6.3 %collective-permute-start.22 = (bf16[64,2560]{1,0:T(8,128)(2,1)S(1)}, bf16[64,2560]{1,0:T(8,128)(2,1)}, u32[]{:S(2)}, u32[]{:S(2)}) collective-permute-start(bf16[64,2560]{1,0:T(8,128)(2,1)S(1)} %get-tuple-element.224), channel_id=1, source_target_pairs={{0,16},{8,24},{16,0},{24,8},{1,17},{9,25},{17,1},{25,9},{2,18},{10... | collective-permute-start | bytes 983048 | tf_op jit(solution)/shard_map/ppermute | solution.py:71
  345.4 5.6 %collective-permute-start.26 = (bf16[4,64,1152]{2,1,0:T(8,128)(2,1)}, bf16[4,64,1152]{2,1,0:T(8,128)(2,1)S(1)}, u32[]{:S(2)}, u32[]{:S(2)}) collective-permute-start(bf16[4,64,1152]{2,1,0:T(8,128)(2,1)} %get-tuple-element.229), channel_id=1, source_target_pairs={{0,5},{1,4},{4,1},{5,0},{2,7},{3,6},{6,3},{7,2},{8,13},{9,12},{12,... | collective-permute-start | bytes 1769480 | tf_op jit(solution)/shard_map/ppermute | solution.py:178
  351.0 22.8 %attend_back.7 = (bf16[2,1024,384]{2,1,0:T(8,128)(2,1)}, bf16[1024,384]{1,0:T(8,128)(2,1)}) custom-call(s32[1]{0:T(128)} %bitcast.place, s32[2,8]{1,0:T(2,128)} %pad_add_fusion.bounds, s32[2048,1]{1,0:T(8,128)} %copy.75.seg_col, s32[1,2048]{1,0:T(1,128)} %bitcast.135, bf16[1024,1536]{1,0:T(8,128)(2,1)} %project.2.refs_0_, ...), custom_call_target="tpu_custom_call" | custom-call | flops 10737418240 | bytes 4194304 | tf_op jit(solution)/shard_map/attend_back/pallas_call | solution.py:479
  378.1 7.6 %input_part.1 = bf16[1024,1024]{1,0:T(8,128)(2,1)} custom-call(bf16[2,1024,384]{2,1,0:T(8,128)(2,1)} %get-tuple-element.262.refs_0_.refs_6_, bf16[2,1024,384]{2,1,0:T(8,128)(2,1)} %get-tuple-element.263.refs_1_.refs_7_, bf16[2,1024,384]{2,1,0:T(8,128)(2,1)} %get-tuple-element.264.refs_2_.refs_8_, bf16[2,1024,384]{2,1,0:T(8,128)(2,1)} %get-tuple-element.265.refs_3_.refs_9_, ...), custom_call_target="tpu_custom_call" | custom-call | flops 3221225472 | bytes 8388608 | tf_op jit(solution)/shard_map/input_part/pallas_call | solution.py:653
  413.3 12.1 %last.1 = (bf16[1024,1024]{1,0:T(8,128)(2,1)}, f32[8,2048]{1,0:T(8,128)}) custom-call(bf16[1024,1024]{1,0:T(8,128)(2,1)} %broadcast_select_fusion.2.x.refs_0_, bf16[1024,32]{1,0:T(8,128)(2,1)} %copy.76.member.refs_1_, bf16[16,1024]{1,0:T(8,128)(2,1)} %pad.18.refs_2_, f32[8,6144]{1,0:T(8,128)} %pad.15.adaptive.refs_3_, ...), custom_call_target="tpu_custom_call" | custom-call | flops 3221225472 | bytes 12582912 | tf_op jit(solution)/shard_map/last/pallas_call | solution.py:702
  430.3 5.0 %collective-permute-start.38 = (bf16[64,4096]{1,0:T(8,128)(2,1)}, bf16[64,4096]{1,0:T(8,128)(2,1)}, u32[]{:S(2)}, u32[]{:S(2)}) collective-permute-start(bf16[64,4096]{1,0:T(8,128)(2,1)} %pad_maximum_fusion.1), channel_id=1, source_target_pairs={{1,2},{2,1},{5,6},{6,5},{9,10},{10,9},{13,14},{14,13},{17,18},{18,... | collective-permute-start | bytes 1572872 | tf_op jit(solution)/shard_map/ppermute | solution.py:53
  457.1 10.2 %collective-permute-done.37 = bf16[1024,1024]{1,0:T(8,128)(2,1)} collective-permute-done((bf16[1024,1024]{1,0:T(8,128)(2,1)S(1)}, bf16[1024,1024]{1,0:T(8,128)(2,1)}, u32[]{:S(2)}, u32[]{:S(2)}) %collective-permute-start.37) | collective-permute-done | bytes 2097184 | tf_op jit(solution)/shard_map/ppermute | solution.py:53
  (256 shorter events, 152.3 us)
Async XLA Ops:
  15.2 31.7 %collective-permute-start.5 = (bf16[1024,1024]{1,0:T(8,128)(2,1)}, bf16[1024,1024]{1,0:T(8,128)(2,1)}, u32[]{:S(2)}, u32[]{:S(2)}) collective-permute-start(bf16[1024,1024]{1,0:T(8,128)(2,1)} %param.10), channel_id=1, source_target_pairs={{1,2},{2,1},{5,6},{6,5},{9,10},{10,9},{13,14},{14,13},{17,18},{18,... | collective-permute-start | bytes 6291464 | tf_op jit(solution)/shard_map/ppermute | solution.py:53
  21.8 24.0 %collective-permute-start.4 = (bf16[64,1536]{1,0:T(8,128)(2,1)S(1)}, bf16[64,1536]{1,0:T(8,128)(2,1)S(1)}, u32[]{:S(2)}, u32[]{:S(2)}) collective-permute-start(bf16[64,1536]{1,0:T(8,128)(2,1)S(1)} %broadcast_select_fusion.4), channel_id=1, source_target_pairs={{0,24},{8,16},{16,8},{24,0},{1,25},{9,17},{17,9},{25,1},{2,26},{10... | collective-permute-start | bytes 589832 | tf_op jit(solution)/shard_map/ppermute | solution.py:71
  25.2 20.6 %collective-permute-start.3 = (bf16[64,1536]{1,0:T(8,128)(2,1)S(1)}, bf16[64,1536]{1,0:T(8,128)(2,1)S(1)}, u32[]{:S(2)}, u32[]{:S(2)}) collective-permute-start(bf16[64,1536]{1,0:T(8,128)(2,1)S(1)} %broadcast_select_fusion.4), channel_id=1, source_target_pairs={{0,16},{8,24},{16,0},{24,8},{1,17},{9,25},{17,1},{25,9},{2,18},{10... | collective-permute-start | bytes 589832 | tf_op jit(solution)/shard_map/ppermute | solution.py:71
  25.2 20.6 %collective-permute-start.2 = (bf16[64,1536]{1,0:T(8,128)(2,1)S(1)}, bf16[64,1536]{1,0:T(8,128)(2,1)}, u32[]{:S(2)}, u32[]{:S(2)}) collective-permute-start(bf16[64,1536]{1,0:T(8,128)(2,1)S(1)} %broadcast_select_fusion.4), channel_id=1, source_target_pairs={{0,8},{8,0},{16,24},{24,16},{1,9},{9,1},{17,25},{25,17},{2,10},{10... | collective-permute-start | bytes 589832 | tf_op jit(solution)/shard_map/ppermute | solution.py:71
  31.5 141.1 %all-gather.2.cloned.1.call-start = ((), (), s32[]{:S(2)}) async-start(), calls=%async_computation.2 | async-start | bytes 10813440 | tf_op jit(solution)/shard_map/all_gather | solution.py:807
  56.1 20.9 %collective-permute-start.8 = (bf16[1024,1024]{1,0:T(8,128)(2,1)}, bf16[1024,1024]{1,0:T(8,128)(2,1)}, u32[]{:S(2)}, u32[]{:S(2)}) collective-permute-start(bf16[1024,1024]{1,0:T(8,128)(2,1)} %first_norm.1.a.refs_9_), channel_id=1, source_target_pairs={{2,0},{0,2},{3,1},{1,3},{6,4},{4,6},{7,5},{5,7},{10,8},{8,10},{11,... | collective-permute-start | bytes 6291464 | tf_op jit(solution)/shard_map/ppermute | solution.py:58
  56.2 19.7 %collective-permute-start.7 = (bf16[4,64,1536]{2,1,0:T(8,128)(2,1)S(1)}, bf16[4,64,1536]{2,1,0:T(8,128)(2,1)S(1)}, u32[]{:S(2)}, u32[]{:S(2)}) collective-permute-start(bf16[4,64,1536]{2,1,0:T(8,128)(2,1)S(1)} %pad_maximum_fusion.own), channel_id=1, source_target_pairs={{0,1},{1,0},{2,3},{3,2},{4,5},{5,4},{6,7},{7,6},{8,9},{9,8},{10,11... | collective-permute-start | bytes 2359304 | tf_op jit(solution)/shard_map/ppermute | solution.py:95
  58.2 18.8 %collective-permute-start.6 = (bf16[4,64,1536]{2,1,0:T(8,128)(2,1)S(1)}, bf16[4,64,1536]{2,1,0:T(8,128)(2,1)S(1)}, u32[]{:S(2)}, u32[]{:S(2)}) collective-permute-start(bf16[4,64,1536]{2,1,0:T(8,128)(2,1)S(1)} %pad_maximum_fusion.own), channel_id=1, source_target_pairs={{0,4},{4,0},{1,5},{5,1},{2,6},{6,2},{3,7},{7,3},{8,12},{12,8},{9,1... | collective-permute-start | bytes 2359304 | tf_op jit(solution)/shard_map/ppermute | solution.py:95
  109.3 44.2 %collective-permute-start.11 = (bf16[1024,1024]{1,0:T(8,128)(2,1)S(1)}, bf16[1024,1024]{1,0:T(8,128)(2,1)}, u32[]{:S(2)}, u32[]{:S(2)}) collective-permute-start(bf16[1024,1024]{1,0:T(8,128)(2,1)S(1)} %copy-done.2), channel_id=1, source_target_pairs={{1,2},{2,1},{5,6},{6,5},{9,10},{10,9},{13,14},{14,13},{17,18},{18,... | collective-permute-start | bytes 6291464 | tf_op jit(solution)/shard_map/ppermute | solution.py:53
  221.8 38.2 %collective-permute-start.17 = (bf16[1024,1024]{1,0:T(8,128)(2,1)S(1)}, bf16[1024,1024]{1,0:T(8,128)(2,1)}, u32[]{:S(2)}, u32[]{:S(2)}) collective-permute-start(bf16[1024,1024]{1,0:T(8,128)(2,1)S(1)} %copy-done.4), channel_id=1, source_target_pairs={{1,2},{2,1},{5,6},{6,5},{9,10},{10,9},{13,14},{14,13},{17,18},{18,... | collective-permute-start | bytes 6291464 | tf_op jit(solution)/shard_map/ppermute | solution.py:53
  230.3 32.8 %collective-permute-start.14 = (bf16[1024,1024]{1,0:T(8,128)(2,1)}, bf16[1024,1024]{1,0:T(8,128)(2,1)}, u32[]{:S(2)}, u32[]{:S(2)}) collective-permute-start(bf16[1024,1024]{1,0:T(8,128)(2,1)} %convolution_convert_fusion), channel_id=1, source_target_pairs={{0,2},{2,0},{1,3},{3,1},{4,6},{6,4},{5,7},{7,5},{8,10},{10,8},{9,1... | collective-permute-start | bytes 6291464 | tf_op jit(solution)/shard_map/ppermute | solution.py:63
  230.3 32.8 %collective-permute-start.13 = (bf16[1024,1024]{1,0:T(8,128)(2,1)}, bf16[1024,1024]{1,0:T(8,128)(2,1)}, u32[]{:S(2)}, u32[]{:S(2)}) collective-permute-start(bf16[1024,1024]{1,0:T(8,128)(2,1)} %convolution_convert_fusion.2), channel_id=1, source_target_pairs={{0,2},{2,0},{1,3},{3,1},{4,6},{6,4},{5,7},{7,5},{8,10},{10,8},{9,1... | collective-permute-start | bytes 6291464 | tf_op jit(solution)/shard_map/ppermute | solution.py:63
  233.1 29.9 %collective-permute-start.15 = (bf16[1024,512]{1,0:T(8,128)(2,1)}, bf16[1024,512]{1,0:T(8,128)(2,1)S(1)}, u32[]{:S(2)}, u32[]{:S(2)}) collective-permute-start(bf16[1024,512]{1,0:T(8,128)(2,1)} %convolution_convert_fusion.4), channel_id=1, source_target_pairs={{0,2},{2,0},{1,3},{3,1},{4,6},{6,4},{5,7},{7,5},{8,10},{10,8},{9,1... | collective-permute-start | bytes 3145736 | tf_op jit(solution)/shard_map/ppermute | solution.py:63
  271.4 57.9 %collective-permute-start.18 = (bf16[4,64,2560]{2,1,0:T(8,128)(2,1)}, bf16[4,64,2560]{2,1,0:T(8,128)(2,1)S(1)}, u32[]{:S(2)}, u32[]{:S(2)}) collective-permute-start(bf16[4,64,2560]{2,1,0:T(8,128)(2,1)} %get-tuple-element.203), channel_id=1, source_target_pairs={{0,4},{4,0},{1,5},{5,1},{2,6},{6,2},{3,7},{7,3},{8,12},{12,8},{9,1... | collective-permute-start | bytes 3932168 | tf_op jit(solution)/shard_map/ppermute | solution.py:180
  274.9 54.4 %collective-permute-start.19 = (bf16[4,64,2560]{2,1,0:T(8,128)(2,1)}, bf16[4,64,2560]{2,1,0:T(8,128)(2,1)S(1)}, u32[]{:S(2)}, u32[]{:S(2)}) collective-permute-start(bf16[4,64,2560]{2,1,0:T(8,128)(2,1)} %get-tuple-element.204), channel_id=1, source_target_pairs={{0,1},{1,0},{2,3},{3,2},{4,5},{5,4},{6,7},{7,6},{8,9},{9,8},{10,11... | collective-permute-start | bytes 3932168 | tf_op jit(solution)/shard_map/ppermute | solution.py:179
  274.9 58.9 %collective-permute-start.20 = (bf16[4,64,2560]{2,1,0:T(8,128)(2,1)}, bf16[4,64,2560]{2,1,0:T(8,128)(2,1)}, u32[]{:S(2)}, u32[]{:S(2)}) collective-permute-start(bf16[4,64,2560]{2,1,0:T(8,128)(2,1)} %get-tuple-element.205), channel_id=1, source_target_pairs={{0,5},{1,4},{4,1},{5,0},{2,7},{3,6},{6,3},{7,2},{8,13},{9,12},{12,... | collective-permute-start | bytes 3932168 | tf_op jit(solution)/shard_map/ppermute | solution.py:178
  337.9 35.8 %collective-permute-start.22 = (bf16[64,2560]{1,0:T(8,128)(2,1)S(1)}, bf16[64,2560]{1,0:T(8,128)(2,1)}, u32[]{:S(2)}, u32[]{:S(2)}) collective-permute-start(bf16[64,2560]{1,0:T(8,128)(2,1)S(1)} %get-tuple-element.224), channel_id=1, source_target_pairs={{0,16},{8,24},{16,0},{24,8},{1,17},{9,25},{17,1},{25,9},{2,18},{10... | collective-permute-start | bytes 983048 | tf_op jit(solution)/shard_map/ppermute | solution.py:71
  344.2 29.6 %collective-permute-start.23 = (bf16[64,2560]{1,0:T(8,128)(2,1)S(1)}, bf16[64,2560]{1,0:T(8,128)(2,1)}, u32[]{:S(2)}, u32[]{:S(2)}) collective-permute-start(bf16[64,2560]{1,0:T(8,128)(2,1)S(1)} %get-tuple-element.225), channel_id=1, source_target_pairs={{0,24},{8,16},{16,8},{24,0},{1,25},{9,17},{17,9},{25,1},{2,26},{10... | collective-permute-start | bytes 983048 | tf_op jit(solution)/shard_map/ppermute | solution.py:71
  345.3 28.5 %collective-permute-start.24 = (bf16[4,64,1152]{2,1,0:T(8,128)(2,1)}, bf16[4,64,1152]{2,1,0:T(8,128)(2,1)S(1)}, u32[]{:S(2)}, u32[]{:S(2)}) collective-permute-start(bf16[4,64,1152]{2,1,0:T(8,128)(2,1)} %get-tuple-element.227), channel_id=1, source_target_pairs={{0,4},{4,0},{1,5},{5,1},{2,6},{6,2},{3,7},{7,3},{8,12},{12,8},{9,1... | collective-permute-start | bytes 1769480 | tf_op jit(solution)/shard_map/ppermute | solution.py:180
  345.3 28.5 %collective-permute-start.25 = (bf16[4,64,1152]{2,1,0:T(8,128)(2,1)}, bf16[4,64,1152]{2,1,0:T(8,128)(2,1)S(1)}, u32[]{:S(2)}, u32[]{:S(2)}) collective-permute-start(bf16[4,64,1152]{2,1,0:T(8,128)(2,1)} %get-tuple-element.228), channel_id=1, source_target_pairs={{0,1},{1,0},{2,3},{3,2},{4,5},{5,4},{6,7},{7,6},{8,9},{9,8},{10,11... | collective-permute-start | bytes 1769480 | tf_op jit(solution)/shard_map/ppermute | solution.py:179
  345.4 28.4 %collective-permute-start.26 = (bf16[4,64,1152]{2,1,0:T(8,128)(2,1)}, bf16[4,64,1152]{2,1,0:T(8,128)(2,1)S(1)}, u32[]{:S(2)}, u32[]{:S(2)}) collective-permute-start(bf16[4,64,1152]{2,1,0:T(8,128)(2,1)} %get-tuple-element.229), channel_id=1, source_target_pairs={{0,5},{1,4},{4,1},{5,0},{2,7},{3,6},{6,3},{7,2},{8,13},{9,12},{12,... | collective-permute-start | bytes 1769480 | tf_op jit(solution)/shard_map/ppermute | solution.py:178
  385.7 23.2 %collective-permute-start.33 = (bf16[1024,1024]{1,0:T(8,128)(2,1)}, bf16[1024,1024]{1,0:T(8,128)(2,1)S(1)}, u32[]{:S(2)}, u32[]{:S(2)}) collective-permute-start(bf16[1024,1024]{1,0:T(8,128)(2,1)} %input_part.1), channel_id=1, source_target_pairs={{0,2},{2,0},{1,3},{3,1},{4,6},{6,4},{5,7},{7,5},{8,10},{10,8},{9,1... | collective-permute-start | bytes 6291464 | tf_op jit(solution)/shard_map/ppermute | solution.py:63
  430.3 19.3 %collective-permute-start.38 = (bf16[64,4096]{1,0:T(8,128)(2,1)}, bf16[64,4096]{1,0:T(8,128)(2,1)}, u32[]{:S(2)}, u32[]{:S(2)}) collective-permute-start(bf16[64,4096]{1,0:T(8,128)(2,1)} %pad_maximum_fusion.1), channel_id=1, source_target_pairs={{1,2},{2,1},{5,6},{6,5},{9,10},{10,9},{13,14},{14,13},{17,18},{18,... | collective-permute-start | bytes 1572872 | tf_op jit(solution)/shard_map/ppermute | solution.py:53
  439.3 28.0 %collective-permute-start.37 = (bf16[1024,1024]{1,0:T(8,128)(2,1)S(1)}, bf16[1024,1024]{1,0:T(8,128)(2,1)}, u32[]{:S(2)}, u32[]{:S(2)}) collective-permute-start(bf16[1024,1024]{1,0:T(8,128)(2,1)S(1)} %copy-done.5), channel_id=1, source_target_pairs={{1,2},{2,1},{5,6},{6,5},{9,10},{10,9},{13,14},{14,13},{17,18},{18,... | collective-permute-start | bytes 6291464 | tf_op jit(solution)/shard_map/ppermute | solution.py:53
  (67 other events, 636.1 us)
Sparse Core Ops, SparseCore 0:
  77.2 95.4 all-gather.1

commit v3 on v2

--- a/solution.py
+++ b/solution.py
@@ -181,21 +181,29 @@
     return own, from_zb, from_hh, from_both
 
 
-def cut_line(pieces):
-    total = sum(piece.astype(F32) for piece in pieces).astype(BF16)
-    mine = lax.axis_index("za")
-    return [
-        lax.dynamic_index_in_dim(total, mine ^ bits, 0, keepdims=False)
-        for bits in range(total.shape[0])
-    ]
-
-
-def swap_line(cuts):
-    return [cuts[0]] + [across(cut, bits) for bits, cut in enumerate(cuts) if bits]
-
-
-def total_of(cuts):
-    return sum(cut.astype(F32) for cut in cuts).astype(BF16)
+def add_up(pieces):
+    return sum(piece.astype(F32) for piece in pieces).astype(BF16)
+
+
+def cut_line(total, bit):
+    pairs = total.reshape(total.shape[0] // 2, 2, *total.shape[1:])
+    place = (lax.axis_index("za") // bit) % 2
+    keep = lax.dynamic_index_in_dim(pairs, place, 1, keepdims=False)
+    send = lax.dynamic_index_in_dim(pairs, 1 - place, 1, keepdims=False)
+    return keep, send
+
+
+def swap_line(cuts, bit):
+    return cuts[0], across(cuts[1], bit)
+
+
+def line_rest(pieces):
+    total = add_up(pieces)
+    count = total.shape[0]
+    apart = lax.axis_size("za") // count
+    mine = lax.axis_index("za") // apart
+    cuts = [lax.dynamic_index_in_dim(total, mine ^ n, 0, keepdims=False) for n in range(count)]
+    return add_up([cuts[0]] + [across(cut, n * apart) for n, cut in enumerate(cuts) if n])
 
 
 def together(*values):
@@ -302,6 +310,14 @@
     )(place, a, w, cosine, sine)
 
 
+def stack_heads(values, heads):
+    none = jnp.zeros_like(values)
+    lanes = values.shape[1]
+    return jnp.concatenate(
+        [jnp.where(lane_mask(lanes, head), values, none) for head in range(heads)], axis=0
+    )
+
+
 def lane_mask(lanes, head):
     return lax.broadcasted_iota(jnp.int32, (1, lanes), 1) // HEAD_DIM == head
 
@@ -328,46 +344,128 @@
             run(width)
 
 
+def head_sums(values):
+    lanes = values.shape[1]
+    row = lax.broadcasted_iota(jnp.int32, (lanes, lanes), 0) // HEAD_DIM
+    column = lax.broadcasted_iota(jnp.int32, (lanes, lanes), 1) // HEAD_DIM
+    same = (row == column).astype(BF16)
+    high = values.astype(BF16)
+    low = (values - high.astype(F32)).astype(BF16)
+    return dot(high, same) + dot(low, same)
+
+
+def swap_heads(values):
+    parts = [pltpu.roll(values[:, at : at + 128], HEAD_DIM, 1) for at in range(0, values.shape[1], 128)]
+    return parts[0] if len(parts) == 1 else jnp.concatenate(parts, axis=1)
+
+
+def largest_sum(ref, step):
+    lanes = ref.shape[1]
+    row = lax.broadcasted_iota(jnp.int32, (lanes, lanes), 0) // HEAD_DIM
+    column = lax.broadcasted_iota(jnp.int32, (lanes, lanes), 1) // HEAD_DIM
+    same = (row == column).astype(BF16)
+    largest = jnp.zeros((1, lanes), F32)
+    for at in range(0, ref.shape[0], step):
+        values = ref[at : at + step, :]
+        sums = dot(values * values, same)
+        largest = jnp.maximum(largest, jnp.max(sums, axis=0, keepdims=True))
+    return largest
+
+
 def attend_kernel(pieces, heads, step, place, bounds, seg_col, seg_row, *refs):
     inputs = refs[:pieces]
     outs = refs[pieces : 2 * pieces]
-    lse, q_all, k_all, v_all, o_all, bias = refs[2 * pieces :]
+    lse, q_all, k_all, v_all, v_even, v_odd, o_all, bias, highest, total, product = refs[2 * pieces :]
     rows = inputs[0].shape[0]
+    frames, lanes = q_all.shape
+    even = lax.broadcasted_iota(jnp.int32, (1, lanes), 1) // HEAD_DIM % 2 == 0
     for piece in range(pieces):
         span = pl.ds(piece_start(place, piece, pieces, rows), rows)
         spread(inputs[piece], span, (q_all, k_all, v_all))
-    frames, lanes = q_all.shape
-    lane = lax.broadcasted_iota(jnp.int32, (1, 128), 1)
-
-    def one_block(i, _):
-        block = pl.ds(pl.multiple_of(i * step, step), step)
-        low = pl.multiple_of(bounds[0, i], 128)
-
+        value = v_all[span, :]
+        v_even[span, :] = jnp.where(even, value, jnp.ones_like(value))
+        v_odd[span, :] = jnp.where(even, jnp.ones_like(value), value)
+    limit = jnp.sqrt(largest_sum(q_all, 2 * step) * largest_sum(k_all, 2 * step))
+    shift = limit * 1.02 - 60.0
+
+    def each_block(run):
+        def one_block(i, _):
+            block = pl.ds(pl.multiple_of(i * step, step), step)
+            run(block, pl.multiple_of(bounds[0, i], 128), bounds[1, i])
+            return 0
+
+        lax.fori_loop(0, frames // step, one_block, 0)
+
+    def set_bias(block, span, width):
+        same = seg_col[block, :] == seg_row[0:1, span]
+        bias[:, 0:width] = jnp.where(same, 0.0, MASKED)
+
+    def shifted(block, low, count):
         def run(width):
             width = width * step
             span = pl.ds(low, width)
-            same = seg_col[block, :] == seg_row[0:1, span]
-            bias[:, 0:width] = jnp.where(same, 0.0, MASKED)
-            query, key, value = q_all[block, :], k_all[span, :], v_all[span, :]
-            result = jnp.zeros((step, lanes), F32)
-            stats = jnp.zeros((step, 128), F32)
+            set_bias(block, span, width)
+            query, key = q_all[block, :], k_all[span, :]
+            above = jnp.zeros((step, lanes), F32)
+            below = jnp.ones((step, lanes), F32)
             for head in range(heads):
-                keep = lane_mask(lanes, head)
-                masked = jnp.where(keep, query, jnp.zeros_like(query))
+                masked = jnp.where(lane_mask(lanes, head), query, jnp.zeros_like(query))
                 scores = dot(masked, key, NT) + bias[:, 0:width]
-                highest = jnp.max(scores, axis=1, keepdims=True)
-                weight = jnp.exp(scores - highest)
-                total = jnp.sum(weight, axis=1, keepdims=True)
-                part = dot(weight.astype(BF16), value)
-                result = jnp.where(keep, part / total, result)
-                stats = jnp.where(lane == head, highest + jnp.log(total), stats)
-            o_all[block, :] = result.astype(BF16)
-            lse[0, block, :] = stats
-
-        each_width(bounds[1, i], frames // step, run)
-        return 0
-
-    lax.fori_loop(0, frames // step, one_block, 0)
+                at = head * HEAD_DIM
+                weight = jnp.exp(scores - shift[:, at : at + 1]).astype(BF16)
+                part = dot(weight, (v_odd if head % 2 else v_even)[span, :])
+                above = jnp.where(lane_mask(lanes, head), part, above)
+                below = jnp.where(lane_mask(lanes, head ^ 1), part, below)
+            sums = swap_heads(below)
+            o_all[block, :] = (above / sums).astype(BF16)
+            lse[0, block, :] = sums
+
+        each_width(count, frames // step, run)
+
+    def exact(block, low, count):
+        query = q_all[block, :]
+        highest[...] = jnp.full_like(highest, MASKED)
+        total[...] = jnp.zeros_like(total)
+        product[...] = jnp.zeros_like(product)
+
+        def one_step(j, _):
+            span = pl.ds(pl.multiple_of(low + j * step, 128), step)
+            set_bias(block, span, step)
+            key, value = k_all[span, :], v_all[span, :]
+            for head in range(heads):
+                masked = jnp.where(lane_mask(lanes, head), query, jnp.zeros_like(query))
+                scores = dot(masked, key, NT) + bias[:, 0:step]
+                before = highest[head, :, 0:1]
+                top = jnp.maximum(before, jnp.max(scores, axis=1, keepdims=True))
+                weight = jnp.exp(scores - top)
+                fade = jnp.exp(before - top)
+                highest[head] = jnp.broadcast_to(top, (step, 128))
+                total[head] = total[head] * fade + jnp.sum(weight, axis=1, keepdims=True)
+                product[head] = product[head] * fade + dot(weight.astype(BF16), value)
+            return 0
+
+        lax.fori_loop(0, count, one_step, 0)
+        result = jnp.zeros((step, lanes), F32)
+        logs = jnp.zeros((step, lanes), F32)
+        for head in range(heads):
+            keep = lane_mask(lanes, head)
+            sums = total[head, :, 0:1]
+            result = jnp.where(keep, product[head] / sums, result)
+            logs = jnp.where(keep, highest[head, :, 0:1] + jnp.log(sums), logs)
+        o_all[block, :] = result.astype(BF16)
+        lse[0, block, :] = logs
+
+    each_block(shifted)
+    safe = jnp.min(lse[0]) > 1e-30
+
+    @pl.when(safe)
+    def _():
+        lse[0] = shift + jnp.log(lse[0])
+
+    @pl.when(jnp.logical_not(safe))
+    def _():
+        each_block(exact)
+
     for piece in range(pieces):
         outs[piece][...] = o_all[pl.ds(piece_start(place, piece, pieces, rows), rows), :]
 
@@ -385,11 +483,17 @@
         functools.partial(attend_kernel, pieces, heads, step),
         grid=(groups,),
         out_shape=[jax.ShapeDtypeStruct((rows, groups * lanes), BF16)] * pieces
-        + [jax.ShapeDtypeStruct((groups, frames, 128), F32)],
+        + [jax.ShapeDtypeStruct((groups, frames, lanes), F32)],
         in_specs=[smem, smem, whole(seg_col.shape), whole(seg_row.shape)] + specs,
         out_specs=[pl.BlockSpec((rows, lanes), lambda g: (0, g))] * pieces
-        + [pl.BlockSpec((1, frames, 128), lambda g: (g, 0, 0))],
-        scratch_shapes=[pltpu.VMEM((frames, lanes), BF16)] * 4 + [pltpu.VMEM((step, frames), F32)],
+        + [pl.BlockSpec((1, frames, lanes), lambda g: (g, 0, 0))],
+        scratch_shapes=[pltpu.VMEM((frames, lanes), BF16)] * 6
+        + [
+            pltpu.VMEM((step, frames), F32),
+            pltpu.VMEM((heads, step, 128), F32),
+            pltpu.VMEM((heads, step, 128), F32),
+            pltpu.VMEM((heads, step, lanes), F32),
+        ],
         compiler_params=params(),
         cost_estimate=cost(area * 4 * 256, frames * columns * 4, area),
         name="attend",
@@ -397,20 +501,29 @@
     return results[:pieces], results[pieces]
 
 
-def attend_back_kernel(pieces, first, heads, step, place, bounds, seg_col, seg_row, *refs):
+def attend_back_kernel(pieces, heads, step, place, bounds, seg_col, seg_row, *refs):
     inputs = refs[: 3 * pieces]
-    lse, cosine, sine = refs[3 * pieces : 3 * pieces + 3]
-    normed = refs[3 * pieces + 3 : 4 * pieces + 3]
+    lse = refs[3 * pieces]
+    later = refs[3 * pieces + 1 : 4 * pieces + 3]
     out, grad_w = refs[4 * pieces + 3 : 4 * pieces + 5]
-    q_all, k_all, v_all, o_all, do_all, dq_all, dk_all, dv_all, bias, weights, slopes = refs[
-        4 * pieces + 5 :
+    q_all, k_all, v_all, do_all, centre, dq_all, dk_all, dv_all, bias, weights, slopes = refs[
+        4 * pieces + 5 : 4 * pieces + 16
     ]
+    held, sems = refs[4 * pieces + 16 : -1], refs[-1]
+    copies = [
+        pltpu.make_async_copy(source, target, sems.at[n])
+        for n, (source, target) in enumerate(zip(later, held))
+    ]
+    for copy in copies:
+        copy.start()
+    cosine, sine, *normed = held
     rows = inputs[0].shape[0]
     for piece in range(pieces):
         span = pl.ds(piece_start(place, piece, pieces, rows), rows)
         spread(inputs[3 * piece], span, (q_all, k_all, v_all))
-        o_all[span, :] = inputs[3 * piece + 1][...]
-        do_all[span, :] = inputs[3 * piece + 2][...]
+        grad = inputs[3 * piece + 2][...]
+        do_all[span, :] = grad
+        centre[span, :] = head_sums(grad.astype(F32) * inputs[3 * piece + 1][...].astype(F32))
     frames, lanes = q_all.shape
     dk_all[...] = jnp.zeros_like(dk_all)
     dv_all[...] = jnp.zeros_like(dv_all)
@@ -426,30 +539,34 @@
             bias[:, 0:width] = jnp.where(same, 0.0, MASKED)
             query, key, value = q_all[block, :], k_all[span, :], v_all[span, :]
             grad = do_all[block, :]
-            product = grad.astype(F32) * o_all[block, :].astype(F32)
-            result = jnp.zeros((step, lanes), F32)
-            queries, grads = [], []
+            queries = stack_heads(query, heads)
+            grads = stack_heads(grad, heads)
             for head in range(heads):
-                keep = lane_mask(lanes, head)
-                queries.append(jnp.where(keep, query, jnp.zeros_like(query)))
-                grads.append(jnp.where(keep, grad, jnp.zeros_like(grad)))
-                centre = jnp.sum(jnp.where(keep, product, 0.0), axis=1, keepdims=True)
-                scores = dot(queries[head], key, NT) + bias[:, 0:width]
-                weight = jnp.exp(scores - lse[0, block, first + head : first + head + 1])
-                slope = dot(grads[head], value, NT) - centre
-                slope = (weight * slope).astype(BF16)
-                at = pl.ds(head * step, step)
+                at = slice(head * step, (head + 1) * step)
+                column = slice(head * HEAD_DIM, head * HEAD_DIM + 1)
+                scores = dot(queries[at], key, NT) + bias[:, 0:width]
+                weight = jnp.exp(scores - lse[0, block, column])
                 weights[at, 0:width] = weight.astype(BF16)
-                slopes[at, 0:width] = slope
-                result = jnp.where(keep, dot(slope, key), result)
+            for head in range(heads):
+                at = slice(head * step, (head + 1) * step)
+                column = slice(head * HEAD_DIM, head * HEAD_DIM + 1)
+                slope = dot(grads[at], value, NT) - centre[block, column]
+                slopes[at, 0:width] = (weights[at, 0:width].astype(F32) * slope).astype(BF16)
+            part = dot(slopes[:, 0:width], key)
+            result = part[0:step]
+            for head in range(1, heads):
+                here = part[head * step : (head + 1) * step]
+                result = jnp.where(lane_mask(lanes, head), here, result)
             dq_all[block, :] = result * HEAD_DIM**-0.5
-            dv_all[span, :] += dot(weights[:, 0:width], jnp.concatenate(grads, axis=0), TN)
-            dk_all[span, :] += dot(slopes[:, 0:width], jnp.concatenate(queries, axis=0), TN)
+            dv_all[span, :] += dot(weights[:, 0:width], grads, TN)
+            dk_all[span, :] += dot(slopes[:, 0:width], queries, TN)
 
         each_width(bounds[1, i], frames // step, run)
         return 0
 
     lax.fori_loop(0, frames // step, one_block, 0)
+    for copy in copies:
+        copy.wait()
     for piece in range(pieces):
         span = pl.ds(piece_start(place, piece, pieces, rows), rows)
         cos = cosine[span, :]
@@ -477,7 +594,7 @@
     smem = pl.BlockSpec(memory_space=pltpu.SMEM)
     area = frames * frames // 2 * heads
     return pl.pallas_call(
-        functools.partial(attend_back_kernel, pieces, pair % per_group * heads, heads, step),
+        functools.partial(attend_back_kernel, pieces, heads, step),
         grid=(1,),
         out_shape=[
             jax.ShapeDtypeStruct((pieces, rows, 3 * lanes), BF16),
@@ -487,17 +604,20 @@
         + specs
         + [
             pl.BlockSpec(
-                (1, frames, 128), lambda i: (pair // per_group, 0, 0), pipeline_mode=pl.Buffered(1)
+                (1, frames, 128),
+                lambda i: (pair // per_group, 0, pair % per_group),
+                pipeline_mode=pl.Buffered(1),
             ),
-            whole(cosine.shape, 1),
-            whole(sine.shape, 1),
         ]
-        + [whole(normed[0].shape, 1)] * pieces,
+        + [pl.BlockSpec(memory_space=pl.ANY)] * (pieces + 2),
         out_specs=[whole((pieces, rows, 3 * lanes), 1), whole((width, 3 * lanes), 1)],
-        scratch_shapes=[pltpu.VMEM((frames, lanes), BF16)] * 5
-        + [pltpu.VMEM((frames, lanes), F32)] * 3
+        scratch_shapes=[pltpu.VMEM((frames, lanes), BF16)] * 4
+        + [pltpu.VMEM((frames, lanes), F32)] * 4
         + [pltpu.VMEM((step, frames), F32)]
-        + [pltpu.VMEM((heads * step, frames), BF16)] * 2,
+        + [pltpu.VMEM((heads * step, frames), BF16)] * 2
+        + [pltpu.VMEM(cosine.shape, F32)] * 2
+        + [pltpu.VMEM(normed[0].shape, BF16)] * pieces
+        + [pltpu.SemaphoreType.DMA((pieces + 2,))],
         compiler_params=params(),
         cost_estimate=cost(area * 10 * 256, frames * lanes * 16, area),
         name="attend_back",
@@ -692,12 +812,13 @@
     dadaptive[:, width:] += gather(member_flip[...], da1 * normed)
 
 
-def last(x, member, member_flip, adaptive, dx2, arrived, slopes, weights):
-    rows, width = x.shape
+def last(half, x, member, member_flip, adaptive, dx2, arrived, slopes, weights):
+    rows, width = x.shape[0] // 2, x.shape[1]
     tile = min(256, rows)
+    first = half * (rows // tile)
 
     def tiled(columns):
-        return pl.BlockSpec((tile, columns), lambda i: (i, 0))
+        return pl.BlockSpec((tile, columns), lambda i: (first + i, 0))
 
     return pl.pallas_call(
         functools.partial(last_kernel, len(slopes), len(arrived)),
@@ -705,18 +826,18 @@
         in_specs=[
             tiled(width),
             tiled(32),
-            pl.BlockSpec((16, tile), lambda i: (0, i)),
+            pl.BlockSpec((16, tile), lambda i: (0, first + i)),
             whole(adaptive.shape, 1),
             tiled(width),
         ]
         + [tiled(width)] * len(arrived)
-        + [pl.BlockSpec((None, tile, s.shape[2]), lambda i: (0, i, 0)) for s in slopes]
+        + [pl.BlockSpec((None, tile, s.shape[2]), lambda i: (0, first + i, 0)) for s in slopes]
         + [whole(weights.shape, 1)],
         out_shape=[
             jax.ShapeDtypeStruct((rows, width), BF16),
             jax.ShapeDtypeStruct((8, 2 * width), F32),
         ],
-        out_specs=[tiled(width), whole((8, 2 * width))],
+        out_specs=[pl.BlockSpec((tile, width), lambda i: (i, 0)), whole((8, 2 * width))],
         compiler_params=params(),
         cost_estimate=cost(2 * rows * width * sum(s.shape[2] for s in slopes), rows * width * 12),
         name="last",
@@ -800,13 +921,16 @@
 
     x = moved(frames)
     held = gather_line(qkv_shard)
-    held, adaptive, x, cosine, sine, member = together(held, adaptive, x, cosine, sine, member)
+    held, adaptive, x, cosine, sine, member, mlp_shard = together(
+        held, adaptive, x, cosine, sine, member, mlp_shard
+    )
     near = gather_near(held)
-    a1_all = around(first_norm(x, member, adaptive))
-    near, a1_all, mlp_shard, grad_out = together(near, a1_all, mlp_shard, grad_out)
     mlp_full = lax.all_gather(mlp_shard, ALL, axis=0, tiled=True)
     mlp_full = mlp_full.reshape(-1, pieces, own_rows, mlp_shard.shape[1])
-    qkv_full = gathered(*gather_far(*near))
+    a1 = first_norm(x, member, adaptive)
+    near, a1, grad_out = together(near, a1, grad_out)
+    far, a1_all = together(gather_far(*near), around(a1))
+    qkv_full = gathered(*far)
     places = [((place + piece) % pieces).reshape(1) for piece in range(pieces)]
     qkv = [
         project(places[piece], a1_all[piece], qkv_full, cosine, sine, lanes)
@@ -859,32 +983,36 @@
     if pairs > 1:
         early = cut_plane([[grad] for grad in grads_qkv])
     late, early, slopes, grads_qkv = together(late, early, slopes, grads_qkv)
-    late, qkv = together(cut_line(late), qkv)
-    late = swap_line(late)
+    late, qkv = together(cut_line(add_up(late), 1), qkv)
+    late = swap_line(late, 1)
     if pairs > 1:
         early = swap_plane(early)
         next_pair()
     late, early, slopes, grads_qkv = together(late, early, slopes, grads_qkv)
     final = cut_plane([grads_qkv[-1:]])
+    late = add_up(late)
     if pairs > 1:
-        early = cut_line(early)
-    final, early, slopes = together(final, early, slopes)
+        early = cut_line(add_up(early), 1)
+    final, early, late, slopes, dx2 = together(final, early, late, slopes, dx2)
     final = swap_plane(final)
+    late = line_rest([late])
     if pairs > 1:
-        early = swap_line(early)
-    arrived = [to_sub(input_part(slopes, qkv_full, piece), piece) for piece in range(1, pieces)]
-    final, early, arrived = together(final, early, arrived)
-    final, dx2 = together(cut_line(final), dx2)
-    final = swap_line(final)
-    grad_frames, dada_early = last(
-        x, member, member_flip, adaptive, dx2, arrived, slopes, qkv_full
-    )
-    late, early, final, grad_frames, dada_early = together(
-        late, early, final, grad_frames, dada_early
-    )
-    grad_frames = moved(grad_frames).astype(F32)
-    sums = [total_of(cuts) for cuts in (late, early, final) if cuts]
-    sums = moved(jnp.concatenate(sums, axis=1))
+        early = swap_line(early, 1)
+    parts = [input_part(slopes, qkv_full, piece) for piece in range(1, pieces)]
+    final, early, late, parts = together(final, early, late, parts)
+    arrived = [to_sub(part, piece) for piece, part in enumerate(parts, 1)]
+    final = line_rest(final)
+    sums = [late]
+    if pairs > 1:
+        sums.append(line_rest(early))
+    final, sums, arrived, dx2 = together(final, sums, arrived, dx2)
+    sums = moved(jnp.concatenate(sums + [final], axis=1))
+    def rows_half(half, dx2):
+        return last(half, x, member, member_flip, adaptive, dx2, arrived, slopes, qkv_full)
+
+    sums, dx2, (frames_low, dada_low) = together(sums, dx2, rows_half(0, dx2))
+    frames_low, (frames_high, dada_high) = together(moved(frames_low), rows_half(1, dx2))
+    dada_early = dada_low + dada_high
     late, rest = sums[:, : mlp_shard.shape[1]], sums[:, mlp_shard.shape[1] :]
     hidden_columns = w_up.shape[1]
     grad_up = late[:, :hidden_columns]
@@ -892,7 +1020,9 @@
     grad_outw = late[:, 2 * hidden_columns :]
     dadaptive = jnp.concatenate([dada_early, dada_late], axis=1)[:clips]
     dadaptive = jnp.transpose(dadaptive.reshape(clips, -1, columns), (1, 0, 2))
+    dadaptive, frames_high = together(dadaptive, frames_high)
     dadaptive = lax.all_to_all(dadaptive, ALL, 0, 0, tiled=True)
+    grad_frames = jnp.concatenate([frames_low, moved(frames_high)], axis=0).astype(F32)
     dadaptive = dadaptive.reshape(za, zb, cores, hh, hl, clips, columns)
     dadaptive = jnp.sum(dadaptive, axis=(2, 4)).reshape(-1, columns)
     grad_ada = dot(condition, dadaptive, TN, HIGHEST)

time: 486 us -> 460 us (0.947)
  starting transfers between devices: 82.1 us -> 65.2 us
    ppermute x1, waiting for transfers between devices: 16.6 us -> 0.53 us  [gather_near(): lax.ppermute(held, 'hh', SWAP)]
    ppermute x1, waiting for transfers between devices: 1.16 us -> 15.1 us  [gather_near(): lax.ppermute(held, 'zb', SWAP)]
    all_gather x1, waiting for transfers between devices: 13.4 us -> 0.01 us  [body(): mlp_full = lax.all_gather(mlp_shard, ALL, axis=0, tiled=True)]
    ppermute x1, waiting for transfers between devices: 0.04 us -> 10.9 us  [gather_far(): both_low = lax.ppermute(by_zb[:half], 'hh', SWAP)]
    ppermute x12 -> x10, starting transfers between devices: 24.1 us -> 14.3 us  [across(): return lax.ppermute(value, 'za', [(i, i ^ bit) for i in range(size)])]
    ppermute x1, waiting for transfers between devices: 8.06 us -> 0.01 us  [gather_far(): both_high = lax.ppermute(by_hh[half:], 'zb', SWAP)]
    ppermute x3, waiting for transfers between devices: 4.47 us -> 11.4 us  [swap_plane(): lax.ppermute(to_both, ('zb', 'hh'), [(0, 3), (1, 2), (2, 1), (3, 0)])]
    ppermute x7 -> x8, waiting for transfers between devices: 11.9 us -> 5.21 us  [moved(): lax.ppermute(value, ('core', 'hh'), [(1, 2), (2, 1)])]
  transfers between devices with their start and end apart: 42 -> 41, of which waited for: 12 -> 13; matrix products, arithmetic and copies ran while one was open for 10% -> 12% of each run, Pallas kernels for 35% -> 39%
where the time goes in v3:
time: 460 us; the launch traced here: 452 us
  Pallas kernels  228 us (50%)
  waiting for transfers between devices  71.4 us (16%)
  starting transfers between devices  65.2 us (14%)
  other arithmetic  34.8 us (8%)
  matrix products  24 us (5%)
  between operations  15.4 us (3%)
  local copies, waits for them, and re-layouts  13.4 us (3%)
    pallas_call x4, Pallas kernels, attend_back(): pl.pallas_call(functools.partial(attend_back_kernel, pieces, heads, step)...  89.3 us
    pallas_call x1, Pallas kernels, middle(): pl.pallas_call(functools.partial(middle_kernel, pieces), grid_spec=pltpu....  38.8 us
    pallas_call x1, Pallas kernels, attend(): pl.pallas_call(functools.partial(attend_kernel, pieces, heads, step), gri...  33.9 us
    ppermute x8, starting transfers between devices, moved(): lax.ppermute(value, ('core', 'hh'), [(1, 2), (2, 1)])  27.5 us
    dot_general x7, matrix products, dot(): lax.dot_general(a, b, dims, precision=precision, preferred_element_type=F32)  23.1 us
    pallas_call x2, Pallas kernels, last(): pl.pallas_call(functools.partial(last_kernel, len(slopes), len(arrived)),...  16.1 us
    pallas_call x3, Pallas kernels, cut_plane(): pl.pallas_call(functools.partial(cut_kernel, [len(group) for group in wei...  16 us
    pallas_call x2, Pallas kernels, project(): pl.pallas_call(functools.partial(project_kernel, lanes), grid_spec=pltpu....  16 us
  transfers between devices with their start and end apart: 41, of which 13 were waited for; matrix products, arithmetic and copies ran while one was open for 12% of the time, Pallas kernels for 39%

profile of v3, /device:TPU:1, one launch (start us, length us, event | category | flops | bytes accessed | tf_op | source)
XLA Modules:
  0.0 451.9 jit_solution(2007415785236839366)
XLA Ops:
  27.1 5.3 %all-to-all-start = ((f32[32,4,192]{2,1,0:T(4,128)}), f32[32,4,192]{2,1,0:T(4,128)S(1)}, u32[]{:S(2)}, u32[]{:S(2)}) async-start(f32[32,4,192]{2,1,0:T(4,128)} %bitcast.6), calls=%async_computation | async-start | bytes 262144 | tf_op jit(solution)/shard_map/all_to_all | solution.py:888
  32.9 5.6 %fusion = (f32[2048,128]{1,0:T(8,128)}, f32[2048,128]{1,0:T(8,128)}) fusion(f32[128]{0:T(128)S(1)} %get-tuple-element.317, f32[128]{0:T(128)S(1)} %get-tuple-element.318, f32[2048]{0:T(1024)S(1)} %subtract_convert_fusion), kind=kLoop, calls=%fused_computation.16 | loop fusion | flops 524288 | bytes 2106368 | tf_op jit(solution)/shard_map/mul | solution.py:903
  38.6 6.4 %all-to-all-done = f32[32,4,192]{2,1,0:T(4,128)S(1)} async-done(((f32[32,4,192]{2,1,0:T(4,128)}), f32[32,4,192]{2,1,0:T(4,128)S(1)}, u32[]{:S(2)}, u32[]{:S(2)}) %all-to-all-start) | async-done | bytes 98336 | tf_op jit(solution)/shard_map/all_to_all | solution.py:888
  52.7 4.8 %first_norm.1.a.refs_9_ = bf16[1024,1024]{1,0:T(8,128)(2,1)} custom-call(bf16[1024,1024]{1,0:T(8,128)(2,1)} %broadcast_select_fusion.2.x.refs_0_, bf16[1024,32]{1,0:T(8,128)(2,1)} %copy.81.member.refs_1_, f32[8,6144]{1,0:T(8,128)} %pad.15.adaptive.refs_3_), custom_call_target="tpu_custom_call" | custom-call | flops 41943040 | bytes 4194304 | tf_op jit(solution)/shard_map/first_norm/pallas_call | solution.py:245
  57.5 15.1 %collective-permute-done.6.by_zb = bf16[4,64,1536]{2,1,0:T(8,128)(2,1)S(1)} collective-permute-done((bf16[4,64,1536]{2,1,0:T(8,128)(2,1)S(1)}, bf16[4,64,1536]{2,1,0:T(8,128)(2,1)S(1)}, u32[]{:S(2)}, u32[]{:S(2)}) %collective-permute-start.6) | collective-permute-done | bytes 786464 | tf_op jit(solution)/shard_map/ppermute | solution.py:95
  76.0 10.9 %collective-permute-done.8.both_low = bf16[2,64,1536]{2,1,0:T(8,128)(2,1)S(1)} collective-permute-done((bf16[2,64,1536]{2,1,0:T(8,128)(2,1)S(1)}, bf16[2,64,1536]{2,1,0:T(8,128)(2,1)S(1)}, u32[]{:S(2)}, u32[]{:S(2)}) %collective-permute-start.8) | collective-permute-done | bytes 393248 | tf_op jit(solution)/shard_map/ppermute | solution.py:100
  87.8 5.0 %place.1 = bf16[4,2,2,64,1536]{4,3,2,1,0:T(8,128)(2,1)} custom-call(s32[6]{0:T(128)} %stack.64.where, bf16[4,64,1536]{2,1,0:T(8,128)(2,1)} %copy-done.1, bf16[4,64,1536]{2,1,0:T(8,128)(2,1)} %copy-done.5, bf16[4,64,1536]{2,1,0:T(8,128)(2,1)} %copy-done.6, bf16[2,64,1536]{2,1,0:T(8,128)(2,1)} %copy-done.11, bf16[2,64,1536]{2,1,0:T(8,128)(2,1)} %copy-done.12), custom_call_target="tpu_custom_call" | custom-call | bytes 6291456 | tf_op jit(solution)/shard_map/place/pallas_call | solution.py:112
  92.8 8.0 %project.3.refs_1_.refs_3_ = bf16[1024,1536]{1,0:T(8,128)(2,1)} custom-call(s32[1]{0:T(128)} %bitcast.25.place, bf16[1024,1024]{1,0:T(8,128)(2,1)} %collective-permute-done.10.a.refs_10_, bf16[1024,1536]{1,0:T(8,128)(2,1)} %bitcast.116, f32[2048,128]{1,0:T(8,128)} %get-tuple-element.168.cosine.refs_7_, f32[2048,128]{1,0:T(8,128)} %get-tuple-element.169.sine.refs_8_), custom_call_target="tpu_custom_call" | custom-call | flops 3221225472 | bytes 5242880 | tf_op jit(solution)/shard_map/project/pallas_call | solution.py:293
  100.8 8.1 %project.2.refs_0_ = bf16[1024,1536]{1,0:T(8,128)(2,1)} custom-call(s32[1]{0:T(128)} %bitcast.17.place, bf16[1024,1024]{1,0:T(8,128)(2,1)} %first_norm.1.a.refs_9_, bf16[1024,1536]{1,0:T(8,128)(2,1)} %bitcast.117, f32[2048,128]{1,0:T(8,128)} %get-tuple-element.168.cosine.refs_7_, f32[2048,128]{1,0:T(8,128)} %get-tuple-element.169.sine.refs_8_), custom_call_target="tpu_custom_call" | custom-call | flops 3221225472 | bytes 5242880 | tf_op jit(solution)/shard_map/project/pallas_call | solution.py:293
  108.8 5.5 %collective-permute-start.11 = (bf16[1024,1024]{1,0:T(8,128)(2,1)S(1)}, bf16[1024,1024]{1,0:T(8,128)(2,1)}, u32[]{:S(2)}, u32[]{:S(2)}) collective-permute-start(bf16[1024,1024]{1,0:T(8,128)(2,1)S(1)} %copy-done.3), channel_id=1, source_target_pairs={{1,2},{2,1},{5,6},{6,5},{9,10},{10,9},{13,14},{14,13},{17,18},{18,... | collective-permute-start | bytes 6291464 | tf_op jit(solution)/shard_map/ppermute | solution.py:53
  116.7 33.9 %attend.1 = (bf16[1024,512]{1,0:T(8,128)(2,1)}, bf16[1024,512]{1,0:T(8,128)(2,1)}, f32[2,2048,256]{2,1,0:T(8,128)}) custom-call(s32[1]{0:T(128)} %bitcast.place, s32[2,8]{1,0:T(2,128)} %pad_add_fusion.bounds, s32[2048,1]{1,0:T(8,128)} %copy.80.seg_col, s32[1,2048]{1,0:T(1,128)} %bitcast.141, bf16[1024,1536]{1,0:T(8,128)(2,1)} %project.2.refs_0_, ...), custom_call_target="tpu_custom_call" | custom-call | flops 17179869184 | bytes 12582912 | tf_op jit(solution)/shard_map/attend/pallas_call | solution.py:482
  157.5 38.8 %middle.1 = (bf16[1024,1024]{1,0:T(8,128)(2,1)}, f32[1024,1024]{1,0:T(8,128)}, bf16[1024,1024]{1,0:T(8,128)(2,1)}, bf16[1024,1024]{1,0:T(8,128)(2,1)}, bf16[1024...) custom-call(s32[1]{0:T(128)} %bitcast.place, ...), custom_call_target="tpu_custom_call" | custom-call | flops 30064771072 | bytes 31457280 | tf_op jit(solution)/shard_map/middle/pallas_call | solution.py:725
  223.1 22.4 %attend_back.4 = (bf16[2,1024,384]{2,1,0:T(8,128)(2,1)}, bf16[1024,384]{1,0:T(8,128)(2,1)}) custom-call(s32[1]{0:T(128)} %bitcast.place, s32[2,8]{1,0:T(2,128)} %pad_add_fusion.bounds, s32[2048,1]{1,0:T(8,128)} %copy.80.seg_col, s32[1,2048]{1,0:T(1,128)} %bitcast.142, bf16[1024,1536]{1,0:T(8,128)(2,1)} %project.2.refs_0_, ...), custom_call_target="tpu_custom_call" | custom-call | flops 10737418240 | bytes 4194304 | tf_op jit(solution)/shard_map/attend_back/pallas_call | solution.py:596
  249.7 7.3 %cut.3 = (bf16[4,64,2560]{2,1,0:T(8,128)(2,1)}, bf16[4,64,2560]{2,1,0:T(8,128)(2,1)}, bf16[4,64,2560]{2,1,0:T(8,128)(2,1)}, bf16[4,64,2560]{2,1,0:T(8,128)(2,1)}) custom-call(s32[2]{0:T(128)} %pad_add_fusion.3.where, bf16[4,2,2,64,1024]{4,3,2,1,0:T(8,128)(2,1)} %bitcast.125, bf16[4,2,2,64,1024]{4,3,2,1,0:T(8,128)(2,1)} %bitcast.28.refs_1_, ...), custom_call_target="tpu_custom_call" | custom-call | bytes 15728640 | tf_op jit(solution)/shard_map/cut/pallas_call | solution.py:158
  260.4 22.5 %attend_back.6 = (bf16[2,1024,384]{2,1,0:T(8,128)(2,1)}, bf16[1024,384]{1,0:T(8,128)(2,1)}) custom-call(s32[1]{0:T(128)} %bitcast.place, s32[2,8]{1,0:T(2,128)} %pad_add_fusion.bounds, s32[2048,1]{1,0:T(8,128)} %copy.80.seg_col, s32[1,2048]{1,0:T(1,128)} %bitcast.143, bf16[1024,1536]{1,0:T(8,128)(2,1)} %project.2.refs_0_, ...), custom_call_target="tpu_custom_call" | custom-call | flops 10737418240 | bytes 4194304 | tf_op jit(solution)/shard_map/attend_back/pallas_call | solution.py:596
  282.8 22.1 %attend_back.5 = (bf16[2,1024,384]{2,1,0:T(8,128)(2,1)}, bf16[1024,384]{1,0:T(8,128)(2,1)}) custom-call(s32[1]{0:T(128)} %bitcast.place, s32[2,8]{1,0:T(2,128)} %pad_add_fusion.bounds, s32[2048,1]{1,0:T(8,128)} %copy.80.seg_col, s32[1,2048]{1,0:T(1,128)} %bitcast.144, bf16[1024,1536]{1,0:T(8,128)(2,1)} %project.2.refs_0_, ...), custom_call_target="tpu_custom_call" | custom-call | flops 10737418240 | bytes 4194304 | tf_op jit(solution)/shard_map/attend_back/pallas_call | solution.py:596
  309.7 8.1 %collective-permute-done.20 = bf16[4,64,2560]{2,1,0:T(8,128)(2,1)} collective-permute-done((bf16[4,64,2560]{2,1,0:T(8,128)(2,1)}, bf16[4,64,2560]{2,1,0:T(8,128)(2,1)}, u32[]{:S(2)}, u32[]{:S(2)}) %collective-permute-start.20) | collective-permute-done | bytes 1310752 | tf_op jit(solution)/shard_map/ppermute | solution.py:178
  322.6 22.3 %attend_back.7 = (bf16[2,1024,384]{2,1,0:T(8,128)(2,1)}, bf16[1024,384]{1,0:T(8,128)(2,1)}) custom-call(s32[1]{0:T(128)} %bitcast.place, s32[2,8]{1,0:T(2,128)} %pad_add_fusion.bounds, s32[2048,1]{1,0:T(8,128)} %copy.80.seg_col, s32[1,2048]{1,0:T(1,128)} %bitcast.145, bf16[1024,1536]{1,0:T(8,128)(2,1)} %project.2.refs_0_, ...), custom_call_target="tpu_custom_call" | custom-call | flops 10737418240 | bytes 4194304 | tf_op jit(solution)/shard_map/attend_back/pallas_call | solution.py:596
  362.1 7.6 %input_part.1 = bf16[1024,1024]{1,0:T(8,128)(2,1)} custom-call(bf16[2,1024,384]{2,1,0:T(8,128)(2,1)} %get-tuple-element.262.refs_0_.refs_6_, bf16[2,1024,384]{2,1,0:T(8,128)(2,1)} %get-tuple-element.263.refs_1_.refs_7_, bf16[2,1024,384]{2,1,0:T(8,128)(2,1)} %get-tuple-element.264.refs_2_.refs_8_, bf16[2,1024,384]{2,1,0:T(8,128)(2,1)} %get-tuple-element.265.refs_3_.refs_9_, ...), custom_call_target="tpu_custom_call" | custom-call | flops 3221225472 | bytes 8388608 | tf_op jit(solution)/shard_map/input_part/pallas_call | solution.py:773
  384.2 6.6 %collective-permute-done.33 = bf16[64,1152]{1,0:T(8,128)(2,1)S(1)} collective-permute-done((bf16[64,1152]{1,0:T(8,128)(2,1)S(1)}, bf16[64,1152]{1,0:T(8,128)(2,1)S(1)}, u32[]{:S(2)}, u32[]{:S(2)}) %collective-permute-start.33) | collective-permute-done | bytes 147488 | tf_op jit(solution)/shard_map/ppermute | solution.py:71
  393.5 8.0 %last.2 = (bf16[512,1024]{1,0:T(8,128)(2,1)}, f32[8,2048]{1,0:T(8,128)}) custom-call(bf16[1024,1024]{1,0:T(8,128)(2,1)} %broadcast_select_fusion.2.x.refs_0_, bf16[1024,32]{1,0:T(8,128)(2,1)} %copy.81.member.refs_1_, bf16[16,1024]{1,0:T(8,128)(2,1)} %pad.18.refs_2_, f32[8,6144]{1,0:T(8,128)} %pad.15.adaptive.refs_3_, ...), custom_call_target="tpu_custom_call" | custom-call | flops 1610612736 | bytes 6291456 | tf_op jit(solution)/shard_map/last/pallas_call | solution.py:823
  404.7 8.1 %last.3 = (bf16[512,1024]{1,0:T(8,128)(2,1)}, f32[8,2048]{1,0:T(8,128)}) custom-call(bf16[1024,1024]{1,0:T(8,128)(2,1)} %broadcast_select_fusion.2.x.refs_0_, bf16[1024,32]{1,0:T(8,128)(2,1)} %copy.81.member.refs_1_, bf16[16,1024]{1,0:T(8,128)(2,1)} %pad.18.refs_2_, f32[8,6144]{1,0:T(8,128)} %pad.15.adaptive.refs_3_, ...), custom_call_target="tpu_custom_call" | custom-call | flops 1610612736 | bytes 6291456 | tf_op jit(solution)/shard_map/last/pallas_call | solution.py:823
  412.8 5.2 %collective-permute-done.36 = bf16[512,1024]{1,0:T(8,128)(2,1)} collective-permute-done((bf16[512,1024]{1,0:T(8,128)(2,1)}, bf16[512,1024]{1,0:T(8,128)(2,1)}, u32[]{:S(2)}, u32[]{:S(2)}) %collective-permute-start.36) | collective-permute-done | bytes 1048608 | tf_op jit(solution)/shard_map/ppermute | solution.py:53
  429.9 8.5 %all-to-all-done.1 = f32[32,4,192]{2,1,0:T(4,128)S(1)} async-done(((f32[32,4,192]{2,1,0:T(4,128)}), f32[32,4,192]{2,1,0:T(4,128)S(1)}, u32[]{:S(2)}, u32[]{:S(2)}) %all-to-all-start.1) | async-done | bytes 98336 | tf_op jit(solution)/shard_map/all_to_all | solution.py:1024
  (254 shorter events, 140.3 us)
Async XLA Ops:
  15.2 32.5 %collective-permute-start.5 = (bf16[1024,1024]{1,0:T(8,128)(2,1)}, bf16[1024,1024]{1,0:T(8,128)(2,1)}, u32[]{:S(2)}, u32[]{:S(2)}) collective-permute-start(bf16[1024,1024]{1,0:T(8,128)(2,1)} %param.10), channel_id=1, source_target_pairs={{1,2},{2,1},{5,6},{6,5},{9,10},{10,9},{13,14},{14,13},{17,18},{18,... | collective-permute-start | bytes 6291464 | tf_op jit(solution)/shard_map/ppermute | solution.py:53
  22.7 23.2 %collective-permute-start.2 = (bf16[64,1536]{1,0:T(8,128)(2,1)S(1)}, bf16[64,1536]{1,0:T(8,128)(2,1)S(1)}, u32[]{:S(2)}, u32[]{:S(2)}) collective-permute-start(bf16[64,1536]{1,0:T(8,128)(2,1)S(1)} %broadcast_select_fusion.6), channel_id=1, source_target_pairs={{0,8},{8,0},{16,24},{24,16},{1,9},{9,1},{17,25},{25,17},{2,10},{10... | collective-permute-start | bytes 589832 | tf_op jit(solution)/shard_map/ppermute | solution.py:71
  24.0 21.8 %collective-permute-start.3 = (bf16[64,1536]{1,0:T(8,128)(2,1)S(1)}, bf16[64,1536]{1,0:T(8,128)(2,1)S(1)}, u32[]{:S(2)}, u32[]{:S(2)}) collective-permute-start(bf16[64,1536]{1,0:T(8,128)(2,1)S(1)} %broadcast_select_fusion.6), channel_id=1, source_target_pairs={{0,16},{8,24},{16,0},{24,8},{1,17},{9,25},{17,1},{25,9},{2,18},{10... | collective-permute-start | bytes 589832 | tf_op jit(solution)/shard_map/ppermute | solution.py:71
  26.4 19.5 %collective-permute-start.4 = (bf16[64,1536]{1,0:T(8,128)(2,1)S(1)}, bf16[64,1536]{1,0:T(8,128)(2,1)S(1)}, u32[]{:S(2)}, u32[]{:S(2)}) collective-permute-start(bf16[64,1536]{1,0:T(8,128)(2,1)S(1)} %broadcast_select_fusion.6), channel_id=1, source_target_pairs={{0,24},{8,16},{16,8},{24,0},{1,25},{9,17},{17,9},{25,1},{2,26},{10... | collective-permute-start | bytes 589832 | tf_op jit(solution)/shard_map/ppermute | solution.py:71
  27.1 17.9 %all-to-all-start = ((f32[32,4,192]{2,1,0:T(4,128)}), f32[32,4,192]{2,1,0:T(4,128)S(1)}, u32[]{:S(2)}, u32[]{:S(2)}) async-start(f32[32,4,192]{2,1,0:T(4,128)} %bitcast.6), calls=%async_computation | async-start | bytes 262144 | tf_op jit(solution)/shard_map/all_to_all | solution.py:888
  32.4 124.1 %all-gather.2.cloned.1.call-start = ((), (), s32[]{:S(2)}) async-start(), calls=%async_computation.2 | async-start | bytes 10813440 | tf_op jit(solution)/shard_map/all_gather | solution.py:928
  51.2 21.5 %collective-permute-start.6 = (bf16[4,64,1536]{2,1,0:T(8,128)(2,1)S(1)}, bf16[4,64,1536]{2,1,0:T(8,128)(2,1)S(1)}, u32[]{:S(2)}, u32[]{:S(2)}) collective-permute-start(bf16[4,64,1536]{2,1,0:T(8,128)(2,1)S(1)} %pad_maximum_fusion.own), channel_id=1, source_target_pairs={{0,4},{4,0},{1,5},{5,1},{2,6},{6,2},{3,7},{7,3},{8,12},{12,8},{9,1... | collective-permute-start | bytes 2359304 | tf_op jit(solution)/shard_map/ppermute | solution.py:95
  51.9 21.3 %collective-permute-start.7 = (bf16[4,64,1536]{2,1,0:T(8,128)(2,1)S(1)}, bf16[4,64,1536]{2,1,0:T(8,128)(2,1)S(1)}, u32[]{:S(2)}, u32[]{:S(2)}) collective-permute-start(bf16[4,64,1536]{2,1,0:T(8,128)(2,1)S(1)} %pad_maximum_fusion.own), channel_id=1, source_target_pairs={{0,1},{1,0},{2,3},{3,2},{4,5},{5,4},{6,7},{7,6},{8,9},{9,8},{10,11... | collective-permute-start | bytes 2359304 | tf_op jit(solution)/shard_map/ppermute | solution.py:95
  108.8 41.8 %collective-permute-start.11 = (bf16[1024,1024]{1,0:T(8,128)(2,1)S(1)}, bf16[1024,1024]{1,0:T(8,128)(2,1)}, u32[]{:S(2)}, u32[]{:S(2)}) collective-permute-start(bf16[1024,1024]{1,0:T(8,128)(2,1)S(1)} %copy-done.3), channel_id=1, source_target_pairs={{1,2},{2,1},{5,6},{6,5},{9,10},{10,9},{13,14},{14,13},{17,18},{18,... | collective-permute-start | bytes 6291464 | tf_op jit(solution)/shard_map/ppermute | solution.py:53
  196.3 49.2 %collective-permute-start.17 = (bf16[1024,1024]{1,0:T(8,128)(2,1)}, bf16[1024,1024]{1,0:T(8,128)(2,1)}, u32[]{:S(2)}, u32[]{:S(2)}) collective-permute-start(bf16[1024,1024]{1,0:T(8,128)(2,1)} %get-tuple-element.194), channel_id=1, source_target_pairs={{1,2},{2,1},{5,6},{6,5},{9,10},{10,9},{13,14},{14,13},{17,18},{18,... | collective-permute-start | bytes 6291464 | tf_op jit(solution)/shard_map/ppermute | solution.py:53
  199.6 22.6 %collective-permute-start.16 = (bf16[1024,512]{1,0:T(8,128)(2,1)}, bf16[1024,512]{1,0:T(8,128)(2,1)S(1)}, u32[]{:S(2)}, u32[]{:S(2)}) collective-permute-start(bf16[1024,512]{1,0:T(8,128)(2,1)} %get-tuple-element.190), channel_id=1, source_target_pairs={{2,0},{0,2},{3,1},{1,3},{6,4},{4,6},{7,5},{5,7},{10,8},{8,10},{11,... | collective-permute-start | bytes 3145736 | tf_op jit(solution)/shard_map/ppermute | solution.py:58
  206.0 42.7 %collective-permute-start.15 = (bf16[1024,512]{1,0:T(8,128)(2,1)}, bf16[1024,512]{1,0:T(8,128)(2,1)S(1)}, u32[]{:S(2)}, u32[]{:S(2)}) collective-permute-start(bf16[1024,512]{1,0:T(8,128)(2,1)} %convolution_convert_fusion.4), channel_id=1, source_target_pairs={{0,2},{2,0},{1,3},{3,1},{4,6},{6,4},{5,7},{7,5},{8,10},{10,8},{9,1... | collective-permute-start | bytes 3145736 | tf_op jit(solution)/shard_map/ppermute | solution.py:63
  210.3 38.4 %collective-permute-start.14 = (bf16[1024,1024]{1,0:T(8,128)(2,1)}, bf16[1024,1024]{1,0:T(8,128)(2,1)}, u32[]{:S(2)}, u32[]{:S(2)}) collective-permute-start(bf16[1024,1024]{1,0:T(8,128)(2,1)} %convolution_convert_fusion), channel_id=1, source_target_pairs={{0,2},{2,0},{1,3},{3,1},{4,6},{6,4},{5,7},{7,5},{8,10},{10,8},{9,1... | collective-permute-start | bytes 6291464 | tf_op jit(solution)/shard_map/ppermute | solution.py:63
  214.1 34.6 %collective-permute-start.13 = (bf16[1024,1024]{1,0:T(8,128)(2,1)}, bf16[1024,1024]{1,0:T(8,128)(2,1)}, u32[]{:S(2)}, u32[]{:S(2)}) collective-permute-start(bf16[1024,1024]{1,0:T(8,128)(2,1)} %convolution_convert_fusion.2), channel_id=1, source_target_pairs={{0,2},{2,0},{1,3},{3,1},{4,6},{6,4},{5,7},{7,5},{8,10},{10,8},{9,1... | collective-permute-start | bytes 6291464 | tf_op jit(solution)/shard_map/ppermute | solution.py:63
  257.0 52.7 %collective-permute-start.18 = (bf16[4,64,2560]{2,1,0:T(8,128)(2,1)}, bf16[4,64,2560]{2,1,0:T(8,128)(2,1)S(1)}, u32[]{:S(2)}, u32[]{:S(2)}) collective-permute-start(bf16[4,64,2560]{2,1,0:T(8,128)(2,1)} %get-tuple-element.207), channel_id=1, source_target_pairs={{0,4},{4,0},{1,5},{5,1},{2,6},{6,2},{3,7},{7,3},{8,12},{12,8},{9,1... | collective-permute-start | bytes 3932168 | tf_op jit(solution)/shard_map/ppermute | solution.py:180
  259.1 50.6 %collective-permute-start.19 = (bf16[4,64,2560]{2,1,0:T(8,128)(2,1)}, bf16[4,64,2560]{2,1,0:T(8,128)(2,1)S(1)}, u32[]{:S(2)}, u32[]{:S(2)}) collective-permute-start(bf16[4,64,2560]{2,1,0:T(8,128)(2,1)} %get-tuple-element.208), channel_id=1, source_target_pairs={{0,1},{1,0},{2,3},{3,2},{4,5},{5,4},{6,7},{7,6},{8,9},{9,8},{10,11... | collective-permute-start | bytes 3932168 | tf_op jit(solution)/shard_map/ppermute | solution.py:179
  259.1 58.7 %collective-permute-start.20 = (bf16[4,64,2560]{2,1,0:T(8,128)(2,1)}, bf16[4,64,2560]{2,1,0:T(8,128)(2,1)}, u32[]{:S(2)}, u32[]{:S(2)}) collective-permute-start(bf16[4,64,2560]{2,1,0:T(8,128)(2,1)} %get-tuple-element.209), channel_id=1, source_target_pairs={{0,5},{1,4},{4,1},{5,0},{2,7},{3,6},{6,3},{7,2},{8,13},{9,12},{12,... | collective-permute-start | bytes 3932168 | tf_op jit(solution)/shard_map/ppermute | solution.py:178
  319.8 28.5 %collective-permute-start.21 = (bf16[2,64,2560]{2,1,0:T(8,128)(2,1)S(1)}, bf16[2,64,2560]{2,1,0:T(8,128)(2,1)S(1)}, u32[]{:S(2)}, u32[]{:S(2)}) collective-permute-start(bf16[2,64,2560]{2,1,0:T(8,128)(2,1)S(1)} %get-tuple-element.227), channel_id=1, source_target_pairs={{0,8},{8,0},{16,24},{24,16},{1,9},{9,1},{17,25},{25,17},{2,10},{10... | collective-permute-start | bytes 1966088 | tf_op jit(solution)/shard_map/ppermute | solution.py:71
  319.9 25.1 %collective-permute-start.22 = (bf16[4,64,1152]{2,1,0:T(8,128)(2,1)}, bf16[4,64,1152]{2,1,0:T(8,128)(2,1)S(1)}, u32[]{:S(2)}, u32[]{:S(2)}) collective-permute-start(bf16[4,64,1152]{2,1,0:T(8,128)(2,1)} %get-tuple-element.229), channel_id=1, source_target_pairs={{0,4},{4,0},{1,5},{5,1},{2,6},{6,2},{3,7},{7,3},{8,12},{12,8},{9,1... | collective-permute-start | bytes 1769480 | tf_op jit(solution)/shard_map/ppermute | solution.py:180
  321.3 23.7 %collective-permute-start.23 = (bf16[4,64,1152]{2,1,0:T(8,128)(2,1)}, bf16[4,64,1152]{2,1,0:T(8,128)(2,1)S(1)}, u32[]{:S(2)}, u32[]{:S(2)}) collective-permute-start(bf16[4,64,1152]{2,1,0:T(8,128)(2,1)} %get-tuple-element.230), channel_id=1, source_target_pairs={{0,1},{1,0},{2,3},{3,2},{4,5},{5,4},{6,7},{7,6},{8,9},{9,8},{10,11... | collective-permute-start | bytes 1769480 | tf_op jit(solution)/shard_map/ppermute | solution.py:179
  321.6 26.7 %collective-permute-start.24 = (bf16[4,64,1152]{2,1,0:T(8,128)(2,1)}, bf16[4,64,1152]{2,1,0:T(8,128)(2,1)}, u32[]{:S(2)}, u32[]{:S(2)}) collective-permute-start(bf16[4,64,1152]{2,1,0:T(8,128)(2,1)} %get-tuple-element.231), channel_id=1, source_target_pairs={{0,5},{1,4},{4,1},{5,0},{2,7},{3,6},{6,3},{7,2},{8,13},{9,12},{12,... | collective-permute-start | bytes 1769480 | tf_op jit(solution)/shard_map/ppermute | solution.py:178
  353.9 17.7 %collective-permute-start.29 = (bf16[64,2560]{1,0:T(8,128)(2,1)S(1)}, bf16[64,2560]{1,0:T(8,128)(2,1)S(1)}, u32[]{:S(2)}, u32[]{:S(2)}) collective-permute-start(bf16[64,2560]{1,0:T(8,128)(2,1)S(1)} %dynamic-slice_bitcast_fusion.2), channel_id=1, source_target_pairs={{0,16},{8,24},{16,0},{24,8},{1,17},{9,25},{17,1},{25,9},{2,18},{10... | collective-permute-start | bytes 983048 | tf_op jit(solution)/shard_map/ppermute | solution.py:71
  372.5 18.4 %collective-permute-start.34 = (bf16[1024,1024]{1,0:T(8,128)(2,1)}, bf16[1024,1024]{1,0:T(8,128)(2,1)S(1)}, u32[]{:S(2)}, u32[]{:S(2)}) collective-permute-start(bf16[1024,1024]{1,0:T(8,128)(2,1)} %input_part.1), channel_id=1, source_target_pairs={{0,2},{2,0},{1,3},{3,1},{4,6},{6,4},{5,7},{7,5},{8,10},{10,8},{9,1... | collective-permute-start | bytes 6291464 | tf_op jit(solution)/shard_map/ppermute | solution.py:63
  420.3 20.6 %collective-permute-start.37 = (bf16[512,1024]{1,0:T(8,128)(2,1)S(1)}, bf16[512,1024]{1,0:T(8,128)(2,1)}, u32[]{:S(2)}, u32[]{:S(2)}) collective-permute-start(bf16[512,1024]{1,0:T(8,128)(2,1)S(1)} %copy-done.8), channel_id=1, source_target_pairs={{1,2},{2,1},{5,6},{6,5},{9,10},{10,9},{13,14},{14,13},{17,18},{18,... | collective-permute-start | bytes 3145736 | tf_op jit(solution)/shard_map/ppermute | solution.py:53
  (61 other events, 542.9 us)
Sparse Core Ops, SparseCore 0:
  51.3 97.6 all-gather.1

commit v4 on v3

--- a/solution.py
+++ b/solution.py
@@ -48,9 +48,16 @@
     return pl.BlockSpec(shape, lambda *_: zeros, pipeline_mode=pl.Buffered(buffers))
 
 
+def sent(value):
+    return lax.ppermute(value, ("core", "hh"), [(1, 2), (2, 1)])
+
+
+def staying():
+    return lax.axis_index("core") == lax.axis_index("hh")
+
+
 def moved(value):
-    stays = lax.axis_index("core") == lax.axis_index("hh")
-    return jnp.where(stays, value, lax.ppermute(value, ("core", "hh"), [(1, 2), (2, 1)]))
+    return jnp.where(staying(), value, sent(value))
 
 
 def from_sub(value, step):
@@ -69,22 +76,6 @@
 def across(value, bit):
     size = lax.axis_size("za")
     return lax.ppermute(value, "za", [(i, i ^ bit) for i in range(size)])
-
-
-def place_kernel(half, where, own, by_zb, by_hh, both_low, both_high, out):
-    zb = where[0]
-    hh = where[1]
-    out[0, zb, hh] = own[0]
-    out[0, 1 - zb, hh] = by_zb[0]
-    out[0, zb, 1 - hh] = by_hh[0]
-
-    @pl.when(pl.program_id(0) < half)
-    def _():
-        out[0, 1 - zb, 1 - hh] = both_low[0]
-
-    @pl.when(pl.program_id(0) >= half)
-    def _():
-        out[0, 1 - zb, 1 - hh] = both_high[0]
 
 
 def gather_line(shard):
@@ -100,33 +91,6 @@
     both_low = lax.ppermute(by_zb[:half], "hh", SWAP)
     both_high = lax.ppermute(by_hh[half:], "zb", SWAP)
     return held, by_zb, by_hh, both_low, both_high
-
-
-def gathered(held, by_zb, by_hh, both_low, both_high):
-    size, rows, columns = held.shape
-    half = size // 2
-    where = [lax.axis_index("zb"), lax.axis_index("hh")]
-    where += [lax.axis_index("za") ^ bits for bits in range(size)]
-    where = jnp.stack(where).astype(jnp.int32)
-    block = (1, rows, columns)
-    full = pl.pallas_call(
-        functools.partial(place_kernel, half),
-        grid_spec=pltpu.PrefetchScalarGridSpec(
-            num_scalar_prefetch=1,
-            grid=(size,),
-            in_specs=[pl.BlockSpec(block, lambda i, w: (i, 0, 0))] * 3
-            + [
-                pl.BlockSpec(block, lambda i, w: (jnp.minimum(i, half - 1), 0, 0)),
-                pl.BlockSpec(block, lambda i, w: (jnp.maximum(i - half, 0), 0, 0)),
-            ],
-            out_specs=pl.BlockSpec((1, 2, 2, rows, columns), lambda i, w: (w[2 + i], 0, 0, 0, 0)),
-        ),
-        out_shape=jax.ShapeDtypeStruct((size, 2, 2, rows, columns), held.dtype),
-        compiler_params=params(),
-        cost_estimate=cost(0, size * 4 * rows * columns * 4),
-        name="place",
-    )(where, held, by_zb, by_hh, both_low, both_high)
-    return full.reshape(size * 4 * rows, columns)
 
 
 FOUR = ((0, 0), (1, 0), (0, 1), (1, 1))
@@ -203,7 +167,7 @@
     apart = lax.axis_size("za") // count
     mine = lax.axis_index("za") // apart
     cuts = [lax.dynamic_index_in_dim(total, mine ^ n, 0, keepdims=False) for n in range(count)]
-    return add_up([cuts[0]] + [across(cut, n * apart) for n, cut in enumerate(cuts) if n])
+    return [cuts[0]] + [across(cut, n * apart) for n, cut in enumerate(cuts) if n]
 
 
 def together(*values):
@@ -231,31 +195,35 @@
     return (dot(member_flip, high) + dot(member_flip, low))[0:8]
 
 
-def first_norm_kernel(x, member, adaptive, out):
+def first_norm_kernel(stays, there, here, member, adaptive, out, x):
     width = x.shape[1]
+    x[...] = jnp.where(stays[0] == 1, there[...], here[...])
     normed, _ = norm(x[...].astype(F32))
     shift = pick(member[...], adaptive[:, :width])
     scale = pick(member[...], adaptive[:, width : 2 * width])
     out[...] = (normed * (1.0 + scale) + shift).astype(BF16)
 
 
-def first_norm(x, member, adaptive):
-    rows, width = x.shape
+def first_norm(stays, there, here, member, adaptive):
+    rows, width = here.shape
     tile = min(256, rows)
+    tiled = pl.BlockSpec((tile, width), lambda i: (i, 0))
     return pl.pallas_call(
         first_norm_kernel,
         grid=(rows // tile,),
-        out_shape=jax.ShapeDtypeStruct((rows, width), BF16),
+        out_shape=[jax.ShapeDtypeStruct((rows, width), BF16)] * 2,
         in_specs=[
-            pl.BlockSpec((tile, width), lambda i: (i, 0)),
+            pl.BlockSpec(memory_space=pltpu.SMEM),
+            tiled,
+            tiled,
             pl.BlockSpec((tile, 32), lambda i: (i, 0)),
             whole(adaptive.shape),
         ],
-        out_specs=pl.BlockSpec((tile, width), lambda i: (i, 0)),
+        out_specs=[tiled, tiled],
         compiler_params=params(),
-        cost_estimate=cost(rows * width * 40, rows * width * 4),
+        cost_estimate=cost(rows * width * 40, rows * width * 8),
         name="first_norm",
-    )(x, member, adaptive)
+    )(stays, there, here, member, adaptive)
 
 
 def turn(values, cosine, sine):
@@ -272,9 +240,33 @@
     return parts[0] if len(parts) == 1 else jnp.concatenate(parts, axis=1)
 
 
-def project_kernel(lanes, place, a, w, cosine, sine, out):
-    for start in range(0, w.shape[1], 3 * lanes):
-        products = dot(a[...], w[:, start : start + 3 * lanes])
+def project_kernel(pieces, tiles, lanes, where, *refs):
+    a_refs, refs = refs[:pieces], refs[pieces:]
+    own, by_zb, by_hh, both_low, both_high, cosine, sine, out, w, a, weights = refs
+    size, rows, columns = own.shape
+    i = pl.program_id(0)
+
+    @pl.when(i == 0)
+    def _():
+        zb, hh = where[0], where[1]
+        for n in range(size):
+            z = where[2 + n]
+            low = n < size // 2
+            both = both_low[n] if low else both_high[n - size // 2]
+            shards = ((zb, hh, own[n]), (1 - zb, hh, by_zb[n]), (zb, 1 - hh, by_hh[n]))
+            for at_zb, at_hh, shard in shards + ((1 - zb, 1 - hh, both),):
+                start = pl.multiple_of(((z * 2 + at_zb) * 2 + at_hh) * rows, rows)
+                weights[pl.ds(start, rows), :] = shard
+        w[...] = weights[...]
+
+    for piece in range(pieces):
+
+        @pl.when(i // tiles == piece)
+        def _(piece=piece):
+            a[...] = a_refs[piece][...]
+
+    for start in range(0, columns, 3 * lanes):
+        products = dot(a[...], weights[:, start : start + 3 * lanes])
         for at in range(0, 3 * lanes, 128):
             product = products[:, at : at + 128]
             kind = at // 128 % 3
@@ -285,29 +277,49 @@
             out[:, start + at : start + at + 128] = product.astype(BF16)
 
 
-def project(place, a, w, cosine, sine, lanes):
-    rows, width = a.shape
-    columns = w.shape[1]
+def project(place, a_all, shards, cosine, sine, lanes):
+    pieces = len(a_all)
+    rows, width = a_all[0].shape
+    size, own_rows, columns = shards[0].shape
     tile = min(256, rows)
     tiles = rows // tile
+    where = [lax.axis_index("zb"), lax.axis_index("hh")]
+    where += [lax.axis_index("za") ^ bits for bits in range(size)]
+    where += [(place + piece) % pieces for piece in range(pieces)]
+    where = jnp.stack(where).astype(jnp.int32)
+
+    def rows_of(piece):
+        return pl.BlockSpec(
+            (tile, width), lambda i, w: (jnp.clip(i - piece * tiles, 0, tiles - 1), 0)
+        )
+
+    def tables():
+        return pl.BlockSpec(
+            (tile, 128), lambda i, w: (w[2 + size + i // tiles] * tiles + lax.rem(i, tiles), 0)
+        )
+
     return pl.pallas_call(
-        functools.partial(project_kernel, lanes),
+        functools.partial(project_kernel, pieces, tiles, lanes),
         grid_spec=pltpu.PrefetchScalarGridSpec(
             num_scalar_prefetch=1,
-            grid=(tiles,),
-            in_specs=[
-                pl.BlockSpec((tile, width), lambda i, s: (i, 0)),
-                whole(w.shape, 1),
-                pl.BlockSpec((tile, 128), lambda i, s: (s[0] * tiles + i, 0)),
-                pl.BlockSpec((tile, 128), lambda i, s: (s[0] * tiles + i, 0)),
+            grid=(pieces * tiles,),
+            in_specs=[rows_of(piece) for piece in range(pieces)]
+            + [whole(shard.shape, 1) for shard in shards]
+            + [tables(), tables()],
+            out_specs=[
+                pl.BlockSpec((None, tile, columns), lambda i, w: (i // tiles, lax.rem(i, tiles), 0)),
+                whole((width, columns), 1),
             ],
-            out_specs=pl.BlockSpec((tile, columns), lambda i, s: (i, 0)),
+            scratch_shapes=[pltpu.VMEM((tile, width), BF16), pltpu.VMEM((width, columns), BF16)],
         ),
-        out_shape=jax.ShapeDtypeStruct((rows, columns), BF16),
+        out_shape=[
+            jax.ShapeDtypeStruct((pieces, rows, columns), BF16),
+            jax.ShapeDtypeStruct((width, columns), BF16),
+        ],
         compiler_params=params(),
-        cost_estimate=cost(2 * rows * width * columns, rows * (width + columns) * 2),
+        cost_estimate=cost(2 * pieces * rows * width * columns, pieces * rows * (width + columns) * 2),
         name="project",
-    )(place, a, w, cosine, sine)
+    )(where, *a_all, *shards, cosine, sine)
 
 
 def stack_heads(values, heads):
@@ -471,12 +483,14 @@
 
 
 def attend(place, bounds, seg_col, seg_row, qkv, lanes, step):
-    pieces = len(qkv)
-    rows, columns = qkv[0].shape
+    pieces, rows, columns = qkv.shape
     groups = columns // (3 * lanes)
     heads = lanes // HEAD_DIM
     frames = rows * pieces
-    specs = [pl.BlockSpec((rows, 3 * lanes), lambda g: (0, g))] * pieces
+    specs = [
+        pl.BlockSpec((None, rows, 3 * lanes), lambda g, piece=piece: (piece, 0, g))
+        for piece in range(pieces)
+    ]
     smem = pl.BlockSpec(memory_space=pltpu.SMEM)
     area = frames * frames // 2 * heads * groups
     results = pl.pallas_call(
@@ -497,7 +511,7 @@
         compiler_params=params(),
         cost_estimate=cost(area * 4 * 256, frames * columns * 4, area),
         name="attend",
-    )(place, bounds, seg_col, seg_row, *qkv)
+    )(place, bounds, seg_col, seg_row, *[qkv] * pieces)
     return results[:pieces], results[pieces]
 
 
@@ -571,26 +585,33 @@
         span = pl.ds(piece_start(place, piece, pieces, rows), rows)
         cos = cosine[span, :]
         sin = -sine[span, :]
-        out[piece, :, 0:lanes] = turn(dq_all[span, :], cos, sin).astype(BF16)
-        out[piece, :, lanes : 2 * lanes] = turn(dk_all[span, :], cos, sin).astype(BF16)
-        out[piece, :, 2 * lanes : 3 * lanes] = dv_all[span, :].astype(BF16)
+        slopes_here = (
+            turn(dq_all[span, :], cos, sin), turn(dk_all[span, :], cos, sin), dv_all[span, :]
+        )
+        for kind, slope in enumerate(slopes_here):
+            for at in range(0, lanes, 128):
+                start = 3 * at + kind * 128
+                out[piece, :, start : start + 128] = slope[:, at : at + 128].astype(BF16)
     grad_w[...] = sum(dot(normed[p][...], out[p], TN) for p in range(pieces)).astype(BF16)
 
 
 def attend_back(
-    place, bounds, seg_col, seg_row, qkv, attended, grads, lse, cosine, sine, normed, pair, step
+    place, bounds, seg_col, seg_row, qkv, attended, grads, lse, cosine, sine, normed, first, count, step
 ):
-    pieces = len(qkv)
-    rows = qkv[0].shape[0]
-    lanes, heads = 128, 128 // HEAD_DIM
+    pieces, rows, _ = qkv.shape
+    lanes = 128 * count
+    heads = lanes // HEAD_DIM
+    block = first // count
     width = normed[0].shape[1]
-    per_group = attended[0].shape[1] // lanes // lse.shape[0]
+    per_group = lse.shape[2] // lanes
     frames = rows * pieces
     specs, arrays = [], []
     for piece in range(pieces):
-        specs.append(pl.BlockSpec((rows, 3 * lanes), lambda i: (0, pair)))
-        specs += [pl.BlockSpec((rows, lanes), lambda i: (0, pair))] * 2
-        arrays += [qkv[piece], attended[piece], grads[piece]]
+        specs.append(
+            pl.BlockSpec((None, rows, 3 * lanes), lambda i, piece=piece: (piece, 0, block), pipeline_mode=pl.Buffered(1))
+        )
+        specs += [pl.BlockSpec((rows, lanes), lambda i: (0, block), pipeline_mode=pl.Buffered(1))] * 2
+        arrays += [qkv, attended[piece], grads[piece]]
     smem = pl.BlockSpec(memory_space=pltpu.SMEM)
     area = frames * frames // 2 * heads
     return pl.pallas_call(
@@ -604,8 +625,8 @@
         + specs
         + [
             pl.BlockSpec(
-                (1, frames, 128),
-                lambda i: (pair // per_group, 0, pair % per_group),
+                (1, frames, lanes),
+                lambda i: (block // per_group, 0, block % per_group),
                 pipeline_mode=pl.Buffered(1),
             ),
         ]
@@ -639,8 +660,8 @@
 
 
 def middle_kernel(pieces, place, *refs):
-    x, member, member_flip, adaptive, dy = refs[:5]
-    refs = refs[5:]
+    x, member, member_flip, adaptive, dy, dy_moved = refs[:6]
+    refs = refs[6:]
     attended, refs = refs[:pieces], refs[pieces:]
     w_out, refs = refs[:pieces], refs[pieces:]
     w_up, refs = refs[:pieces], refs[pieces:]
@@ -669,7 +690,7 @@
         slopes.append(slope)
         branch2 = branch2 + dot(value, flat(w_down[p]), NT)
     mixed[...] = (x2 + gate2 * branch2).astype(BF16)
-    upstream = dy[...].astype(F32)
+    upstream = jnp.where(place[1] == 1, dy[...], dy_moved[...]).astype(F32)
     d2 = (upstream * gate2).astype(BF16)
     d2_out[...] = d2
     da2 = jnp.zeros_like(x2)
@@ -695,7 +716,7 @@
         dadaptive[:, n * width : (n + 1) * width] += gather(member_flip[...], term)
 
 
-def middle(place, x, member, member_flip, adaptive, dy, attended, weights):
+def middle(place, x, member, member_flip, adaptive, dy, dy_moved, attended, weights):
     pieces = len(attended)
     rows, width = x.shape
     head_columns = attended[0].shape[1]
@@ -732,6 +753,7 @@
             tiled(32),
             pl.BlockSpec((16, tile), lambda i, s: (0, i)),
             whole(adaptive.shape, 1),
+            tiled(width),
             tiled(width),
         ]
         + [tiled(head_columns)] * pieces
@@ -754,7 +776,7 @@
         compiler_params=params(),
         cost_estimate=cost(work, rows * width * 30, rows * hidden * pieces),
         name="middle",
-    )(place, x, member, member_flip, adaptive, dy, *attended, *[weights] * (3 * pieces))
+    )(place, x, member, member_flip, adaptive, dy, dy_moved, *attended, *[weights] * (3 * pieces))
     head, rest = results[:6], results[6:]
     return head, rest[:pieces], rest[pieces : 2 * pieces], rest[2 * pieces :]
 
@@ -766,19 +788,19 @@
 
 
 def input_part(slopes, weights, piece):
-    rows, columns = slopes[0].shape[1:]
-    width = weights.shape[0]
+    rows = slopes[0].shape[1]
+    width, columns = weights.shape
     tile = min(256, rows)
     groups = len(slopes)
     return pl.pallas_call(
         functools.partial(part_kernel, groups),
         grid=(rows // tile,),
-        in_specs=[pl.BlockSpec((None, tile, columns), lambda i: (piece, i, 0))] * groups
+        in_specs=[pl.BlockSpec((None, tile, s.shape[2]), lambda i: (piece, i, 0)) for s in slopes]
         + [whole(weights.shape, 1)],
         out_shape=jax.ShapeDtypeStruct((rows, width), BF16),
         out_specs=pl.BlockSpec((tile, width), lambda i: (i, 0)),
         compiler_params=params(),
-        cost_estimate=cost(2 * rows * width * columns * groups, rows * width * 8),
+        cost_estimate=cost(2 * rows * width * columns, rows * width * 8),
         name="input_part",
     )(*slopes, weights)
 
@@ -919,7 +941,8 @@
     member_flip = jnp.pad(member.T, ((0, 8), (0, 0)))
     member = jnp.concatenate([member, member, member, jnp.zeros_like(member)], axis=1)
 
-    x = moved(frames)
+    x = sent(frames)
+    stays = staying().astype(jnp.int32)
     held = gather_line(qkv_shard)
     held, adaptive, x, cosine, sine, member, mlp_shard = together(
         held, adaptive, x, cosine, sine, member, mlp_shard
@@ -927,18 +950,13 @@
     near = gather_near(held)
     mlp_full = lax.all_gather(mlp_shard, ALL, axis=0, tiled=True)
     mlp_full = mlp_full.reshape(-1, pieces, own_rows, mlp_shard.shape[1])
-    a1 = first_norm(x, member, adaptive)
+    a1, x = first_norm(stays.reshape(1), frames, x, member, adaptive)
     near, a1, grad_out = together(near, a1, grad_out)
     far, a1_all = together(gather_far(*near), around(a1))
-    qkv_full = gathered(*far)
-    places = [((place + piece) % pieces).reshape(1) for piece in range(pieces)]
-    qkv = [
-        project(places[piece], a1_all[piece], qkv_full, cosine, sine, lanes)
-        for piece in range(pieces)
-    ]
+    qkv, qkv_full = project(place, a1_all, far, cosine, sine, lanes)
     at_place = place.reshape(1)
     qkv, grad_out = together(qkv, grad_out)
-    dy = moved(grad_out)
+    dy = sent(grad_out)
     attended, lse = attend(at_place, bounds, seg_col, seg_row, qkv, lanes, step)
     attended, lse, dy = together(attended, lse, dy)
     attended_own = [attended[0]] + [
@@ -946,13 +964,13 @@
     ]
 
     head, active, dhidden, dattended = middle(
-        at_place, x, member, member_flip, adaptive, dy, attended_own, mlp_full
+        jnp.stack([place, stays]), x, member, member_flip, adaptive, grad_out, dy, attended_own, mlp_full
     )
     mixed, dx2, a2, d2, d1, dada_late = head
     grads_attended = [dattended[0]] + [
         from_sub_piece(dattended, step_) for step_ in range(1, pieces)
     ]
-    mixed_back = moved(mixed)
+    mixed_back = sent(mixed)
 
     def summed(left, right):
         parts = [dot(left, part, TN).astype(BF16) for part in right]
@@ -960,34 +978,35 @@
 
     late = [summed(a2, dhidden), summed(d2, active), summed(d1, attended_own)]
 
-    def back(pair, qkv):
+    def back(first, count, qkv):
         return attend_back(
             at_place, bounds, seg_col, seg_row, qkv, attended, grads_attended, lse, cosine, sine,
-            a1_all, pair, step,
+            a1_all, first, count, step,
         )
 
     slopes, grads_qkv = [], []
     early = final = None
 
-    def next_pair():
-        slope, grad = back(len(slopes), qkv)
+    def next_pairs(first, count):
+        slope, grad = back(first, count, qkv)
         slopes.append(slope)
         grads_qkv.append(grad)
 
-    next_pair()
-    late, slopes, grads_qkv, mixed_back = together(late, slopes, grads_qkv, mixed_back)
+    late, grads_attended = together(late, grads_attended)
     late, qkv = together(cut_plane(late), qkv)
     late = swap_plane(late)
-    while len(slopes) < pairs - 1:
-        next_pair()
+    for pair in range(max(pairs - 1, 1)):
+        next_pairs(pair, 1)
     if pairs > 1:
         early = cut_plane([[grad] for grad in grads_qkv])
-    late, early, slopes, grads_qkv = together(late, early, slopes, grads_qkv)
+    late, early, slopes, grads_qkv, mixed_back = together(
+        late, early, slopes, grads_qkv, mixed_back
+    )
     late, qkv = together(cut_line(add_up(late), 1), qkv)
     late = swap_line(late, 1)
     if pairs > 1:
         early = swap_plane(early)
-        next_pair()
+        next_pairs(pairs - 1, 1)
     late, early, slopes, grads_qkv = together(late, early, slopes, grads_qkv)
     final = cut_plane([grads_qkv[-1:]])
     late = add_up(late)
@@ -1001,26 +1020,27 @@
     parts = [input_part(slopes, qkv_full, piece) for piece in range(1, pieces)]
     final, early, late, parts = together(final, early, late, parts)
     arrived = [to_sub(part, piece) for piece, part in enumerate(parts, 1)]
-    final = line_rest(final)
-    sums = [late]
-    if pairs > 1:
-        sums.append(line_rest(early))
-    final, sums, arrived, dx2 = together(final, sums, arrived, dx2)
-    sums = moved(jnp.concatenate(sums + [final], axis=1))
+    rest = [line_rest(cuts) for cuts in (early, final) if cuts]
+    arrived, dx2, late = together(arrived, dx2, late)
+
     def rows_half(half, dx2):
         return last(half, x, member, member_flip, adaptive, dx2, arrived, slopes, qkv_full)
 
-    sums, dx2, (frames_low, dada_low) = together(sums, dx2, rows_half(0, dx2))
-    frames_low, (frames_high, dada_high) = together(moved(frames_low), rows_half(1, dx2))
+    late = moved(add_up(late))
+    late, rest, dx2, (frames_low, dada_low) = together(late, rest, dx2, rows_half(0, dx2))
+    rest = moved(jnp.concatenate([add_up(cuts) for cuts in rest], axis=1))
+    late, rest, frames_low, (frames_high, dada_high) = together(
+        late, rest, moved(frames_low), rows_half(1, dx2)
+    )
     dada_early = dada_low + dada_high
-    late, rest = sums[:, : mlp_shard.shape[1]], sums[:, mlp_shard.shape[1] :]
     hidden_columns = w_up.shape[1]
     grad_up = late[:, :hidden_columns]
     grad_down = late[:, hidden_columns : 2 * hidden_columns]
     grad_outw = late[:, 2 * hidden_columns :]
     dadaptive = jnp.concatenate([dada_early, dada_late], axis=1)[:clips]
     dadaptive = jnp.transpose(dadaptive.reshape(clips, -1, columns), (1, 0, 2))
-    dadaptive, frames_high = together(dadaptive, frames_high)
+    dadaptive, frames_high, mixed, mixed_back = together(dadaptive, frames_high, mixed, mixed_back)
+    mixed_back = jnp.where(staying(), mixed, mixed_back)
     dadaptive = lax.all_to_all(dadaptive, ALL, 0, 0, tiled=True)
     grad_frames = jnp.concatenate([frames_low, moved(frames_high)], axis=0).astype(F32)
     dadaptive = dadaptive.reshape(za, zb, cores, hh, hl, clips, columns)

time: 460 us -> 447 us (0.972)
  waiting for transfers between devices: 71.4 us -> 50.1 us
  starting transfers between devices: 65.2 us -> 85.5 us
  Pallas kernels: 228 us -> 213 us
    ppermute x10, waiting for transfers between devices: 11.9 us -> 0.03 us  [across(): return lax.ppermute(value, 'za', [(i, i ^ bit) for i in range(size)])]
    ppermute x10, starting transfers between devices: 14.3 us -> 23.6 us  [across(): return lax.ppermute(value, 'za', [(i, i ^ bit) for i in range(size)])]
    all_to_all x1, waiting for transfers between devices: 8.48 us -> 0.96 us  [body(): dadaptive = lax.all_to_all(dadaptive, ALL, 0, 0, tiled=True)]
    ppermute x8 -> x9, waiting for transfers between devices: 5.21 us -> 12.4 us  [sent(): return lax.ppermute(value, ('core', 'hh'), [(1, 2), (2, 1)])]
    ppermute x3, waiting for transfers between devices: 11.4 us -> 4.33 us  [swap_plane(): lax.ppermute(to_both, ('zb', 'hh'), [(0, 3), (1, 2), (2, 1), (3, 0)])]
    select_n x8 -> x7, other arithmetic: 12.5 us -> 5.47 us  [the longest x1 3.18 us: body(): mixed_back = jnp.where(staying(), mixed, mixed_back)]
    pallas_call x4, Pallas kernels: 89.3 us -> 83.3 us  [attend_back(): pl.pallas_call(functools.partial(attend_back_kernel, pieces, heads, step)...]
    ppermute x3, starting transfers between devices: 0.31 us -> 6.25 us  [swap_plane(): from_hh = lax.ppermute(to_hh, 'hh', SWAP)]
  transfers between devices with their start and end apart: 41 -> 42, of which waited for: 13 -> 10; matrix products, arithmetic and copies ran while one was open for 12% -> 13% of each run, Pallas kernels for 39% -> 38%
where the time goes in v4:
time: 447 us; the launch traced here: 443 us
  Pallas kernels  213 us (48%)
  starting transfers between devices  85.5 us (19%)
  waiting for transfers between devices  50.1 us (11%)
  other arithmetic  35.3 us (8%)
  matrix products  26.4 us (6%)
  local copies, waits for them, and re-layouts  17.1 us (4%)
  between operations  15.5 us (3%)
    pallas_call x4, Pallas kernels, attend_back(): pl.pallas_call(functools.partial(attend_back_kernel, pieces, heads, step)...  83.3 us
    pallas_call x1, Pallas kernels, middle(): pl.pallas_call(functools.partial(middle_kernel, pieces), grid_spec=pltpu....  39.7 us
    pallas_call x1, Pallas kernels, attend(): pl.pallas_call(functools.partial(attend_kernel, pieces, heads, step), gri...  30.1 us
    ppermute x9, starting transfers between devices, sent(): return lax.ppermute(value, ('core', 'hh'), [(1, 2), (2, 1)])  27.8 us
    dot_general x7, matrix products, dot(): lax.dot_general(a, b, dims, precision=precision, preferred_element_type=F32)  24.4 us
    ppermute x10, starting transfers between devices, across(): return lax.ppermute(value, 'za', [(i, i ^ bit) for i in range(size)])  23.6 us
    pallas_call x2, Pallas kernels, last(): pl.pallas_call(functools.partial(last_kernel, len(slopes), len(arrived)),...  16.1 us
    pallas_call x3, Pallas kernels, cut_plane(): pl.pallas_call(functools.partial(cut_kernel, [len(group) for group in wei...  16.1 us
  transfers between devices with their start and end apart: 42, of which 10 were waited for; matrix products, arithmetic and copies ran while one was open for 13% of the time, Pallas kernels for 38%

profile of v4, /device:TPU:1, one launch (start us, length us, event | category | flops | bytes accessed | tf_op | source)
XLA Modules:
  0.0 442.9 jit_solution(7859549193204992358)
XLA Ops:
  8.7 4.5 %collective-permute-start = (bf16[64,1536]{1,0:T(8,128)(2,1)S(1)}, bf16[64,1536]{1,0:T(8,128)(2,1)S(1)}, u32[]{:S(2)}, u32[]{:S(2)}) collective-permute-start(bf16[64,1536]{1,0:T(8,128)(2,1)S(1)} %reshape.294), channel_id=1, source_target_pairs={{1,2},{2,1},{5,6},{6,5},{9,10},{10,9},{13,14},{14,13},{17,18},{18,... | collective-permute-start | bytes 589832 | tf_op jit(solution)/shard_map/ppermute | solution.py:52
  28.7 5.3 %all-to-all-start = ((f32[32,4,192]{2,1,0:T(4,128)}), f32[32,4,192]{2,1,0:T(4,128)S(1)}, u32[]{:S(2)}, u32[]{:S(2)}) async-start(f32[32,4,192]{2,1,0:T(4,128)} %bitcast.9), calls=%async_computation | async-start | bytes 262144 | tf_op jit(solution)/shard_map/all_to_all | solution.py:910
  35.0 5.6 %fusion = (f32[2048,128]{1,0:T(8,128)}, f32[2048,128]{1,0:T(8,128)}) fusion(f32[128]{0:T(128)S(1)} %copy-done.32, f32[128]{0:T(128)S(1)} %copy-done.33, f32[2048]{0:T(1024)S(1)} %subtract_convert_fusion), kind=kLoop, calls=%fused_computation.14 | loop fusion | flops 524288 | bytes 2106368 | tf_op jit(solution)/shard_map/mul | solution.py:925
  50.3 5.8 %first_norm.1 = (bf16[1024,1024]{1,0:T(8,128)(2,1)}, bf16[1024,1024]{1,0:T(8,128)(2,1)}) custom-call(s32[1]{0:T(128)} %bitcast.3.stays, bf16[1024,1024]{1,0:T(8,128)(2,1)} %there.1, bf16[1024,1024]{1,0:T(8,128)(2,1)} %copy-done.3, bf16[1024,32]{1,0:T(8,128)(2,1)} %copy.79.member.refs_1_, f32[8,6144]{1,0:T(8,128)} %pad.15.adaptive.refs_3_), custom_call_target="tpu_custom_call" | custom-call | flops 41943040 | bytes 8388608 | tf_op jit(solution)/shard_map/first_norm/pallas_call | solution.py:211
  56.0 12.3 %collective-permute-done.6.refs_3_ = bf16[4,64,1536]{2,1,0:T(8,128)(2,1)} collective-permute-done((bf16[4,64,1536]{2,1,0:T(8,128)(2,1)S(1)}, bf16[4,64,1536]{2,1,0:T(8,128)(2,1)}, u32[]{:S(2)}, u32[]{:S(2)}) %collective-permute-start.6) | collective-permute-done | bytes 786464 | tf_op jit(solution)/shard_map/ppermute | solution.py:86
  75.6 9.9 %collective-permute-done.8.refs_5_ = bf16[2,64,1536]{2,1,0:T(8,128)(2,1)S(1)} collective-permute-done((bf16[2,64,1536]{2,1,0:T(8,128)(2,1)S(1)}, bf16[2,64,1536]{2,1,0:T(8,128)(2,1)S(1)}, u32[]{:S(2)}, u32[]{:S(2)}) %collective-permute-start.8) | collective-permute-done | bytes 393248 | tf_op jit(solution)/shard_map/ppermute | solution.py:91
  90.0 14.4 %project.1 = (bf16[2,1024,1536]{2,1,0:T(8,128)(2,1)}, bf16[1024,1536]{1,0:T(8,128)(2,1)}) custom-call(s32[8]{0:T(128)} %stack.87.where, bf16[1024,1024]{1,0:T(8,128)(2,1)} %get-tuple-element.175.refs_0_.refs_9_, bf16[1024,1024]{1,0:T(8,128)(2,1)} %collective-permute-done.10.refs_1_.refs_10_, bf16[4,64,1536]{2,1,0:T(8,128)(2,1)} %copy-done.8, ...), custom_call_target="tpu_custom_call" | custom-call | flops 6442450944 | bytes 10485760 | tf_op jit(solution)/shard_map/project/pallas_call | solution.py:301
  109.8 30.1 %attend.1 = (bf16[1024,512]{1,0:T(8,128)(2,1)}, bf16[1024,512]{1,0:T(8,128)(2,1)}, f32[2,2048,256]{2,1,0:T(8,128)}) custom-call(s32[1]{0:T(128)} %bitcast.2.place, s32[2,8]{1,0:T(2,128)} %pad_add_fusion.bounds, s32[2048,1]{1,0:T(8,128)} %copy.80.seg_col, s32[1,2048]{1,0:T(1,128)} %bitcast.132, ...), custom_call_target="tpu_custom_call" | custom-call | flops 17179869184 | bytes 12582912 | tf_op jit(solution)/shard_map/attend/pallas_call | solution.py:496
  139.9 8.7 %collective-permute-done.11.refs_5_ = bf16[1024,1024]{1,0:T(8,128)(2,1)S(1)} collective-permute-done((bf16[1024,1024]{1,0:T(8,128)(2,1)}, bf16[1024,1024]{1,0:T(8,128)(2,1)S(1)}, u32[]{:S(2)}, u32[]{:S(2)}) %collective-permute-start.11) | collective-permute-done | bytes 2097184 | tf_op jit(solution)/shard_map/ppermute | solution.py:52
  152.5 39.7 %middle.1 = (bf16[1024,1024]{1,0:T(8,128)(2,1)}, f32[1024,1024]{1,0:T(8,128)}, bf16[1024,1024]{1,0:T(8,128)(2,1)}, bf16[1024,1024]{1,0:T(8,128)(2,1)}, bf16[1024...) custom-call(s32[2]{0:T(128)} %pad_add_fusion.2.place, ...), custom_call_target="tpu_custom_call" | custom-call | flops 30064771072 | bytes 31457280 | tf_op jit(solution)/shard_map/middle/pallas_call | solution.py:746
  192.2 6.2 %convolution_convert_fusion = bf16[1024,1024]{1,0:T(8,128)(2,1)} fusion(bf16[1024,1024]{1,0:T(8,128)(2,1)} %get-tuple-element.198, bf16[1024,1024]{1,0:T(8,128)(2,1)} %get-tuple-element.200), kind=kOutput, calls=%fused_computation.3 | convolution fusion | flops 2148532224 | bytes 6291456 | tf_op jit(solution)/shard_map/dot_general | solution.py:31
  220.5 7.4 %cut.3 = (bf16[4,64,2560]{2,1,0:T(8,128)(2,1)}, bf16[4,64,2560]{2,1,0:T(8,128)(2,1)}, bf16[4,64,2560]{2,1,0:T(8,128)(2,1)}, bf16[4,64,2560]{2,1,0:T(8,128)(2,1)}) custom-call(s32[2]{0:T(128)} %pad_add_fusion.1.where, bf16[4,2,2,64,1024]{4,3,2,1,0:T(8,128)(2,1)} %bitcast.117, bf16[4,2,2,64,1024]{4,3,2,1,0:T(8,128)(2,1)} %bitcast.28.refs_1_, ...), custom_call_target="tpu_custom_call" | custom-call | bytes 15728640 | tf_op jit(solution)/shard_map/cut/pallas_call | solution.py:122
  230.5 20.0 %attend_back.6 = (bf16[2,1024,384]{2,1,0:T(8,128)(2,1)}, bf16[1024,384]{1,0:T(8,128)(2,1)}) custom-call(s32[1]{0:T(128)} %bitcast.2.place, s32[2,8]{1,0:T(2,128)} %pad_add_fusion.bounds, s32[2048,1]{1,0:T(8,128)} %copy.80.seg_col, s32[1,2048]{1,0:T(1,128)} %bitcast.133, bf16[2,1024,1536]{2,1,0:T(8,128)(2,1)} %get-tuple-element.246.refs_0_.refs_1_.refs_3_, ...), custom_call_target="tpu_custom_call" | custom-call | flops 10737418240 | bytes 4194304 | tf_op jit(solution)/shard_map/attend_back/pallas_call | solution.py:617
  250.6 23.9 %attend_back.5 = (bf16[2,1024,384]{2,1,0:T(8,128)(2,1)}, bf16[1024,384]{1,0:T(8,128)(2,1)}) custom-call(s32[1]{0:T(128)} %bitcast.2.place, s32[2,8]{1,0:T(2,128)} %pad_add_fusion.bounds, s32[2048,1]{1,0:T(8,128)} %copy.80.seg_col, s32[1,2048]{1,0:T(1,128)} %bitcast.134, bf16[2,1024,1536]{2,1,0:T(8,128)(2,1)} %get-tuple-element.246.refs_0_.refs_1_.refs_3_, ...), custom_call_target="tpu_custom_call" | custom-call | flops 10737418240 | bytes 4194304 | tf_op jit(solution)/shard_map/attend_back/pallas_call | solution.py:617
  274.4 19.6 %attend_back.4 = (bf16[2,1024,384]{2,1,0:T(8,128)(2,1)}, bf16[1024,384]{1,0:T(8,128)(2,1)}) custom-call(s32[1]{0:T(128)} %bitcast.2.place, s32[2,8]{1,0:T(2,128)} %pad_add_fusion.bounds, s32[2048,1]{1,0:T(8,128)} %copy.80.seg_col, s32[1,2048]{1,0:T(1,128)} %bitcast.135, bf16[2,1024,1536]{2,1,0:T(8,128)(2,1)} %get-tuple-element.246.refs_0_.refs_1_.refs_3_, ...), custom_call_target="tpu_custom_call" | custom-call | flops 10737418240 | bytes 4194304 | tf_op jit(solution)/shard_map/attend_back/pallas_call | solution.py:617
  294.0 4.8 %cut.4 = (bf16[4,64,1152]{2,1,0:T(8,128)(2,1)}, bf16[4,64,1152]{2,1,0:T(8,128)(2,1)}, bf16[4,64,1152]{2,1,0:T(8,128)(2,1)}, bf16[4,64,1152]{2,1,0:T(8,128)(2,1)}) custom-call(s32[2]{0:T(128)} %pad_add_fusion.1.where, bf16[4,2,2,64,384]{4,3,2,1,0:T(8,128)(2,1)} %bitcast.123, bf16[4,2,2,64,384]{4,3,2,1,0:T(8,128)(2,1)} %bitcast.122, ...), custom_call_target="tpu_custom_call" | custom-call | bytes 4718592 | tf_op jit(solution)/shard_map/cut/pallas_call | solution.py:122
  301.7 10.8 %collective-permute-start.21 = (bf16[2,64,2560]{2,1,0:T(8,128)(2,1)S(1)}, bf16[2,64,2560]{2,1,0:T(8,128)(2,1)S(1)}, u32[]{:S(2)}, u32[]{:S(2)}) collective-permute-start(bf16[2,64,2560]{2,1,0:T(8,128)(2,1)S(1)} %get-tuple-element.238), channel_id=1, source_target_pairs={{0,8},{8,0},{16,24},{24,16},{1,9},{9,1},{17,25},{25,17},{2,10},{10... | collective-permute-start | bytes 1966088 | tf_op jit(solution)/shard_map/ppermute | solution.py:78
  314.4 6.2 %collective-permute-start.23 = (bf16[4,64,1152]{2,1,0:T(8,128)(2,1)}, bf16[4,64,1152]{2,1,0:T(8,128)(2,1)S(1)}, u32[]{:S(2)}, u32[]{:S(2)}) collective-permute-start(bf16[4,64,1152]{2,1,0:T(8,128)(2,1)} %get-tuple-element.241), channel_id=1, source_target_pairs={{0,1},{1,0},{2,3},{3,2},{4,5},{5,4},{6,7},{7,6},{8,9},{9,8},{10,11... | collective-permute-start | bytes 1769480 | tf_op jit(solution)/shard_map/ppermute | solution.py:143
  320.6 19.8 %attend_back.7 = (bf16[2,1024,384]{2,1,0:T(8,128)(2,1)}, bf16[1024,384]{1,0:T(8,128)(2,1)}) custom-call(s32[1]{0:T(128)} %bitcast.2.place, s32[2,8]{1,0:T(2,128)} %pad_add_fusion.bounds, s32[2048,1]{1,0:T(8,128)} %copy.80.seg_col, s32[1,2048]{1,0:T(1,128)} %bitcast.136, bf16[2,1024,1536]{2,1,0:T(8,128)(2,1)} %get-tuple-element.246.refs_0_.refs_1_.refs_3_, ...), custom_call_target="tpu_custom_call" | custom-call | flops 10737418240 | bytes 4194304 | tf_op jit(solution)/shard_map/attend_back/pallas_call | solution.py:617
  340.4 4.3 collective-permute-done.24
  358.4 7.6 %input_part.1 = bf16[1024,1024]{1,0:T(8,128)(2,1)} custom-call(bf16[2,1024,384]{2,1,0:T(8,128)(2,1)} %get-tuple-element.272.refs_0_.refs_6_, bf16[2,1024,384]{2,1,0:T(8,128)(2,1)} %get-tuple-element.273.refs_1_.refs_7_, bf16[2,1024,384]{2,1,0:T(8,128)(2,1)} %get-tuple-element.274.refs_2_.refs_8_, bf16[2,1024,384]{2,1,0:T(8,128)(2,1)} %get-tuple-element.275.refs_3_.refs_9_, ...), custom_call_target="tpu_custom_call" | custom-call | flops 3221225472 | bytes 8388608 | tf_op jit(solution)/shard_map/input_part/pallas_call | solution.py:795
  378.6 8.0 %last.2 = (bf16[512,1024]{1,0:T(8,128)(2,1)}, f32[8,2048]{1,0:T(8,128)}) custom-call(bf16[1024,1024]{1,0:T(8,128)(2,1)} %get-tuple-element.168.refs_0_, bf16[1024,32]{1,0:T(8,128)(2,1)} %copy.79.member.refs_1_, bf16[16,1024]{1,0:T(8,128)(2,1)} %pad.18.refs_2_, f32[8,6144]{1,0:T(8,128)} %pad.15.adaptive.refs_3_, f32[1024,1024]{1,0:T(8,128)} %get-tuple-element.302.refs_4_, ...), custom_call_target="tpu_custom_call" | custom-call | flops 1610612736 | bytes 6291456 | tf_op jit(solution)/shard_map/last/pallas_call | solution.py:845
  394.1 8.1 %last.3 = (bf16[512,1024]{1,0:T(8,128)(2,1)}, f32[8,2048]{1,0:T(8,128)}) custom-call(bf16[1024,1024]{1,0:T(8,128)(2,1)} %get-tuple-element.168.refs_0_, bf16[1024,32]{1,0:T(8,128)(2,1)} %copy.79.member.refs_1_, bf16[16,1024]{1,0:T(8,128)(2,1)} %pad.18.refs_2_, f32[8,6144]{1,0:T(8,128)} %pad.15.adaptive.refs_3_, f32[1024,1024]{1,0:T(8,128)} %get-tuple-element.302.refs_4_, ...), custom_call_target="tpu_custom_call" | custom-call | flops 1610612736 | bytes 6291456 | tf_op jit(solution)/shard_map/last/pallas_call | solution.py:845
  411.0 5.8 %all-to-all-start.1 = ((f32[32,4,192]{2,1,0:T(4,128)}), f32[32,4,192]{2,1,0:T(4,128)}, u32[]{:S(2)}, u32[]{:S(2)}) async-start(f32[32,4,192]{2,1,0:T(4,128)} %bitcast.127), calls=%async_computation.1 | async-start | bytes 262144 | tf_op jit(solution)/shard_map/all_to_all | solution.py:1044
  (263 shorter events, 138.7 us)
Async XLA Ops:
  15.2 32.4 %collective-permute-start.5 = (bf16[1024,1024]{1,0:T(8,128)(2,1)}, bf16[1024,1024]{1,0:T(8,128)(2,1)S(1)}, u32[]{:S(2)}, u32[]{:S(2)}) collective-permute-start(bf16[1024,1024]{1,0:T(8,128)(2,1)} %there.1), channel_id=1, source_target_pairs={{1,2},{2,1},{5,6},{6,5},{9,10},{10,9},{13,14},{14,13},{17,18},{18,... | collective-permute-start | bytes 6291464 | tf_op jit(solution)/shard_map/ppermute | solution.py:52
  24.3 21.5 %collective-permute-start.2 = (bf16[64,1536]{1,0:T(8,128)(2,1)S(1)}, bf16[64,1536]{1,0:T(8,128)(2,1)S(1)}, u32[]{:S(2)}, u32[]{:S(2)}) collective-permute-start(bf16[64,1536]{1,0:T(8,128)(2,1)S(1)} %broadcast_select_fusion.5), channel_id=1, source_target_pairs={{0,8},{8,0},{16,24},{24,16},{1,9},{9,1},{17,25},{25,17},{2,10},{10... | collective-permute-start | bytes 589832 | tf_op jit(solution)/shard_map/ppermute | solution.py:78
  25.7 20.1 %collective-permute-start.3 = (bf16[64,1536]{1,0:T(8,128)(2,1)S(1)}, bf16[64,1536]{1,0:T(8,128)(2,1)S(1)}, u32[]{:S(2)}, u32[]{:S(2)}) collective-permute-start(bf16[64,1536]{1,0:T(8,128)(2,1)S(1)} %broadcast_select_fusion.5), channel_id=1, source_target_pairs={{0,16},{8,24},{16,0},{24,8},{1,17},{9,25},{17,1},{25,9},{2,18},{10... | collective-permute-start | bytes 589832 | tf_op jit(solution)/shard_map/ppermute | solution.py:78
  28.0 17.8 %collective-permute-start.4 = (bf16[64,1536]{1,0:T(8,128)(2,1)S(1)}, bf16[64,1536]{1,0:T(8,128)(2,1)S(1)}, u32[]{:S(2)}, u32[]{:S(2)}) collective-permute-start(bf16[64,1536]{1,0:T(8,128)(2,1)S(1)} %broadcast_select_fusion.5), channel_id=1, source_target_pairs={{0,24},{8,16},{16,8},{24,0},{1,25},{9,17},{17,9},{25,1},{2,26},{10... | collective-permute-start | bytes 589832 | tf_op jit(solution)/shard_map/ppermute | solution.py:78
  34.0 117.5 %all-gather.2.cloned.1.call-start = ((), (), s32[]{:S(2)}) async-start(), calls=%async_computation.2 | async-start | bytes 10813440 | tf_op jit(solution)/shard_map/all_gather | solution.py:951
  47.6 20.8 %collective-permute-start.6 = (bf16[4,64,1536]{2,1,0:T(8,128)(2,1)S(1)}, bf16[4,64,1536]{2,1,0:T(8,128)(2,1)}, u32[]{:S(2)}, u32[]{:S(2)}) collective-permute-start(bf16[4,64,1536]{2,1,0:T(8,128)(2,1)S(1)} %pad_maximum_fusion.refs_2_), channel_id=1, source_target_pairs={{0,4},{4,0},{1,5},{5,1},{2,6},{6,2},{3,7},{7,3},{8,12},{12,8},{9,1... | collective-permute-start | bytes 2359304 | tf_op jit(solution)/shard_map/ppermute | solution.py:86
  48.3 20.8 %collective-permute-start.7 = (bf16[4,64,1536]{2,1,0:T(8,128)(2,1)S(1)}, bf16[4,64,1536]{2,1,0:T(8,128)(2,1)}, u32[]{:S(2)}, u32[]{:S(2)}) collective-permute-start(bf16[4,64,1536]{2,1,0:T(8,128)(2,1)S(1)} %pad_maximum_fusion.refs_2_), channel_id=1, source_target_pairs={{0,1},{1,0},{2,3},{3,2},{4,5},{5,4},{6,7},{7,6},{8,9},{9,8},{10,11... | collective-permute-start | bytes 2359304 | tf_op jit(solution)/shard_map/ppermute | solution.py:86
  69.0 20.2 %collective-permute-start.10 = (bf16[1024,1024]{1,0:T(8,128)(2,1)}, bf16[1024,1024]{1,0:T(8,128)(2,1)}, u32[]{:S(2)}, u32[]{:S(2)}) collective-permute-start(bf16[1024,1024]{1,0:T(8,128)(2,1)} %get-tuple-element.175.refs_0_.refs_9_), channel_id=1, source_target_pairs={{2,0},{0,2},{3,1},{1,3},{6,4},{4,6},{7,5},{5,7},{10,8},{8,10},{11,... | collective-permute-start | bytes 6291464 | tf_op jit(solution)/shard_map/ppermute | solution.py:65
  104.4 44.3 %collective-permute-start.11 = (bf16[1024,1024]{1,0:T(8,128)(2,1)}, bf16[1024,1024]{1,0:T(8,128)(2,1)S(1)}, u32[]{:S(2)}, u32[]{:S(2)}) collective-permute-start(bf16[1024,1024]{1,0:T(8,128)(2,1)} %refs_4_), channel_id=1, source_target_pairs={{1,2},{2,1},{5,6},{6,5},{9,10},{10,9},{13,14},{14,13},{17,18},{18,... | collective-permute-start | bytes 6291464 | tf_op jit(solution)/shard_map/ppermute | solution.py:52
  198.4 21.1 %collective-permute-start.14 = (bf16[1024,1024]{1,0:T(8,128)(2,1)}, bf16[1024,1024]{1,0:T(8,128)(2,1)}, u32[]{:S(2)}, u32[]{:S(2)}) collective-permute-start(bf16[1024,1024]{1,0:T(8,128)(2,1)} %convolution_convert_fusion), channel_id=1, source_target_pairs={{0,2},{2,0},{1,3},{3,1},{4,6},{6,4},{5,7},{7,5},{8,10},{10,8},{9,1... | collective-permute-start | bytes 6291464 | tf_op jit(solution)/shard_map/ppermute | solution.py:70
  202.3 17.2 %collective-permute-start.13 = (bf16[1024,1024]{1,0:T(8,128)(2,1)}, bf16[1024,1024]{1,0:T(8,128)(2,1)}, u32[]{:S(2)}, u32[]{:S(2)}) collective-permute-start(bf16[1024,1024]{1,0:T(8,128)(2,1)} %convolution_convert_fusion.2), channel_id=1, source_target_pairs={{0,2},{2,0},{1,3},{3,1},{4,6},{6,4},{5,7},{7,5},{8,10},{10,8},{9,1... | collective-permute-start | bytes 6291464 | tf_op jit(solution)/shard_map/ppermute | solution.py:70
  206.9 91.9 %collective-permute-start.20 = (bf16[1024,1024]{1,0:T(8,128)(2,1)S(1)}, bf16[1024,1024]{1,0:T(8,128)(2,1)}, u32[]{:S(2)}, u32[]{:S(2)}) collective-permute-start(bf16[1024,1024]{1,0:T(8,128)(2,1)S(1)} %copy-done.1), channel_id=1, source_target_pairs={{1,2},{2,1},{5,6},{6,5},{9,10},{10,9},{13,14},{14,13},{17,18},{18,... | collective-permute-start | bytes 6291464 | tf_op jit(solution)/shard_map/ppermute | solution.py:52
  227.8 71.0 %collective-permute-start.17 = (bf16[4,64,2560]{2,1,0:T(8,128)(2,1)}, bf16[4,64,2560]{2,1,0:T(8,128)(2,1)}, u32[]{:S(2)}, u32[]{:S(2)}) collective-permute-start(bf16[4,64,2560]{2,1,0:T(8,128)(2,1)} %get-tuple-element.215), channel_id=1, source_target_pairs={{0,4},{4,0},{1,5},{5,1},{2,6},{6,2},{3,7},{7,3},{8,12},{12,8},{9,1... | collective-permute-start | bytes 3932168 | tf_op jit(solution)/shard_map/ppermute | solution.py:144
  229.3 69.5 %collective-permute-start.18 = (bf16[4,64,2560]{2,1,0:T(8,128)(2,1)}, bf16[4,64,2560]{2,1,0:T(8,128)(2,1)}, u32[]{:S(2)}, u32[]{:S(2)}) collective-permute-start(bf16[4,64,2560]{2,1,0:T(8,128)(2,1)} %get-tuple-element.216), channel_id=1, source_target_pairs={{0,1},{1,0},{2,3},{3,2},{4,5},{5,4},{6,7},{7,6},{8,9},{9,8},{10,11... | collective-permute-start | bytes 3932168 | tf_op jit(solution)/shard_map/ppermute | solution.py:143
  229.3 69.5 %collective-permute-start.19 = (bf16[4,64,2560]{2,1,0:T(8,128)(2,1)}, bf16[4,64,2560]{2,1,0:T(8,128)(2,1)}, u32[]{:S(2)}, u32[]{:S(2)}) collective-permute-start(bf16[4,64,2560]{2,1,0:T(8,128)(2,1)} %get-tuple-element.217), channel_id=1, source_target_pairs={{0,5},{1,4},{4,1},{5,0},{2,7},{3,6},{6,3},{7,2},{8,13},{9,12},{12,... | collective-permute-start | bytes 3932168 | tf_op jit(solution)/shard_map/ppermute | solution.py:142
  301.7 43.1 %collective-permute-start.21 = (bf16[2,64,2560]{2,1,0:T(8,128)(2,1)S(1)}, bf16[2,64,2560]{2,1,0:T(8,128)(2,1)S(1)}, u32[]{:S(2)}, u32[]{:S(2)}) collective-permute-start(bf16[2,64,2560]{2,1,0:T(8,128)(2,1)S(1)} %get-tuple-element.238), channel_id=1, source_target_pairs={{0,8},{8,0},{16,24},{24,16},{1,9},{9,1},{17,25},{25,17},{2,10},{10... | collective-permute-start | bytes 1966088 | tf_op jit(solution)/shard_map/ppermute | solution.py:78
  312.5 27.9 %collective-permute-start.22 = (bf16[4,64,1152]{2,1,0:T(8,128)(2,1)}, bf16[4,64,1152]{2,1,0:T(8,128)(2,1)S(1)}, u32[]{:S(2)}, u32[]{:S(2)}) collective-permute-start(bf16[4,64,1152]{2,1,0:T(8,128)(2,1)} %get-tuple-element.240), channel_id=1, source_target_pairs={{0,4},{4,0},{1,5},{5,1},{2,6},{6,2},{3,7},{7,3},{8,12},{12,8},{9,1... | collective-permute-start | bytes 1769480 | tf_op jit(solution)/shard_map/ppermute | solution.py:144
  314.4 26.0 %collective-permute-start.23 = (bf16[4,64,1152]{2,1,0:T(8,128)(2,1)}, bf16[4,64,1152]{2,1,0:T(8,128)(2,1)S(1)}, u32[]{:S(2)}, u32[]{:S(2)}) collective-permute-start(bf16[4,64,1152]{2,1,0:T(8,128)(2,1)} %get-tuple-element.241), channel_id=1, source_target_pairs={{0,1},{1,0},{2,3},{3,2},{4,5},{5,4},{6,7},{7,6},{8,9},{9,8},{10,11... | collective-permute-start | bytes 1769480 | tf_op jit(solution)/shard_map/ppermute | solution.py:143
  320.6 24.2 %collective-permute-start.24 = (bf16[4,64,1152]{2,1,0:T(8,128)(2,1)}, bf16[4,64,1152]{2,1,0:T(8,128)(2,1)}, u32[]{:S(2)}, u32[]{:S(2)}) collective-permute-start(bf16[4,64,1152]{2,1,0:T(8,128)(2,1)} %get-tuple-element.242), channel_id=1, source_target_pairs={{0,5},{1,4},{4,1},{5,0},{2,7},{3,6},{6,3},{7,2},{8,13},{9,12},{12,... | collective-permute-start | bytes 1769480 | tf_op jit(solution)/shard_map/ppermute | solution.py:142
  370.8 16.6 %collective-permute-start.33 = (bf16[64,384]{1,0:T(8,128)(2,1)S(1)}, bf16[64,384]{1,0:T(8,128)(2,1)}, u32[]{:S(2)}, u32[]{:S(2)}) collective-permute-start(bf16[64,384]{1,0:T(8,128)(2,1)S(1)} %get-tuple-element.330), channel_id=1, source_target_pairs={{0,8},{8,0},{16,24},{24,16},{1,9},{9,1},{17,25},{25,17},{2,10},{10... | collective-permute-start | bytes 147464 | tf_op jit(solution)/shard_map/ppermute | solution.py:78
  371.0 16.4 %collective-permute-start.34 = (bf16[64,384]{1,0:T(8,128)(2,1)S(1)}, bf16[64,384]{1,0:T(8,128)(2,1)}, u32[]{:S(2)}, u32[]{:S(2)}) collective-permute-start(bf16[64,384]{1,0:T(8,128)(2,1)S(1)} %get-tuple-element.329), channel_id=1, source_target_pairs={{0,16},{8,24},{16,0},{24,8},{1,17},{9,25},{17,1},{25,9},{2,18},{10... | collective-permute-start | bytes 147464 | tf_op jit(solution)/shard_map/ppermute | solution.py:78
  387.4 18.5 %collective-permute-start.37 = (bf16[512,1024]{1,0:T(8,128)(2,1)}, bf16[512,1024]{1,0:T(8,128)(2,1)S(1)}, u32[]{:S(2)}, u32[]{:S(2)}) collective-permute-start(bf16[512,1024]{1,0:T(8,128)(2,1)} %get-tuple-element.301), channel_id=1, source_target_pairs={{1,2},{2,1},{5,6},{6,5},{9,10},{10,9},{13,14},{14,13},{17,18},{18,... | collective-permute-start | bytes 3145736 | tf_op jit(solution)/shard_map/ppermute | solution.py:52
  408.5 23.2 %collective-permute-start.38 = (bf16[512,1024]{1,0:T(8,128)(2,1)}, bf16[512,1024]{1,0:T(8,128)(2,1)}, u32[]{:S(2)}, u32[]{:S(2)}) collective-permute-start(bf16[512,1024]{1,0:T(8,128)(2,1)} %get-tuple-element.312), channel_id=1, source_target_pairs={{1,2},{2,1},{5,6},{6,5},{9,10},{10,9},{13,14},{14,13},{17,18},{18,... | collective-permute-start | bytes 3145736 | tf_op jit(solution)/shard_map/ppermute | solution.py:52
  411.0 16.6 %all-to-all-start.1 = ((f32[32,4,192]{2,1,0:T(4,128)}), f32[32,4,192]{2,1,0:T(4,128)}, u32[]{:S(2)}, u32[]{:S(2)}) async-start(f32[32,4,192]{2,1,0:T(4,128)} %bitcast.127), calls=%async_computation.1 | async-start | bytes 262144 | tf_op jit(solution)/shard_map/all_to_all | solution.py:1044
  (68 other events, 663.8 us)
Sparse Core Ops, SparseCore 0:
  47.7 101.9 all-gather.1

commit v5 on v4

--- a/solution.py
+++ b/solution.py
@@ -31,8 +31,8 @@
     return lax.dot_general(a, b, dims, precision=precision, preferred_element_type=F32)
 
 
-def params(**more):
-    return pltpu.CompilerParams(vmem_limit_bytes=VMEM_LIMIT, **more)
+def params(limit=VMEM_LIMIT):
+    return pltpu.CompilerParams(vmem_limit_bytes=limit)
 
 
 def cost(flops, bytes_accessed, transcendentals=0):
@@ -799,7 +799,7 @@
         + [whole(weights.shape, 1)],
         out_shape=jax.ShapeDtypeStruct((rows, width), BF16),
         out_specs=pl.BlockSpec((tile, width), lambda i: (i, 0)),
-        compiler_params=params(),
+        compiler_params=params(20 * 1024 * 1024),
         cost_estimate=cost(2 * rows * width * columns, rows * width * 8),
         name="input_part",
     )(*slopes, weights)

time: 447 us -> 451 us (level)
  starting transfers between devices: 85.5 us -> 68.2 us
  Pallas kernels: 213 us -> 230 us
  local copies, waits for them, and re-layouts: 17.1 us -> 23.5 us
  waiting for transfers between devices: 50.1 us -> 44.2 us
    pallas_call x4, Pallas kernels: 83.3 us -> 97.1 us  [attend_back(): pl.pallas_call(functools.partial(attend_back_kernel, pieces, heads, step)...]
    ppermute x10, starting transfers between devices: 23.6 us -> 12 us  [across(): return lax.ppermute(value, 'za', [(i, i ^ bit) for i in range(size)])]
    ppermute x3, starting transfers between devices: 6.25 us -> 0.01 us  [swap_plane(): from_hh = lax.ppermute(to_hh, 'hh', SWAP)]
    unnamed x100 -> x120, local copies, waits for them, and re-layouts: 4.28 us -> 9.9 us
    pallas_call x1, Pallas kernels: 30.1 us -> 35.6 us  [attend(): pl.pallas_call(functools.partial(attend_kernel, pieces, heads, step), gri...]
    ppermute x9, waiting for transfers between devices: 12.4 us -> 7.74 us  [sent(): return lax.ppermute(value, ('core', 'hh'), [(1, 2), (2, 1)])]
  transfers between devices with their start and end apart: 42 -> 42, of which waited for: 10 -> 12; matrix products, arithmetic and copies ran while one was open for 13% -> 13% of each run, Pallas kernels for 38% -> 42%
where the time goes in v5:
time: 451 us; the launch traced here: 445 us
  Pallas kernels  230 us (51%)
  starting transfers between devices  68.2 us (15%)
  waiting for transfers between devices  44.2 us (10%)
  other arithmetic  37.1 us (8%)
  matrix products  26.4 us (6%)
  local copies, waits for them, and re-layouts  23.5 us (5%)
  between operations  15.5 us (3%)
    pallas_call x4, Pallas kernels, attend_back(): pl.pallas_call(functools.partial(attend_back_kernel, pieces, heads, step)...  97.1 us
    pallas_call x1, Pallas kernels, middle(): pl.pallas_call(functools.partial(middle_kernel, pieces), grid_spec=pltpu....  39.7 us
    pallas_call x1, Pallas kernels, attend(): pl.pallas_call(functools.partial(attend_kernel, pieces, heads, step), gri...  35.6 us
    ppermute x9, starting transfers between devices, sent(): return lax.ppermute(value, ('core', 'hh'), [(1, 2), (2, 1)])  27.2 us
    dot_general x7, matrix products, dot(): lax.dot_general(a, b, dims, precision=precision, preferred_element_type=F32)  24.4 us
    pallas_call x3, Pallas kernels, cut_plane(): pl.pallas_call(functools.partial(cut_kernel, [len(group) for group in wei...  16.4 us
    pallas_call x2, Pallas kernels, last(): pl.pallas_call(functools.partial(last_kernel, len(slopes), len(arrived)),...  16.1 us
    pallas_call x1, Pallas kernels, project(): pl.pallas_call(functools.partial(project_kernel, pieces, tiles, lanes), g...  14.4 us
  transfers between devices with their start and end apart: 42, of which 12 were waited for; matrix products, arithmetic and copies ran while one was open for 13% of the time, Pallas kernels for 42%

profile of v5, /device:TPU:1, one launch (start us, length us, event | category | flops | bytes accessed | tf_op | source)
XLA Modules:
  0.0 444.8 jit_solution(8998237698904481161)
XLA Ops:
  8.7 4.5 %collective-permute-start = (bf16[64,1536]{1,0:T(8,128)(2,1)S(1)}, bf16[64,1536]{1,0:T(8,128)(2,1)S(1)}, u32[]{:S(2)}, u32[]{:S(2)}) collective-permute-start(bf16[64,1536]{1,0:T(8,128)(2,1)S(1)} %reshape.294), channel_id=1, source_target_pairs={{1,2},{2,1},{5,6},{6,5},{9,10},{10,9},{13,14},{14,13},{17,18},{18,... | collective-permute-start | bytes 589832 | tf_op jit(solution)/shard_map/ppermute | solution.py:52
  28.7 5.3 %all-to-all-start = ((f32[32,4,192]{2,1,0:T(4,128)}), f32[32,4,192]{2,1,0:T(4,128)S(1)}, u32[]{:S(2)}, u32[]{:S(2)}) async-start(f32[32,4,192]{2,1,0:T(4,128)} %bitcast.9), calls=%async_computation | async-start | bytes 262144 | tf_op jit(solution)/shard_map/all_to_all | solution.py:910
  35.0 5.7 %fusion = (f32[2048,128]{1,0:T(8,128)}, f32[2048,128]{1,0:T(8,128)}) fusion(f32[128]{0:T(128)S(1)} %copy-done.41, f32[128]{0:T(128)S(1)} %copy-done.42, f32[2048]{0:T(1024)S(1)} %subtract_convert_fusion), kind=kLoop, calls=%fused_computation.14 | loop fusion | flops 524288 | bytes 2106368 | tf_op jit(solution)/shard_map/mul | solution.py:925
  40.8 4.2 all-to-all-done
  50.3 5.7 %first_norm.1 = (bf16[1024,1024]{1,0:T(8,128)(2,1)}, bf16[1024,1024]{1,0:T(8,128)(2,1)}) custom-call(s32[1]{0:T(128)} %bitcast.3.stays, bf16[1024,1024]{1,0:T(8,128)(2,1)} %there.1, bf16[1024,1024]{1,0:T(8,128)(2,1)} %copy-done.8, bf16[1024,32]{1,0:T(8,128)(2,1)} %copy.79.member.refs_1_, f32[8,6144]{1,0:T(8,128)} %pad.15.adaptive.refs_3_), custom_call_target="tpu_custom_call" | custom-call | flops 41943040 | bytes 8388608 | tf_op jit(solution)/shard_map/first_norm/pallas_call | solution.py:211
  56.0 12.4 %collective-permute-done.6.refs_3_ = bf16[4,64,1536]{2,1,0:T(8,128)(2,1)} collective-permute-done((bf16[4,64,1536]{2,1,0:T(8,128)(2,1)S(1)}, bf16[4,64,1536]{2,1,0:T(8,128)(2,1)}, u32[]{:S(2)}, u32[]{:S(2)}) %collective-permute-start.6) | collective-permute-done | bytes 786464 | tf_op jit(solution)/shard_map/ppermute | solution.py:86
  75.6 9.9 %collective-permute-done.8.refs_5_ = bf16[2,64,1536]{2,1,0:T(8,128)(2,1)S(1)} collective-permute-done((bf16[2,64,1536]{2,1,0:T(8,128)(2,1)S(1)}, bf16[2,64,1536]{2,1,0:T(8,128)(2,1)S(1)}, u32[]{:S(2)}, u32[]{:S(2)}) %collective-permute-start.8) | collective-permute-done | bytes 393248 | tf_op jit(solution)/shard_map/ppermute | solution.py:91
  90.0 14.4 %project.1 = (bf16[2,1024,1536]{2,1,0:T(8,128)(2,1)}, bf16[1024,1536]{1,0:T(8,128)(2,1)}) custom-call(s32[8]{0:T(128)} %stack.87.where, bf16[1024,1024]{1,0:T(8,128)(2,1)} %get-tuple-element.175.refs_0_.refs_9_, bf16[1024,1024]{1,0:T(8,128)(2,1)} %collective-permute-done.10.refs_1_.refs_10_, bf16[4,64,1536]{2,1,0:T(8,128)(2,1)} %copy-done.13, ...), custom_call_target="tpu_custom_call" | custom-call | flops 6442450944 | bytes 10485760 | tf_op jit(solution)/shard_map/project/pallas_call | solution.py:301
  109.8 35.6 %attend.1 = (bf16[1024,512]{1,0:T(8,128)(2,1)}, bf16[1024,512]{1,0:T(8,128)(2,1)}, f32[2,2048,256]{2,1,0:T(8,128)}) custom-call(s32[1]{0:T(128)} %bitcast.2.place, s32[2,8]{1,0:T(2,128)} %pad_add_fusion.bounds, s32[2048,1]{1,0:T(8,128)} %copy.80.seg_col, s32[1,2048]{1,0:T(1,128)} %bitcast.132, ...), custom_call_target="tpu_custom_call" | custom-call | flops 17179869184 | bytes 12582912 | tf_op jit(solution)/shard_map/attend/pallas_call | solution.py:496
  152.5 39.7 %middle.1 = (bf16[1024,1024]{1,0:T(8,128)(2,1)}, f32[1024,1024]{1,0:T(8,128)}, bf16[1024,1024]{1,0:T(8,128)(2,1)}, bf16[1024,1024]{1,0:T(8,128)(2,1)}, bf16[1024...) custom-call(s32[2]{0:T(128)} %pad_add_fusion.2.place, ...), custom_call_target="tpu_custom_call" | custom-call | flops 30064771072 | bytes 31457280 | tf_op jit(solution)/shard_map/middle/pallas_call | solution.py:746
  192.2 6.1 %convolution_convert_fusion = bf16[1024,1024]{1,0:T(8,128)(2,1)} fusion(bf16[1024,1024]{1,0:T(8,128)(2,1)} %get-tuple-element.198, bf16[1024,1024]{1,0:T(8,128)(2,1)} %get-tuple-element.200), kind=kOutput, calls=%fused_computation.3 | convolution fusion | flops 2148532224 | bytes 6291456 | tf_op jit(solution)/shard_map/dot_general | solution.py:31
  220.5 7.4 %cut.3 = (bf16[4,64,2560]{2,1,0:T(8,128)(2,1)}, bf16[4,64,2560]{2,1,0:T(8,128)(2,1)}, bf16[4,64,2560]{2,1,0:T(8,128)(2,1)}, bf16[4,64,2560]{2,1,0:T(8,128)(2,1)}) custom-call(s32[2]{0:T(128)} %pad_add_fusion.1.where, bf16[4,2,2,64,1024]{4,3,2,1,0:T(8,128)(2,1)} %bitcast.117, bf16[4,2,2,64,1024]{4,3,2,1,0:T(8,128)(2,1)} %bitcast.28.refs_1_, ...), custom_call_target="tpu_custom_call" | custom-call | bytes 15728640 | tf_op jit(solution)/shard_map/cut/pallas_call | solution.py:122
  230.5 23.6 %attend_back.6 = (bf16[2,1024,384]{2,1,0:T(8,128)(2,1)}, bf16[1024,384]{1,0:T(8,128)(2,1)}) custom-call(s32[1]{0:T(128)} %bitcast.2.place, s32[2,8]{1,0:T(2,128)} %pad_add_fusion.bounds, s32[2048,1]{1,0:T(8,128)} %copy.80.seg_col, s32[1,2048]{1,0:T(1,128)} %bitcast.133, bf16[2,1024,1536]{2,1,0:T(8,128)(2,1)} %get-tuple-element.246.refs_0_.refs_1_.refs_3_, ...), custom_call_target="tpu_custom_call" | custom-call | flops 10737418240 | bytes 4194304 | tf_op jit(solution)/shard_map/attend_back/pallas_call | solution.py:617
  254.2 26.8 %attend_back.5 = (bf16[2,1024,384]{2,1,0:T(8,128)(2,1)}, bf16[1024,384]{1,0:T(8,128)(2,1)}) custom-call(s32[1]{0:T(128)} %bitcast.2.place, s32[2,8]{1,0:T(2,128)} %pad_add_fusion.bounds, s32[2048,1]{1,0:T(8,128)} %copy.80.seg_col, s32[1,2048]{1,0:T(1,128)} %bitcast.134, bf16[2,1024,1536]{2,1,0:T(8,128)(2,1)} %get-tuple-element.246.refs_0_.refs_1_.refs_3_, ...), custom_call_target="tpu_custom_call" | custom-call | flops 10737418240 | bytes 4194304 | tf_op jit(solution)/shard_map/attend_back/pallas_call | solution.py:617
  281.0 23.2 %attend_back.4 = (bf16[2,1024,384]{2,1,0:T(8,128)(2,1)}, bf16[1024,384]{1,0:T(8,128)(2,1)}) custom-call(s32[1]{0:T(128)} %bitcast.2.place, s32[2,8]{1,0:T(2,128)} %pad_add_fusion.bounds, s32[2048,1]{1,0:T(8,128)} %copy.80.seg_col, s32[1,2048]{1,0:T(1,128)} %bitcast.135, bf16[2,1024,1536]{2,1,0:T(8,128)(2,1)} %get-tuple-element.246.refs_0_.refs_1_.refs_3_, ...), custom_call_target="tpu_custom_call" | custom-call | flops 10737418240 | bytes 4194304 | tf_op jit(solution)/shard_map/attend_back/pallas_call | solution.py:617
  304.2 4.8 %cut.4 = (bf16[4,64,1152]{2,1,0:T(8,128)(2,1)}, bf16[4,64,1152]{2,1,0:T(8,128)(2,1)}, bf16[4,64,1152]{2,1,0:T(8,128)(2,1)}, bf16[4,64,1152]{2,1,0:T(8,128)(2,1)}) custom-call(s32[2]{0:T(128)} %pad_add_fusion.1.where, bf16[4,2,2,64,384]{4,3,2,1,0:T(8,128)(2,1)} %bitcast.123, bf16[4,2,2,64,384]{4,3,2,1,0:T(8,128)(2,1)} %bitcast.122, ...), custom_call_target="tpu_custom_call" | custom-call | bytes 4718592 | tf_op jit(solution)/shard_map/cut/pallas_call | solution.py:122
  316.9 23.5 %attend_back.7 = (bf16[2,1024,384]{2,1,0:T(8,128)(2,1)}, bf16[1024,384]{1,0:T(8,128)(2,1)}) custom-call(s32[1]{0:T(128)} %bitcast.2.place, s32[2,8]{1,0:T(2,128)} %pad_add_fusion.bounds, s32[2048,1]{1,0:T(8,128)} %copy.80.seg_col, s32[1,2048]{1,0:T(1,128)} %bitcast.136, bf16[2,1024,1536]{2,1,0:T(8,128)(2,1)} %get-tuple-element.246.refs_0_.refs_1_.refs_3_, ...), custom_call_target="tpu_custom_call" | custom-call | flops 10737418240 | bytes 4194304 | tf_op jit(solution)/shard_map/attend_back/pallas_call | solution.py:617
  344.7 4.2 cut.5
  350.3 4.0 collective-permute-start.29
  362.8 4.9 %input_part.1 = bf16[1024,1024]{1,0:T(8,128)(2,1)} custom-call(bf16[2,1024,384]{2,1,0:T(8,128)(2,1)S(1)} %copy-done.3, bf16[2,1024,384]{2,1,0:T(8,128)(2,1)S(1)} %copy-done.2, bf16[2,1024,384]{2,1,0:T(8,128)(2,1)S(1)} %copy-done.1, bf16[2,1024,384]{2,1,0:T(8,128)(2,1)S(1)} %copy-done.4, bf16[1024,1536]{1,0:T(8,128)(2,1)S(1)} %copy-done), custom_call_target="tpu_custom_call" | custom-call | flops 3221225472 | bytes 8388608 | tf_op jit(solution)/shard_map/input_part/pallas_call | solution.py:795
  380.7 8.0 %last.2 = (bf16[512,1024]{1,0:T(8,128)(2,1)}, f32[8,2048]{1,0:T(8,128)}) custom-call(bf16[1024,1024]{1,0:T(8,128)(2,1)} %get-tuple-element.168.refs_0_, bf16[1024,32]{1,0:T(8,128)(2,1)} %copy.79.member.refs_1_, bf16[16,1024]{1,0:T(8,128)(2,1)} %pad.18.refs_2_, f32[8,6144]{1,0:T(8,128)} %pad.15.adaptive.refs_3_, f32[1024,1024]{1,0:T(8,128)} %get-tuple-element.302.refs_4_, ...), custom_call_target="tpu_custom_call" | custom-call | flops 1610612736 | bytes 6291456 | tf_op jit(solution)/shard_map/last/pallas_call | solution.py:845
  395.4 8.1 %last.3 = (bf16[512,1024]{1,0:T(8,128)(2,1)}, f32[8,2048]{1,0:T(8,128)}) custom-call(bf16[1024,1024]{1,0:T(8,128)(2,1)} %get-tuple-element.168.refs_0_, bf16[1024,32]{1,0:T(8,128)(2,1)} %copy.79.member.refs_1_, bf16[16,1024]{1,0:T(8,128)(2,1)} %pad.18.refs_2_, f32[8,6144]{1,0:T(8,128)} %pad.15.adaptive.refs_3_, f32[1024,1024]{1,0:T(8,128)} %get-tuple-element.302.refs_4_, ...), custom_call_target="tpu_custom_call" | custom-call | flops 1610612736 | bytes 6291456 | tf_op jit(solution)/shard_map/last/pallas_call | solution.py:845
  403.6 4.5 %collective-permute-done.36 = bf16[64,1536]{1,0:T(8,128)(2,1)S(1)} collective-permute-done((bf16[64,1536]{1,0:T(8,128)(2,1)S(1)}, bf16[64,1536]{1,0:T(8,128)(2,1)S(1)}, u32[]{:S(2)}, u32[]{:S(2)}) %collective-permute-start.36) | collective-permute-done | bytes 196640 | tf_op jit(solution)/shard_map/ppermute | solution.py:52
  413.5 5.0 %all-to-all-start.1 = ((f32[32,4,192]{2,1,0:T(4,128)}), f32[32,4,192]{2,1,0:T(4,128)}, u32[]{:S(2)}, u32[]{:S(2)}) async-start(f32[32,4,192]{2,1,0:T(4,128)} %bitcast.127), calls=%async_computation.1 | async-start | bytes 262144 | tf_op jit(solution)/shard_map/all_to_all | solution.py:1044
  (283 shorter events, 137.9 us)
Async XLA Ops:
  15.2 32.4 %collective-permute-start.5 = (bf16[1024,1024]{1,0:T(8,128)(2,1)}, bf16[1024,1024]{1,0:T(8,128)(2,1)S(1)}, u32[]{:S(2)}, u32[]{:S(2)}) collective-permute-start(bf16[1024,1024]{1,0:T(8,128)(2,1)} %there.1), channel_id=1, source_target_pairs={{1,2},{2,1},{5,6},{6,5},{9,10},{10,9},{13,14},{14,13},{17,18},{18,... | collective-permute-start | bytes 6291464 | tf_op jit(solution)/shard_map/ppermute | solution.py:52
  24.3 21.5 %collective-permute-start.2 = (bf16[64,1536]{1,0:T(8,128)(2,1)S(1)}, bf16[64,1536]{1,0:T(8,128)(2,1)S(1)}, u32[]{:S(2)}, u32[]{:S(2)}) collective-permute-start(bf16[64,1536]{1,0:T(8,128)(2,1)S(1)} %broadcast_select_fusion.5), channel_id=1, source_target_pairs={{0,8},{8,0},{16,24},{24,16},{1,9},{9,1},{17,25},{25,17},{2,10},{10... | collective-permute-start | bytes 589832 | tf_op jit(solution)/shard_map/ppermute | solution.py:78
  25.7 20.1 %collective-permute-start.3 = (bf16[64,1536]{1,0:T(8,128)(2,1)S(1)}, bf16[64,1536]{1,0:T(8,128)(2,1)S(1)}, u32[]{:S(2)}, u32[]{:S(2)}) collective-permute-start(bf16[64,1536]{1,0:T(8,128)(2,1)S(1)} %broadcast_select_fusion.5), channel_id=1, source_target_pairs={{0,16},{8,24},{16,0},{24,8},{1,17},{9,25},{17,1},{25,9},{2,18},{10... | collective-permute-start | bytes 589832 | tf_op jit(solution)/shard_map/ppermute | solution.py:78
  28.0 17.8 %collective-permute-start.4 = (bf16[64,1536]{1,0:T(8,128)(2,1)S(1)}, bf16[64,1536]{1,0:T(8,128)(2,1)S(1)}, u32[]{:S(2)}, u32[]{:S(2)}) collective-permute-start(bf16[64,1536]{1,0:T(8,128)(2,1)S(1)} %broadcast_select_fusion.5), channel_id=1, source_target_pairs={{0,24},{8,16},{16,8},{24,0},{1,25},{9,17},{17,9},{25,1},{2,26},{10... | collective-permute-start | bytes 589832 | tf_op jit(solution)/shard_map/ppermute | solution.py:78
  28.7 16.3 %all-to-all-start = ((f32[32,4,192]{2,1,0:T(4,128)}), f32[32,4,192]{2,1,0:T(4,128)S(1)}, u32[]{:S(2)}, u32[]{:S(2)}) async-start(f32[32,4,192]{2,1,0:T(4,128)} %bitcast.9), calls=%async_computation | async-start | bytes 262144 | tf_op jit(solution)/shard_map/all_to_all | solution.py:910
  34.0 117.5 %all-gather.2.cloned.1.call-start = ((), (), s32[]{:S(2)}) async-start(), calls=%async_computation.2 | async-start | bytes 10813440 | tf_op jit(solution)/shard_map/all_gather | solution.py:951
  47.6 20.8 %collective-permute-start.6 = (bf16[4,64,1536]{2,1,0:T(8,128)(2,1)S(1)}, bf16[4,64,1536]{2,1,0:T(8,128)(2,1)}, u32[]{:S(2)}, u32[]{:S(2)}) collective-permute-start(bf16[4,64,1536]{2,1,0:T(8,128)(2,1)S(1)} %pad_maximum_fusion.refs_2_), channel_id=1, source_target_pairs={{0,4},{4,0},{1,5},{5,1},{2,6},{6,2},{3,7},{7,3},{8,12},{12,8},{9,1... | collective-permute-start | bytes 2359304 | tf_op jit(solution)/shard_map/ppermute | solution.py:86
  48.3 20.8 %collective-permute-start.7 = (bf16[4,64,1536]{2,1,0:T(8,128)(2,1)S(1)}, bf16[4,64,1536]{2,1,0:T(8,128)(2,1)}, u32[]{:S(2)}, u32[]{:S(2)}) collective-permute-start(bf16[4,64,1536]{2,1,0:T(8,128)(2,1)S(1)} %pad_maximum_fusion.refs_2_), channel_id=1, source_target_pairs={{0,1},{1,0},{2,3},{3,2},{4,5},{5,4},{6,7},{7,6},{8,9},{9,8},{10,11... | collective-permute-start | bytes 2359304 | tf_op jit(solution)/shard_map/ppermute | solution.py:86
  69.0 20.2 %collective-permute-start.10 = (bf16[1024,1024]{1,0:T(8,128)(2,1)}, bf16[1024,1024]{1,0:T(8,128)(2,1)}, u32[]{:S(2)}, u32[]{:S(2)}) collective-permute-start(bf16[1024,1024]{1,0:T(8,128)(2,1)} %get-tuple-element.175.refs_0_.refs_9_), channel_id=1, source_target_pairs={{2,0},{0,2},{3,1},{1,3},{6,4},{4,6},{7,5},{5,7},{10,8},{8,10},{11,... | collective-permute-start | bytes 6291464 | tf_op jit(solution)/shard_map/ppermute | solution.py:65
  104.4 44.2 %collective-permute-start.11 = (bf16[1024,1024]{1,0:T(8,128)(2,1)}, bf16[1024,1024]{1,0:T(8,128)(2,1)S(1)}, u32[]{:S(2)}, u32[]{:S(2)}) collective-permute-start(bf16[1024,1024]{1,0:T(8,128)(2,1)} %refs_4_), channel_id=1, source_target_pairs={{1,2},{2,1},{5,6},{6,5},{9,10},{10,9},{13,14},{14,13},{17,18},{18,... | collective-permute-start | bytes 6291464 | tf_op jit(solution)/shard_map/ppermute | solution.py:52
  198.4 21.1 %collective-permute-start.14 = (bf16[1024,1024]{1,0:T(8,128)(2,1)}, bf16[1024,1024]{1,0:T(8,128)(2,1)}, u32[]{:S(2)}, u32[]{:S(2)}) collective-permute-start(bf16[1024,1024]{1,0:T(8,128)(2,1)} %convolution_convert_fusion), channel_id=1, source_target_pairs={{0,2},{2,0},{1,3},{3,1},{4,6},{6,4},{5,7},{7,5},{8,10},{10,8},{9,1... | collective-permute-start | bytes 6291464 | tf_op jit(solution)/shard_map/ppermute | solution.py:70
  202.2 17.3 %collective-permute-start.13 = (bf16[1024,1024]{1,0:T(8,128)(2,1)}, bf16[1024,1024]{1,0:T(8,128)(2,1)}, u32[]{:S(2)}, u32[]{:S(2)}) collective-permute-start(bf16[1024,1024]{1,0:T(8,128)(2,1)} %convolution_convert_fusion.2), channel_id=1, source_target_pairs={{0,2},{2,0},{1,3},{3,1},{4,6},{6,4},{5,7},{7,5},{8,10},{10,8},{9,1... | collective-permute-start | bytes 6291464 | tf_op jit(solution)/shard_map/ppermute | solution.py:70
  206.9 102.1 %collective-permute-start.20 = (bf16[1024,1024]{1,0:T(8,128)(2,1)S(1)}, bf16[1024,1024]{1,0:T(8,128)(2,1)}, u32[]{:S(2)}, u32[]{:S(2)}) collective-permute-start(bf16[1024,1024]{1,0:T(8,128)(2,1)S(1)} %copy-done.6), channel_id=1, source_target_pairs={{1,2},{2,1},{5,6},{6,5},{9,10},{10,9},{13,14},{14,13},{17,18},{18,... | collective-permute-start | bytes 6291464 | tf_op jit(solution)/shard_map/ppermute | solution.py:52
  227.8 81.2 %collective-permute-start.17 = (bf16[4,64,2560]{2,1,0:T(8,128)(2,1)}, bf16[4,64,2560]{2,1,0:T(8,128)(2,1)}, u32[]{:S(2)}, u32[]{:S(2)}) collective-permute-start(bf16[4,64,2560]{2,1,0:T(8,128)(2,1)} %get-tuple-element.215), channel_id=1, source_target_pairs={{0,4},{4,0},{1,5},{5,1},{2,6},{6,2},{3,7},{7,3},{8,12},{12,8},{9,1... | collective-permute-start | bytes 3932168 | tf_op jit(solution)/shard_map/ppermute | solution.py:144
  229.3 79.7 %collective-permute-start.18 = (bf16[4,64,2560]{2,1,0:T(8,128)(2,1)}, bf16[4,64,2560]{2,1,0:T(8,128)(2,1)}, u32[]{:S(2)}, u32[]{:S(2)}) collective-permute-start(bf16[4,64,2560]{2,1,0:T(8,128)(2,1)} %get-tuple-element.216), channel_id=1, source_target_pairs={{0,1},{1,0},{2,3},{3,2},{4,5},{5,4},{6,7},{7,6},{8,9},{9,8},{10,11... | collective-permute-start | bytes 3932168 | tf_op jit(solution)/shard_map/ppermute | solution.py:143
  229.3 79.7 %collective-permute-start.19 = (bf16[4,64,2560]{2,1,0:T(8,128)(2,1)}, bf16[4,64,2560]{2,1,0:T(8,128)(2,1)}, u32[]{:S(2)}, u32[]{:S(2)}) collective-permute-start(bf16[4,64,2560]{2,1,0:T(8,128)(2,1)} %get-tuple-element.217), channel_id=1, source_target_pairs={{0,5},{1,4},{4,1},{5,0},{2,7},{3,6},{6,3},{7,2},{8,13},{9,12},{12,... | collective-permute-start | bytes 3932168 | tf_op jit(solution)/shard_map/ppermute | solution.py:142
  311.9 30.3 %collective-permute-start.21 = (bf16[2,64,2560]{2,1,0:T(8,128)(2,1)S(1)}, bf16[2,64,2560]{2,1,0:T(8,128)(2,1)S(1)}, u32[]{:S(2)}, u32[]{:S(2)}) collective-permute-start(bf16[2,64,2560]{2,1,0:T(8,128)(2,1)S(1)} %get-tuple-element.238), channel_id=1, source_target_pairs={{0,8},{8,0},{16,24},{24,16},{1,9},{9,1},{17,25},{25,17},{2,10},{10... | collective-permute-start | bytes 1966088 | tf_op jit(solution)/shard_map/ppermute | solution.py:78
  312.5 27.9 %collective-permute-start.22 = (bf16[4,64,1152]{2,1,0:T(8,128)(2,1)}, bf16[4,64,1152]{2,1,0:T(8,128)(2,1)S(1)}, u32[]{:S(2)}, u32[]{:S(2)}) collective-permute-start(bf16[4,64,1152]{2,1,0:T(8,128)(2,1)} %get-tuple-element.240), channel_id=1, source_target_pairs={{0,4},{4,0},{1,5},{5,1},{2,6},{6,2},{3,7},{7,3},{8,12},{12,8},{9,1... | collective-permute-start | bytes 1769480 | tf_op jit(solution)/shard_map/ppermute | solution.py:144
  315.7 24.7 %collective-permute-start.23 = (bf16[4,64,1152]{2,1,0:T(8,128)(2,1)}, bf16[4,64,1152]{2,1,0:T(8,128)(2,1)S(1)}, u32[]{:S(2)}, u32[]{:S(2)}) collective-permute-start(bf16[4,64,1152]{2,1,0:T(8,128)(2,1)} %get-tuple-element.241), channel_id=1, source_target_pairs={{0,1},{1,0},{2,3},{3,2},{4,5},{5,4},{6,7},{7,6},{8,9},{9,8},{10,11... | collective-permute-start | bytes 1769480 | tf_op jit(solution)/shard_map/ppermute | solution.py:143
  315.7 26.5 %collective-permute-start.24 = (bf16[4,64,1152]{2,1,0:T(8,128)(2,1)}, bf16[4,64,1152]{2,1,0:T(8,128)(2,1)}, u32[]{:S(2)}, u32[]{:S(2)}) collective-permute-start(bf16[4,64,1152]{2,1,0:T(8,128)(2,1)} %get-tuple-element.242), channel_id=1, source_target_pairs={{0,5},{1,4},{4,1},{5,0},{2,7},{3,6},{6,3},{7,2},{8,13},{9,12},{12,... | collective-permute-start | bytes 1769480 | tf_op jit(solution)/shard_map/ppermute | solution.py:142
  350.3 18.3 %collective-permute-start.29 = (bf16[64,2560]{1,0:T(8,128)(2,1)S(1)}, bf16[64,2560]{1,0:T(8,128)(2,1)S(1)}, u32[]{:S(2)}, u32[]{:S(2)}) collective-permute-start(bf16[64,2560]{1,0:T(8,128)(2,1)S(1)} %get-tuple-element.320), channel_id=1, source_target_pairs={{0,16},{8,24},{16,0},{24,8},{1,17},{9,25},{17,1},{25,9},{2,18},{10... | collective-permute-start | bytes 983048 | tf_op jit(solution)/shard_map/ppermute | solution.py:78
  372.9 16.6 %collective-permute-start.33 = (bf16[64,384]{1,0:T(8,128)(2,1)S(1)}, bf16[64,384]{1,0:T(8,128)(2,1)S(1)}, u32[]{:S(2)}, u32[]{:S(2)}) collective-permute-start(bf16[64,384]{1,0:T(8,128)(2,1)S(1)} %get-tuple-element.330), channel_id=1, source_target_pairs={{0,8},{8,0},{16,24},{24,16},{1,9},{9,1},{17,25},{25,17},{2,10},{10... | collective-permute-start | bytes 147464 | tf_op jit(solution)/shard_map/ppermute | solution.py:78
  389.6 18.5 %collective-permute-start.37 = (bf16[512,1024]{1,0:T(8,128)(2,1)}, bf16[512,1024]{1,0:T(8,128)(2,1)S(1)}, u32[]{:S(2)}, u32[]{:S(2)}) collective-permute-start(bf16[512,1024]{1,0:T(8,128)(2,1)} %get-tuple-element.301), channel_id=1, source_target_pairs={{1,2},{2,1},{5,6},{6,5},{9,10},{10,9},{13,14},{14,13},{17,18},{18,... | collective-permute-start | bytes 3145736 | tf_op jit(solution)/shard_map/ppermute | solution.py:52
  410.7 22.9 %collective-permute-start.38 = (bf16[512,1024]{1,0:T(8,128)(2,1)}, bf16[512,1024]{1,0:T(8,128)(2,1)}, u32[]{:S(2)}, u32[]{:S(2)}) collective-permute-start(bf16[512,1024]{1,0:T(8,128)(2,1)} %get-tuple-element.312), channel_id=1, source_target_pairs={{1,2},{2,1},{5,6},{6,5},{9,10},{10,9},{13,14},{14,13},{17,18},{18,... | collective-permute-start | bytes 3145736 | tf_op jit(solution)/shard_map/ppermute | solution.py:52
  (78 other events, 696.6 us)
Sparse Core Ops, SparseCore 0:
  47.7 101.9 all-gather.1
